TPU v7x, 256 devices: a whole 4x4x8 slice. The times are simulated.
256 devices in a mesh: section: 2 (over core), beam: 32 (over z, x), tensor: 4 (over y).
Axes of the slice: x: 4, y: 4, z: 8, core: 2. Of those that a mesh axis runs over, the one named last changes fastest.
Arguments:
- streams_in: bfloat16 [64, 64, 8192], P('beam', None, 'tensor'), may hold values from -14 to 14
- beam_state_cache: bfloat16 [2, 64, 128, 64, 128], P('section', 'beam', 'tensor'), may hold values from -6 to 6
- conv_x_cache: bfloat16 [2, 64, 3, 8192], P('section', 'beam', None, 'tensor'), may hold values from -6 to 6
- conv_bc_cache: bfloat16 [2, 64, 3, 2, 1024], P('section', 'beam', None, None, 'tensor'), may hold values from -6 to 6
- bc_inputs: bfloat16 [2, 64, 64, 2, 1024], P('section', 'beam', None, None, 'tensor'), may hold values from -6 to 6
- unbiased_increments: float32 [2, 64, 64, 128], P('section', 'beam', None, 'tensor'), may hold values from -3 to 15
- parents: int32 [64], replicated, may hold values from 0 to 63, as said below
- lengths: int32 [64], P('beam'), may hold values from 1 to 64, as said below
- input_norm_gain: float32 [2, 8192], P('section', 'tensor'), may hold values from 0.1 to 1.9
- conv_x_weight: float32 [2, 4, 8192], P('section', None, 'tensor'), may hold values from -3 to 3
- conv_bc_weight: float32 [2, 4, 2, 1024], P('section', None, None, 'tensor'), may hold values from -3 to 3
- a_log: float32 [2, 128], P('section', 'tensor'), may hold values from -3.6 to 0
- dt_bias: float32 [2, 128], P('section', 'tensor'), may hold values from -4 to -2
- skip_gain: float32 [2, 128], P('section', 'tensor'), may hold values from 0.5 to 2
- out_gain: float32 [2, 8192], P('section', 'tensor'), may hold values from 0.1 to 1.9
Outputs:
- streams_out: bfloat16 [2, 64, 64, 8192], P('section', 'beam', None, 'tensor')
- ssm_out: bfloat16 [2, 64, 128, 64, 128], P('section', 'beam', 'tensor')
- conv_x_out: bfloat16 [2, 64, 3, 8192], P('section', 'beam', None, 'tensor')
- conv_bc_out: bfloat16 [2, 64, 3, 2, 1024], P('section', 'beam', None, None, 'tensor')
Inputs may be any that keep to these rules, and one draw needn't show every extreme that they name: `parents`: children 2 k .. 2 k + 1 form block k; each child's parent lies in block k - 1, k or k + 1, blocks counted modulo the number of blocks; in every block the first child takes its parent from the block before and the second child from the block after. `lengths`: some child has all 64 tokens valid in every draw.
All inputs are finite; a program needn't handle non-finite values.
Results may differ from a plain program's by a relative error of at most 0.0055.
Values may be sent and summed in bfloat16 or wider, within the bound.
No kernel may reach another device: no remote copies, remote signals or barrier semaphores. Data moves between devices by JAX's collectives and lax.ppermute only.
A program may use at most 64 MiB of HBM per device.

v0:
```python
import functools

import jax
import jax.numpy as jnp
from jax import lax
from jax.experimental import pallas as pl
from jax.experimental.pallas import tpu as pltpu
from jax.sharding import PartitionSpec as P

CH = 8192
EPS = 1e-05
KIDS = 2
T = 64
CD = 2048
HD = 32
N = 128
GC = 1024
F32 = jnp.float32
BF16 = jnp.bfloat16
HIGHEST = lax.Precision.HIGHEST
VMEM = pl.BlockSpec(memory_space=pltpu.VMEM)
SMEM = pl.BlockSpec(memory_space=pltpu.SMEM)
ANY = pl.BlockSpec(memory_space=pl.ANY)


def iota(shape, dim):
    return lax.broadcasted_iota(jnp.int32, shape, dim)


def as_row(col):
    size = col.shape[0]
    keep = iota((size, size), 0) == iota((size, size), 1)
    return jnp.sum(jnp.where(keep, col, 0.0), axis=0, keepdims=True)


def as_col(row):
    size = row.shape[1]
    keep = iota((size, size), 0) == iota((size, size), 1)
    return jnp.sum(jnp.where(keep, row, 0.0), axis=1, keepdims=True)


def silu(v):
    return 0.5 * v * (1.0 + jnp.tanh(0.5 * v))


def dot(a, b, dims, precision=None):
    return lax.dot_general(
        a, b, (dims, ((), ())), precision=precision, preferred_element_type=F32
    )


def three_parts(v):
    high = v.astype(BF16)
    rest = v - high.astype(F32)
    mid = rest.astype(BF16)
    low = (rest - mid.astype(F32)).astype(BF16)
    return [high, mid, low]


def pick_kernel(pick_ref, stream_ref, state_ref, part_ref, fwd_ref, bwd_ref, sems):
    first = pltpu.make_async_copy(state_ref.at[pick_ref[0]], fwd_ref, sems.at[0])
    second = pltpu.make_async_copy(state_ref.at[pick_ref[1]], bwd_ref, sems.at[1])
    first.start()
    second.start()
    for c in range(KIDS):
        s = stream_ref[c].astype(F32)
        part_ref[c : c + 1, :] = as_row(jnp.sum(s * s, axis=1, keepdims=True))
    first.wait()
    second.wait()


def fresh_x(s, total, rows, gain, taps, valid, px_ref):
    scale = lax.rsqrt(total / CH + EPS)
    x_in = (s * scale * gain).astype(BF16).astype(F32)
    px_ref[5:8, :] = rows.astype(F32)
    px_ref[8:72, :] = x_in
    acc = taps[0:1] * px_ref[5:69, :]
    for k in range(1, 4):
        acc = acc + taps[k : k + 1] * px_ref[5 + k : 69 + k, :]
    return silu(acc) * valid


def intra(mix_ref, c, x):
    xb = x.astype(BF16)
    outs = []
    lane = iota((T, 256), 1) // 64
    masks = [jnp.where(lane == j, 1.0, 0.0).astype(BF16) for j in range(4)]
    for q in range(CD // 256):
        xq = xb[:, 256 * q : 256 * (q + 1)]
        rhs = jnp.concatenate([xq * mask for mask in masks], axis=0)
        outs.append(dot(mix_ref[c, :, 256 * q : 256 * (q + 1)], rhs, ((1,), (0,))))
    return jnp.concatenate(outs, axis=1)


def finish(y, s, gain, valid):
    outs = []
    for g in range(CD // GC):
        part = y[:, GC * g : GC * (g + 1)]
        mean = jnp.sum(part * part, axis=1, keepdims=True) * (1.0 / GC)
        outs.append(part * lax.rsqrt(mean + EPS))
    z = jnp.concatenate(outs, axis=1) * gain
    return (s + z * valid).astype(BF16)


def valid_col(length):
    return jnp.where(iota((T, 1), 0) < length, 1.0, 0.0)


def pre_kernel(
    len_ref,
    rows_b_ref,
    rows_a_ref,
    bc_ref,
    inc_ref,
    taps_bc_ref,
    log_ref,
    bias_ref,
    stream_ref,
    p0_ref,
    p1_ref,
    p2_ref,
    p3_ref,
    gain_ref,
    taps_ref,
    skip_ref,
    mix_ref,
    weight_ref,
    grow_ref,
    b_ref,
    c_ref,
    last_ref,
    y_ref,
    bc_out_ref,
    pbc_ref,
    px_ref,
):
    rate = as_col(jnp.exp(log_ref[...]))
    bias = as_col(bias_ref[...])
    upper = jnp.where(iota((T, T), 0) <= iota((T, T), 1), 1.0, 0.0)
    onehot = jnp.where(iota((HD, CD), 0) == iota((HD, CD), 1) // 64, 1.0, 0.0).astype(BF16)
    onehot = jnp.concatenate([onehot] * 3, axis=0)
    diag = iota((T, CD), 1) % T == iota((T, CD), 0)
    causal = iota((T, N), 0) >= iota((T, N), 1) % T
    totals = p0_ref[...] + p1_ref[...] + p2_ref[...] + p3_ref[...]
    for c in range(KIDS):
        length = len_ref[c]
        rows_ref = (rows_b_ref, rows_a_ref)[c]
        rows = rows_ref[...]
        pbc_ref[5:8, :] = rows[:, CD:].astype(F32)
        pbc_ref[8:72, :] = bc_ref[c].astype(F32)
        taps = [
            jnp.concatenate([taps_bc_ref[k, 0:1, :], taps_bc_ref[k, 1:2, :]], axis=1)
            for k in range(4)
        ]
        acc = taps[0] * pbc_ref[5:69, :]
        for k in range(1, 4):
            acc = acc + taps[k] * pbc_ref[5 + k : 69 + k, :]
        bc = silu(acc)
        for k in range(3):
            row = pbc_ref[pl.ds(5 + length + k, 1), :]
            bc_out_ref[c, k] = jnp.concatenate([row[:, :256], row[:, 256:]], axis=0).astype(BF16)
        b_ref[c] = bc[:, :256].astype(BF16)
        c_ref[c] = bc[:, 256:].astype(BF16)
        valid_row = jnp.where(iota((1, T), 1) < length, 1.0, 0.0)
        raw = inc_ref[c] + bias
        dt = (jnp.maximum(raw, 0.0) + jnp.log1p(jnp.exp(-jnp.abs(raw)))) * valid_row
        cum = dot(-dt * rate, upper, ((1,), (0,)), HIGHEST)
        last_ref[c] = jnp.broadcast_to(jnp.exp(cum[:, T - 1 : T]), (HD, N))
        edt = dot(jnp.concatenate(three_parts(dt), axis=0), onehot, ((0,), (0,)))
        ecum = dot(jnp.concatenate(three_parts(cum), axis=0), onehot, ((0,), (0,)))
        row_dt = jnp.sum(jnp.where(diag, edt, 0.0), axis=0, keepdims=True)
        row_cum = jnp.sum(jnp.where(diag, ecum, 0.0), axis=0, keepdims=True)
        grow_ref[c] = jnp.exp(ecum)
        weight_ref[c] = jnp.exp(ecum[T - 1 : T] - ecum) * edt
        for g in range(2):
            bg = bc[:, N * g : N * (g + 1)]
            cg = bc[:, 256 + N * g : 256 + N * (g + 1)]
            inner = dot(cg, jnp.concatenate([bg, bg], axis=0), ((1,), (1,)), HIGHEST)
            inner = jnp.where(causal, inner, 0.0)
            for j in range(8 * g, 8 * g + 8):
                at = slice(N * j, N * (j + 1))
                gap = jnp.minimum(ecum[:, at] - row_cum[:, at], 0.0)
                mix_ref[c, :, at] = (jnp.exp(gap) * inner * row_dt[:, at]).astype(BF16)
        s = stream_ref[c].astype(F32)
        x = fresh_x(
            s,
            as_col(totals[c : c + 1]),
            rows[:, :CD],
            gain_ref[...],
            taps_ref[...],
            valid_col(length),
            px_ref,
        )
        y_ref[c] = intra(mix_ref, c, x) + skip_ref[...] * x


def mid_kernel(
    len_ref,
    y_ref,
    grow_ref,
    c_ref,
    state_b_ref,
    state_a_ref,
    stream_ref,
    gain_ref,
    out_ref,
    part_ref,
    read_ref,
):
    for c in range(KIDS):
        state_ref = (state_b_ref, state_a_ref)[c]
        read = jnp.concatenate(
            [
                dot(c_ref[c, :, N * g : N * (g + 1)], state_ref[GC * g : GC * (g + 1), :], ((1,), (1,)))
                for g in range(2)
            ],
            axis=1,
        )
        read = read * grow_ref[c]
        read_ref[c] = read
        out = finish(
            y_ref[c] + read, stream_ref[c].astype(F32), gain_ref[...], valid_col(len_ref[c])
        )
        out_ref[c] = out
        s = out.astype(F32)
        part_ref[c : c + 1, :] = as_row(jnp.sum(s * s, axis=1, keepdims=True))


def last_kernel(
    len_ref,
    sec_ref,
    stream_ref,
    moved_ref,
    r1_ref,
    r2_ref,
    r3_ref,
    q1_ref,
    q2_ref,
    q3_ref,
    rows_b_ref,
    rows_a_ref,
    gain_in_ref,
    taps_ref,
    skip_ref,
    gain_ref,
    mix_ref,
    weight_ref,
    read_ref,
    b_ref,
    last_ref,
    state_b_ref,
    state_a_ref,
    out_ref,
    new_ref,
    x_out_ref,
    px_ref,
):
    first = sec_ref[0] == 0
    others = jnp.where(
        first,
        r1_ref[...] + r2_ref[...] + r3_ref[...],
        q1_ref[...] + q2_ref[...] + q3_ref[...],
    )
    tails = []
    for c in range(KIDS):
        length = len_ref[c]
        valid = valid_col(length)
        rows_ref = (rows_b_ref, rows_a_ref)[c]
        state_ref = (state_b_ref, state_a_ref)[c]
        s = jnp.where(first, stream_ref[c].astype(F32), moved_ref[c].astype(F32))
        total = jnp.sum(s * s, axis=1, keepdims=True) + as_col(others[c : c + 1])
        x = fresh_x(s, total, rows_ref[:, :CD], gain_in_ref[...], taps_ref[...], valid, px_ref)
        tails.append([px_ref[pl.ds(5 + length + k, 1), :] for k in range(3)])
        y = intra(mix_ref, c, x) + skip_ref[...] * x + read_ref[c]
        out_ref[c] = finish(y, s, gain_ref[...], valid)
        xw = (x * weight_ref[c]).astype(BF16)
        for g in range(2):
            fresh = dot(xw[:, GC * g : GC * (g + 1)], b_ref[c, :, N * g : N * (g + 1)], ((0,), (0,)))
            for h in range(16 * g, 16 * g + 16):
                at = slice(64 * h, 64 * (h + 1))
                off = 64 * (h - 16 * g)
                new_ref[c, at, :] = (
                    last_ref[c, h : h + 1, :] * state_ref[at, :].astype(F32) + fresh[off : off + 64]
                ).astype(BF16)
    for k in range(3):
        x_out_ref[k] = jnp.concatenate([tails[0][k], tails[1][k]], axis=0).astype(BF16)


def shape(dims, kind):
    return jax.ShapeDtypeStruct(dims, kind)


def params(mib):
    return pltpu.CompilerParams(vmem_limit_bytes=mib * 2**20)


def cost(flops, moved, exps=0):
    return pl.CostEstimate(flops=flops, bytes_accessed=moved, transcendentals=exps)


def on_device(
    streams_in,
    beam_state_cache,
    conv_x_cache,
    conv_bc_cache,
    bc_inputs,
    unbiased_increments,
    parents,
    lengths,
    input_norm_gain,
    conv_x_weight,
    conv_bc_weight,
    a_log,
    dt_bias,
    skip_gain,
    out_gain,
):
    peers = lax.axis_size("beam")
    me = lax.axis_index("beam")
    tens = lax.axis_size("tensor")
    section = lax.axis_index("section").astype(jnp.int32)
    pick = jnp.stack(
        [
            parents[KIDS * ((me + 1) % peers)] % KIDS,
            parents[KIDS * ((me + peers - 1) % peers) + 1] % KIDS,
        ]
    ).astype(jnp.int32)
    states = beam_state_cache[0].reshape(KIDS, CD, N)
    part, fwd, bwd = pl.pallas_call(
        pick_kernel,
        out_shape=(shape((KIDS, T), F32), shape((CD, N), BF16), shape((CD, N), BF16)),
        in_specs=[SMEM, VMEM, ANY],
        out_specs=(VMEM, ANY, ANY),
        scratch_shapes=[pltpu.SemaphoreType.DMA((2,))],
        compiler_params=params(8),
        name="pick",
    )(pick, streams_in, states)

    def along(value, axis, steps):
        size = lax.axis_size(axis)
        return lax.ppermute(value, axis, [(i, (i + steps) % size) for i in range(size)])

    packed = jnp.concatenate(
        [conv_x_cache[0], conv_bc_cache[0].reshape(KIDS, 3, 512)], axis=2
    )
    rows_b = along(lax.dynamic_index_in_dim(packed, pick[0], 0, False), "beam", 1)
    rows_a = along(lax.dynamic_index_in_dim(packed, pick[1], 0, False), "beam", -1)
    r1, r2, r3 = [along(part, "tensor", k) for k in range(1, tens)]
    state_b = along(fwd, "beam", 1)
    state_a = along(bwd, "beam", -1)

    bc = bc_inputs[0].reshape(KIDS, T, 512)
    inc = jnp.transpose(unbiased_increments[0], (0, 2, 1))
    skip = jnp.repeat(skip_gain, 64, axis=1)
    taps = conv_x_weight[0]
    mix, weight, grow, b_mat, c_mat, last, y_part, bc_out = pl.pallas_call(
        pre_kernel,
        out_shape=(
            shape((KIDS, T, CD), BF16),
            shape((KIDS, T, CD), F32),
            shape((KIDS, T, CD), F32),
            shape((KIDS, T, 256), BF16),
            shape((KIDS, T, 256), BF16),
            shape((KIDS, HD, N), F32),
            shape((KIDS, T, CD), F32),
            shape((KIDS, 3, 2, 256), BF16),
        ),
        in_specs=[SMEM] + [VMEM] * 15,
        out_specs=tuple([VMEM] * 8),
        scratch_shapes=[pltpu.VMEM((72, 512), F32), pltpu.VMEM((72, CD), F32)],
        compiler_params=params(24),
        cost_estimate=cost(200_000_000, 5_000_000, 1_000_000),
        name="pre",
    )(
        lengths,
        rows_b,
        rows_a,
        bc,
        inc,
        conv_bc_weight[0],
        a_log,
        dt_bias,
        streams_in,
        part,
        r1,
        r2,
        r3,
        input_norm_gain,
        taps,
        skip,
    )
    mid, mid_part, read = pl.pallas_call(
        mid_kernel,
        out_shape=(
            shape((KIDS, T, CD), BF16),
            shape((KIDS, T), F32),
            shape((KIDS, T, CD), F32),
        ),
        in_specs=[SMEM] + [VMEM] * 7,
        out_specs=(VMEM, VMEM, VMEM),
        compiler_params=params(16),
        name="mid",
    )(lengths, y_part, grow, c_mat, state_b, state_a, streams_in, out_gain)

    moved = lax.ppermute(mid, "section", [(0, 1)])
    q1, q2, q3 = [
        lax.ppermute(
            mid_part, ("section", "tensor"), [(i, tens + (i + k) % tens) for i in range(tens)]
        )
        for k in range(1, tens)
    ]
    out, new, x_out = pl.pallas_call(
        last_kernel,
        out_shape=(
            shape((KIDS, T, CD), BF16),
            shape((KIDS, CD, N), BF16),
            shape((3, KIDS, CD), BF16),
        ),
        in_specs=[SMEM, SMEM] + [VMEM] * 21,
        out_specs=(VMEM, VMEM, VMEM),
        scratch_shapes=[pltpu.VMEM((72, CD), F32)],
        compiler_params=params(24),
        name="last",
    )(
        lengths,
        section[None],
        streams_in,
        moved,
        r1,
        r2,
        r3,
        q1,
        q2,
        q3,
        rows_b,
        rows_a,
        input_norm_gain,
        taps,
        skip,
        out_gain,
        mix,
        weight,
        read,
        b_mat,
        last,
        state_b,
        state_a,
    )
    return (
        out[None],
        new.reshape(1, KIDS, HD, 64, N),
        jnp.transpose(x_out, (1, 0, 2))[None],
        bc_out[None],
    )


def solution(mesh):
    placed = (
        P("beam", None, "tensor"),
        P("section", "beam", "tensor", None, None),
        P("section", "beam", None, "tensor"),
        P("section", "beam", None, None, "tensor"),
        P("section", "beam", None, None, "tensor"),
        P("section", "beam", None, "tensor"),
        P(),
        P("beam"),
        P("section", "tensor"),
        P("section", None, "tensor"),
        P("section", None, None, "tensor"),
        P("section", "tensor"),
        P("section", "tensor"),
        P("section", "tensor"),
        P("section", "tensor"),
    )
    return jax.shard_map(
        on_device,
        mesh=mesh,
        in_specs=placed,
        out_specs=(
            P("section", "beam", None, "tensor"),
            P("section", "beam", "tensor", None, None),
            P("section", "beam", None, "tensor"),
            P("section", "beam", None, None, "tensor"),
        ),
        check_vma=False,
    )
```

profile of v0, /device:TPU:1, one launch (start us, length us, event | category | flops | bytes accessed | tf_op | source)
XLA Modules:
  0.0 62.7 jit_solution(2241705534807340480)
XLA Ops:
  0.7 0.0 copy-start.16
  0.7 0.6 %copy-done.16 = s32[64]{0:T(128)S(1)} copy-done((s32[64]{0:T(128)S(1)}, s32[64]{0:T(128)}, u32[]{:S(2)}) %copy-start.16) | copy-done | bytes 280
  1.3 0.6 fusion
  5.8 0.1 pad_add_fusion.pick_ref
  5.9 1.0 %copy-done = bf16[2,64,2048]{2,1,0:T(8,128)(2,1)S(1)} copy-done((bf16[2,64,2048]{2,1,0:T(8,128)(2,1)S(1)}, bf16[2,64,2048]{2,1,0:T(8,128)(2,1)}, u32[]{:S(2)}) %copy-start) | copy-done | bytes 524312
  6.9 1.2 %copy-done.2 = bf16[1,2,32,64,128]{4,3,2,1,0:T(8,128)(2,1)S(1)} copy-done((bf16[1,2,32,64,128]{4,3,2,1,0:T(8,128)(2,1)S(1)}, bf16[1,2,32,64,128]{4,3,2,1,0:T(8,128)(2,1)}, u32[]{:S(2)}) %copy-start.2) | copy-done | bytes 1048600
  8.2 0.0 copy-start.7
  8.2 0.0 copy-start.9
  8.2 0.0 copy-start.10
  8.2 1.5 %pick.1 = (f32[2,64]{1,0:T(2,128)S(1)}, bf16[2048,128]{1,0:T(8,128)(2,1)}, bf16[2048,128]{1,0:T(8,128)(2,1)}) custom-call(s32[2]{0:T(128)S(1)} %pad_add_fusion.pick_ref, bf16[2,64,2048]{2,1,0:T(8,128)(2,1)S(1)} %copy-done, bf16[2,2048,128]{2,1,0:T(8,128)(2,1)S(1)} %bitcast.27), custom_call_target="tpu_custom_call" | custom-call | tf_op jit(solution)/shard_map/pick/pallas_call | solution.py:329
  9.7 0.0 copy-start.1
  9.7 2.1 %collective-permute-start.5 = (bf16[2048,128]{1,0:T(8,128)(2,1)}, bf16[2048,128]{1,0:T(8,128)(2,1)S(1)}, u32[]{:S(2)}, u32[]{:S(2)}) collective-permute-start(bf16[2048,128]{1,0:T(8,128)(2,1)} %get-tuple-element.25), channel_id=1, source_target_pairs={{0,4},{4,8},{8,12},{12,16},{16,20},{20,24},{24,28},{28,32},{32,36}... | collective-permute-start | bytes 1572872 | tf_op jit(solution)/shard_map/ppermute | solution.py:341
  11.9 6.6 %collective-permute-start.6 = (bf16[2048,128]{1,0:T(8,128)(2,1)}, bf16[2048,128]{1,0:T(8,128)(2,1)S(1)}, u32[]{:S(2)}, u32[]{:S(2)}) collective-permute-start(bf16[2048,128]{1,0:T(8,128)(2,1)} %get-tuple-element.26), channel_id=1, source_target_pairs={{0,124},{4,0},{8,4},{12,8},{16,12},{20,16},{24,20},{28,24},{32,28}... | collective-permute-start | bytes 1572872 | tf_op jit(solution)/shard_map/ppermute | solution.py:341
  18.6 0.1 dynamic-slice_maximum_fusion
  18.7 0.1 collective-permute-start
  18.8 4.8 %collective-permute-start.1 = (bf16[3,2560]{1,0:T(4,128)(2,1)S(1)}, bf16[3,2560]{1,0:T(4,128)(2,1)S(1)}, u32[]{:S(2)}, u32[]{:S(2)}) collective-permute-start(bf16[3,2560]{1,0:T(4,128)(2,1)S(1)} %bitcast.34), channel_id=1, source_target_pairs={{0,124},{4,0},{8,4},{12,8},{16,12},{20,16},{24,20},{28,24},{32,28}... | collective-permute-start | bytes 46088 | tf_op jit(solution)/shard_map/ppermute | solution.py:341
  23.6 2.7 %collective-permute-start.4 = (f32[2,64]{1,0:T(2,128)S(1)}, f32[2,64]{1,0:T(2,128)S(1)}, u32[]{:S(2)}, u32[]{:S(2)}) collective-permute-start(f32[2,64]{1,0:T(2,128)S(1)} %get-tuple-element.21.p0_ref), channel_id=1, source_target_pairs={{0,3},{1,0},{2,1},{3,2},{4,7},{5,4},{6,5},{7,6},{8,11},{9,8},{10,9... | collective-permute-start | bytes 1544 | tf_op jit(solution)/shard_map/ppermute | solution.py:341
  26.4 0.7 %collective-permute-done.4.p3_ref.r3_ref = f32[2,64]{1,0:T(2,128)S(1)} collective-permute-done((f32[2,64]{1,0:T(2,128)S(1)}, f32[2,64]{1,0:T(2,128)S(1)}, u32[]{:S(2)}, u32[]{:S(2)}) %collective-permute-start.4) | collective-permute-done | bytes 544 | tf_op jit(solution)/shard_map/ppermute | solution.py:341
  27.1 2.2 %collective-permute-start.3 = (f32[2,64]{1,0:T(2,128)S(1)}, f32[2,64]{1,0:T(2,128)S(1)}, u32[]{:S(2)}, u32[]{:S(2)}) collective-permute-start(f32[2,64]{1,0:T(2,128)S(1)} %get-tuple-element.21.p0_ref), channel_id=1, source_target_pairs={{0,2},{1,3},{2,0},{3,1},{4,6},{5,7},{6,4},{7,5},{8,10},{9,11},{10,... | collective-permute-start | bytes 1544 | tf_op jit(solution)/shard_map/ppermute | solution.py:341
  29.3 2.0 %collective-permute-done.3.p2_ref.r2_ref = f32[2,64]{1,0:T(2,128)S(1)} collective-permute-done((f32[2,64]{1,0:T(2,128)S(1)}, f32[2,64]{1,0:T(2,128)S(1)}, u32[]{:S(2)}, u32[]{:S(2)}) %collective-permute-start.3) | collective-permute-done | bytes 544 | tf_op jit(solution)/shard_map/ppermute | solution.py:341
  31.3 0.8 %collective-permute-start.2 = (f32[2,64]{1,0:T(2,128)S(1)}, f32[2,64]{1,0:T(2,128)S(1)}, u32[]{:S(2)}, u32[]{:S(2)}) collective-permute-start(f32[2,64]{1,0:T(2,128)S(1)} %get-tuple-element.21.p0_ref), channel_id=1, source_target_pairs={{0,1},{1,2},{2,3},{3,0},{4,5},{5,6},{6,7},{7,4},{8,9},{9,10},{10,1... | collective-permute-start | bytes 1544 | tf_op jit(solution)/shard_map/ppermute | solution.py:341
  32.1 0.1 broadcast_in_dim.18
  32.2 0.1 broadcast_in_dim.19.skip_ref
  32.3 0.0 copy-start.5
  32.3 0.1 reshape_squeeze.10.bc_ref
  32.4 2.9 %collective-permute-done.2.p1_ref.r1_ref = f32[2,64]{1,0:T(2,128)S(1)} collective-permute-done((f32[2,64]{1,0:T(2,128)S(1)}, f32[2,64]{1,0:T(2,128)S(1)}, u32[]{:S(2)}, u32[]{:S(2)}) %collective-permute-start.2) | collective-permute-done | bytes 544 | tf_op jit(solution)/shard_map/ppermute | solution.py:341
  35.3 0.0 collective-permute-done.rows_b_ref
  35.3 0.0 collective-permute-done.1.rows_a_ref
  35.3 0.0 copy-start.11
  35.3 0.0 copy-start.12
  35.3 0.6 copy-done.8
  35.9 0.0 copy-done.11
  35.9 0.0 copy-done.12
  35.9 4.4 %pre.1 = (bf16[2,64,2048]{2,1,0:T(8,128)(2,1)S(1)}, f32[2,64,2048]{2,1,0:T(8,128)S(1)}, f32[2,64,2048]{2,1,0:T(8,128)S(1)}, bf16[2,64,256]{2,1,0:T(8,128)(2,1)S(...) custom-call(s32[2]{0:T(128)S(1)} %copy-done.8, ...), custom_call_target="tpu_custom_call" | custom-call | flops 200000000 | bytes 5000000 | tf_op jit(solution)/shard_map/pre/pallas_call | solution.py:356
  40.4 0.0 collective-permute-done.5.state_b_ref
  40.4 0.0 collective-permute-done.6.state_a_ref
  40.4 2.1 %mid.1 = (bf16[2,64,2048]{2,1,0:T(8,128)(2,1)}, f32[2,64]{1,0:T(2,128)S(1)}, f32[2,64,2048]{2,1,0:T(8,128)S(1)}) custom-call(s32[2]{0:T(128)S(1)} %copy-done.8, f32[2,64,2048]{2,1,0:T(8,128)S(1)} %get-tuple-element.22.y_ref, f32[2,64,2048]{2,1,0:T(8,128)S(1)} %get-tuple-element.23.grow_ref, bf16[2,64,256]{2,1,0:T(8,128)(2,1)S(1)} %get-tuple-element.24.c_ref, ...), custom_call_target="tpu_custom_call" | custom-call | tf_op jit(solution)/shard_map/mid/pallas_call | solution.py:392
  42.4 1.0 %copy-done.3 = f32[2,64,2048]{2,1,0:T(8,128)} copy-done((f32[2,64,2048]{2,1,0:T(8,128)}, f32[2,64,2048]{2,1,0:T(8,128)S(1)}, u32[]{:S(2)}) %copy-start.3) | copy-done | bytes 1048600
  43.4 1.3 %collective-permute-start.7 = (bf16[2,64,2048]{2,1,0:T(8,128)(2,1)}, bf16[2,64,2048]{2,1,0:T(8,128)(2,1)}, u32[]{:S(2)}, u32[]{:S(2)}) collective-permute-start(bf16[2,64,2048]{2,1,0:T(8,128)(2,1)} %get-tuple-element.27), channel_id=1, source_target_pairs={{0,128},{1,129},{2,130},{3,131},{4,132},{5,133},{6,134},{7,135},{8... | collective-permute-start | bytes 1572872 | tf_op jit(solution)/shard_map/ppermute | solution.py:405
  44.7 1.3 %collective-permute-start.10 = (f32[2,64]{1,0:T(2,128)S(1)}, f32[2,64]{1,0:T(2,128)S(1)}, u32[]{:S(2)}, u32[]{:S(2)}) collective-permute-start(f32[2,64]{1,0:T(2,128)S(1)} %get-tuple-element.28), channel_id=1, source_target_pairs={{0,131},{1,128},{2,129},{3,130},{4,135},{5,132},{6,133},{7,134},{8... | collective-permute-start | bytes 1544 | tf_op jit(solution)/shard_map/ppermute | solution.py:407
  46.0 1.3 %collective-permute-start.9 = (f32[2,64]{1,0:T(2,128)S(1)}, f32[2,64]{1,0:T(2,128)S(1)}, u32[]{:S(2)}, u32[]{:S(2)}) collective-permute-start(f32[2,64]{1,0:T(2,128)S(1)} %get-tuple-element.28), channel_id=1, source_target_pairs={{0,130},{1,131},{2,128},{3,129},{4,134},{5,135},{6,132},{7,133},{8... | collective-permute-start | bytes 1544 | tf_op jit(solution)/shard_map/ppermute | solution.py:407
  47.3 1.5 %collective-permute-start.8 = (f32[2,64]{1,0:T(2,128)S(1)}, f32[2,64]{1,0:T(2,128)S(1)}, u32[]{:S(2)}, u32[]{:S(2)}) collective-permute-start(f32[2,64]{1,0:T(2,128)S(1)} %get-tuple-element.28), channel_id=1, source_target_pairs={{0,129},{1,130},{2,131},{3,128},{4,133},{5,134},{6,135},{7,132},{8... | collective-permute-start | bytes 1544 | tf_op jit(solution)/shard_map/ppermute | solution.py:407
  48.8 2.5 %collective-permute-done.10.q3_ref = f32[2,64]{1,0:T(2,128)S(1)} collective-permute-done((f32[2,64]{1,0:T(2,128)S(1)}, f32[2,64]{1,0:T(2,128)S(1)}, u32[]{:S(2)}, u32[]{:S(2)}) %collective-permute-start.10) | collective-permute-done | bytes 544 | tf_op jit(solution)/shard_map/ppermute | solution.py:407
  51.3 3.1 %collective-permute-done.9.q2_ref = f32[2,64]{1,0:T(2,128)S(1)} collective-permute-done((f32[2,64]{1,0:T(2,128)S(1)}, f32[2,64]{1,0:T(2,128)S(1)}, u32[]{:S(2)}, u32[]{:S(2)}) %collective-permute-start.9) | collective-permute-done | bytes 544 | tf_op jit(solution)/shard_map/ppermute | solution.py:407
  54.4 2.1 %collective-permute-done.8.q1_ref = f32[2,64]{1,0:T(2,128)S(1)} collective-permute-done((f32[2,64]{1,0:T(2,128)S(1)}, f32[2,64]{1,0:T(2,128)S(1)}, u32[]{:S(2)}, u32[]{:S(2)}) %collective-permute-start.8) | collective-permute-done | bytes 544 | tf_op jit(solution)/shard_map/ppermute | solution.py:407
  56.6 0.0 collective-permute-done.7.moved_ref
  56.6 1.2 %copy-done.4 = f32[2,64,2048]{2,1,0:T(8,128)S(1)} copy-done((f32[2,64,2048]{2,1,0:T(8,128)S(1)}, f32[2,64,2048]{2,1,0:T(8,128)}, u32[]{:S(2)}) %copy-start.4) | copy-done | bytes 1048600
  57.8 4.9 %last.1 = (bf16[2,64,2048]{2,1,0:T(8,128)(2,1)}, bf16[2,2048,128]{2,1,0:T(8,128)(2,1)}, bf16[3,2,2048]{2,1,0:T(2,128)(2,1)}) custom-call(s32[2]{0:T(128)S(1)} %copy-done.8, s32[1]{0:T(128)} %bitcast.sec_ref, bf16[2,64,2048]{2,1,0:T(8,128)(2,1)S(1)} %copy-done.1, bf16[2,64,2048]{2,1,0:T(8,128)(2,1)} %collective-permute-done.7.moved_ref, ...), custom_call_target="tpu_custom_call" | custom-call | tf_op jit(solution)/shard_map/last/pallas_call | solution.py:412
  (24 shorter events, 0.1 us)
Async XLA Ops:
  0.7 0.7 %copy-start.16 = (s32[64]{0:T(128)S(1)}, s32[64]{0:T(128)}, u32[]{:S(2)}) copy-start(s32[64]{0:T(128)} %param.21) | copy-start | bytes 772
  5.9 1.0 %copy-start = (bf16[2,64,2048]{2,1,0:T(8,128)(2,1)S(1)}, bf16[2,64,2048]{2,1,0:T(8,128)(2,1)}, u32[]{:S(2)}) copy-start(bf16[2,64,2048]{2,1,0:T(8,128)(2,1)} %stream_ref.7) | copy-start | bytes 1572868
  6.9 1.2 %copy-start.2 = (bf16[1,2,32,64,128]{4,3,2,1,0:T(8,128)(2,1)S(1)}, bf16[1,2,32,64,128]{4,3,2,1,0:T(8,128)(2,1)}, u32[]{:S(2)}) copy-start(bf16[1,2,32,64,128]{4,3,2,1,0:T(8,128)(2,1)} %param.16) | copy-start | bytes 3145732
  8.2 10.4 %copy-start.15 = (bf16[1,2,3,2,256]{4,3,2,1,0:T(2,128)(2,1)S(1)}, bf16[1,2,3,2,256]{4,3,2,1,0:T(2,128)(2,1)}, u32[]{:S(2)}) copy-start(bf16[1,2,3,2,256]{4,3,2,1,0:T(2,128)(2,1)} %param.18) | copy-start | bytes 18436
  8.2 10.4 %copy-start.14 = (bf16[1,2,3,2048]{3,1,2,0:T(2,128)(2,1)S(1)}, bf16[1,2,3,2048]{3,1,2,0:T(2,128)(2,1)}, u32[]{:S(2)}) copy-start(bf16[1,2,3,2048]{3,1,2,0:T(2,128)(2,1)} %param.17) | copy-start | bytes 73732
  8.2 24.0 %copy-start.17 = (f32[1,32]{1,0:T(1,128)S(1)}, f32[1,32]{1,0:T(1,128)}, u32[]{:S(2)}) copy-start(f32[1,32]{1,0:T(1,128)} %param.28) | copy-start | bytes 388
  8.2 24.1 %copy-start.13 = (bf16[1,2,64,2,256]{4,3,2,1,0:T(2,128)(2,1)S(1)}, bf16[1,2,64,2,256]{4,3,2,1,0:T(2,128)(2,1)}, u32[]{:S(2)}) copy-start(bf16[1,2,64,2,256]{4,3,2,1,0:T(2,128)(2,1)} %param.19) | copy-start | bytes 393220
  8.2 27.1 %copy-start.7 = (f32[1,2048]{1,0:T(1,128)S(1)}, f32[1,2048]{1,0:T(1,128)}, u32[]{:S(2)}) copy-start(f32[1,2048]{1,0:T(1,128)} %gain_in_ref.1) | copy-start | bytes 24580
  8.2 27.1 %copy-start.9 = (f32[1,2,64,32]{2,3,1,0:T(8,128)S(1)}, f32[1,2,64,32]{2,3,1,0:T(8,128)}, u32[]{:S(2)}) copy-start(f32[1,2,64,32]{2,3,1,0:T(8,128)} %param.20) | copy-start | bytes 49156
  8.2 27.1 %copy-start.10 = (f32[1,4,2,256]{3,2,1,0:T(2,128)S(1)}, f32[1,4,2,256]{3,2,1,0:T(2,128)}, u32[]{:S(2)}) copy-start(f32[1,4,2,256]{3,2,1,0:T(2,128)} %param.25) | copy-start | bytes 24580
  9.7 25.6 %copy-start.1 = (bf16[2,64,2048]{2,1,0:T(8,128)(2,1)S(1)}, bf16[2,64,2048]{2,1,0:T(8,128)(2,1)}, u32[]{:S(2)}) copy-start(bf16[2,64,2048]{2,1,0:T(8,128)(2,1)} %stream_ref.7) | copy-start | bytes 1572868
  9.7 30.6 %collective-permute-start.5 = (bf16[2048,128]{1,0:T(8,128)(2,1)}, bf16[2048,128]{1,0:T(8,128)(2,1)S(1)}, u32[]{:S(2)}, u32[]{:S(2)}) collective-permute-start(bf16[2048,128]{1,0:T(8,128)(2,1)} %get-tuple-element.25), channel_id=1, source_target_pairs={{0,4},{4,8},{8,12},{12,16},{16,20},{20,24},{24,28},{28,32},{32,36}... | collective-permute-start | bytes 1572872 | tf_op jit(solution)/shard_map/ppermute | solution.py:341
  11.9 28.5 %collective-permute-start.6 = (bf16[2048,128]{1,0:T(8,128)(2,1)}, bf16[2048,128]{1,0:T(8,128)(2,1)S(1)}, u32[]{:S(2)}, u32[]{:S(2)}) collective-permute-start(bf16[2048,128]{1,0:T(8,128)(2,1)} %get-tuple-element.26), channel_id=1, source_target_pairs={{0,124},{4,0},{8,4},{12,8},{16,12},{20,16},{24,20},{28,24},{32,28}... | collective-permute-start | bytes 1572872 | tf_op jit(solution)/shard_map/ppermute | solution.py:341
  18.7 16.6 %collective-permute-start = (bf16[3,2560]{1,0:T(4,128)(2,1)S(1)}, bf16[3,2560]{1,0:T(4,128)(2,1)S(1)}, u32[]{:S(2)}, u32[]{:S(2)}) collective-permute-start(bf16[3,2560]{1,0:T(4,128)(2,1)S(1)} %bitcast.33), channel_id=1, source_target_pairs={{0,4},{4,8},{8,12},{12,16},{16,20},{20,24},{24,28},{28,32},{32,36}... | collective-permute-start | bytes 46088 | tf_op jit(solution)/shard_map/ppermute | solution.py:341
  18.8 16.5 %collective-permute-start.1 = (bf16[3,2560]{1,0:T(4,128)(2,1)S(1)}, bf16[3,2560]{1,0:T(4,128)(2,1)S(1)}, u32[]{:S(2)}, u32[]{:S(2)}) collective-permute-start(bf16[3,2560]{1,0:T(4,128)(2,1)S(1)} %bitcast.34), channel_id=1, source_target_pairs={{0,124},{4,0},{8,4},{12,8},{16,12},{20,16},{24,20},{28,24},{32,28}... | collective-permute-start | bytes 46088 | tf_op jit(solution)/shard_map/ppermute | solution.py:341
  23.6 3.5 %collective-permute-start.4 = (f32[2,64]{1,0:T(2,128)S(1)}, f32[2,64]{1,0:T(2,128)S(1)}, u32[]{:S(2)}, u32[]{:S(2)}) collective-permute-start(f32[2,64]{1,0:T(2,128)S(1)} %get-tuple-element.21.p0_ref), channel_id=1, source_target_pairs={{0,3},{1,0},{2,1},{3,2},{4,7},{5,4},{6,5},{7,6},{8,11},{9,8},{10,9... | collective-permute-start | bytes 1544 | tf_op jit(solution)/shard_map/ppermute | solution.py:341
  27.1 4.2 %collective-permute-start.3 = (f32[2,64]{1,0:T(2,128)S(1)}, f32[2,64]{1,0:T(2,128)S(1)}, u32[]{:S(2)}, u32[]{:S(2)}) collective-permute-start(f32[2,64]{1,0:T(2,128)S(1)} %get-tuple-element.21.p0_ref), channel_id=1, source_target_pairs={{0,2},{1,3},{2,0},{3,1},{4,6},{5,7},{6,4},{7,5},{8,10},{9,11},{10,... | collective-permute-start | bytes 1544 | tf_op jit(solution)/shard_map/ppermute | solution.py:341
  31.3 3.9 %collective-permute-start.2 = (f32[2,64]{1,0:T(2,128)S(1)}, f32[2,64]{1,0:T(2,128)S(1)}, u32[]{:S(2)}, u32[]{:S(2)}) collective-permute-start(f32[2,64]{1,0:T(2,128)S(1)} %get-tuple-element.21.p0_ref), channel_id=1, source_target_pairs={{0,1},{1,2},{2,3},{3,0},{4,5},{5,6},{6,7},{7,4},{8,9},{9,10},{10,1... | collective-permute-start | bytes 1544 | tf_op jit(solution)/shard_map/ppermute | solution.py:341
  32.3 3.0 %copy-start.5 = (f32[1,4,2048]{2,1,0:T(4,128)S(1)}, f32[1,4,2048]{2,1,0:T(4,128)}, u32[]{:S(2)}) copy-start(f32[1,4,2048]{2,1,0:T(4,128)} %param.24) | copy-start | bytes 98308
  35.3 0.7 %copy-start.8 = (s32[2]{0:T(128)S(1)}, s32[2]{0:T(128)}, u32[]{:S(2)}) copy-start(s32[2]{0:T(128)} %len_ref.5) | copy-start | bytes 28
  35.3 0.7 %copy-start.11 = (f32[1,32]{1,0:T(1,128)S(1)}, f32[1,32]{1,0:T(1,128)}, u32[]{:S(2)}) copy-start(f32[1,32]{1,0:T(1,128)} %log_ref.1) | copy-start | bytes 388
  35.3 0.7 %copy-start.12 = (f32[1,32]{1,0:T(1,128)S(1)}, f32[1,32]{1,0:T(1,128)}, u32[]{:S(2)}) copy-start(f32[1,32]{1,0:T(1,128)} %bias_ref.1) | copy-start | bytes 388
  35.9 4.4 %copy-start.6 = (f32[1,2048]{1,0:T(1,128)S(1)}, f32[1,2048]{1,0:T(1,128)}, u32[]{:S(2)}) copy-start(f32[1,2048]{1,0:T(1,128)} %gain_ref.5) | copy-start | bytes 24580
  42.4 1.0 %copy-start.3 = (f32[2,64,2048]{2,1,0:T(8,128)}, f32[2,64,2048]{2,1,0:T(8,128)S(1)}, u32[]{:S(2)}) copy-start(f32[2,64,2048]{2,1,0:T(8,128)S(1)} %get-tuple-element.31.read_ref) | copy-start | bytes 3145732
  43.4 13.1 %collective-permute-start.7 = (bf16[2,64,2048]{2,1,0:T(8,128)(2,1)}, bf16[2,64,2048]{2,1,0:T(8,128)(2,1)}, u32[]{:S(2)}, u32[]{:S(2)}) collective-permute-start(bf16[2,64,2048]{2,1,0:T(8,128)(2,1)} %get-tuple-element.27), channel_id=1, source_target_pairs={{0,128},{1,129},{2,130},{3,131},{4,132},{5,133},{6,134},{7,135},{8... | collective-permute-start | bytes 1572872 | tf_op jit(solution)/shard_map/ppermute | solution.py:405
  44.7 6.6 %collective-permute-start.10 = (f32[2,64]{1,0:T(2,128)S(1)}, f32[2,64]{1,0:T(2,128)S(1)}, u32[]{:S(2)}, u32[]{:S(2)}) collective-permute-start(f32[2,64]{1,0:T(2,128)S(1)} %get-tuple-element.28), channel_id=1, source_target_pairs={{0,131},{1,128},{2,129},{3,130},{4,135},{5,132},{6,133},{7,134},{8... | collective-permute-start | bytes 1544 | tf_op jit(solution)/shard_map/ppermute | solution.py:407
  46.0 8.4 %collective-permute-start.9 = (f32[2,64]{1,0:T(2,128)S(1)}, f32[2,64]{1,0:T(2,128)S(1)}, u32[]{:S(2)}, u32[]{:S(2)}) collective-permute-start(f32[2,64]{1,0:T(2,128)S(1)} %get-tuple-element.28), channel_id=1, source_target_pairs={{0,130},{1,131},{2,128},{3,129},{4,134},{5,135},{6,132},{7,133},{8... | collective-permute-start | bytes 1544 | tf_op jit(solution)/shard_map/ppermute | solution.py:407
  47.3 9.2 %collective-permute-start.8 = (f32[2,64]{1,0:T(2,128)S(1)}, f32[2,64]{1,0:T(2,128)S(1)}, u32[]{:S(2)}, u32[]{:S(2)}) collective-permute-start(f32[2,64]{1,0:T(2,128)S(1)} %get-tuple-element.28), channel_id=1, source_target_pairs={{0,129},{1,130},{2,131},{3,128},{4,133},{5,134},{6,135},{7,132},{8... | collective-permute-start | bytes 1544 | tf_op jit(solution)/shard_map/ppermute | solution.py:407
  56.6 1.2 %copy-start.4 = (f32[2,64,2048]{2,1,0:T(8,128)S(1)}, f32[2,64,2048]{2,1,0:T(8,128)}, u32[]{:S(2)}) copy-start(f32[2,64,2048]{2,1,0:T(8,128)} %copy-done.3) | copy-start | bytes 3145732
where the time goes:
time: 63.2 us; the launch traced here: 62.7 us
  starting transfers between devices  24.7 us (39%)
  waiting for transfers between devices  13.4 us (21%)
  Pallas kernels  13 us (21%)
  local copies, waits for them, and re-layouts  6.65 us (11%)
  between operations  4.81 us (8%)
    ppermute x7, starting transfers between devices, along(): lax.ppermute(value, axis, [(i, (i + steps) % size) for i in range(size)])  19.4 us
    ppermute x3, waiting for transfers between devices, on_device(): lax.ppermute(mid_part, ('section', 'tensor'), [(i, tens + (i + k) % tens)...  7.76 us
    unnamed x39, local copies, waits for them, and re-layouts  5.81 us
    ppermute x7, waiting for transfers between devices, along(): lax.ppermute(value, axis, [(i, (i + steps) % size) for i in range(size)])  5.64 us
    pallas_call x1, Pallas kernels, on_device(): pl.pallas_call(last_kernel, out_shape=(shape((KIDS, T, CD), BF16), shape(...  4.94 us
    pallas_call x1, Pallas kernels, on_device(): pl.pallas_call(pre_kernel, out_shape=(shape((KIDS, T, CD), BF16), shape((...  4.43 us
    ppermute x3, starting transfers between devices, on_device(): lax.ppermute(mid_part, ('section', 'tensor'), [(i, tens + (i + k) % tens)...  4.06 us
    pallas_call x1, Pallas kernels, on_device(): pl.pallas_call(mid_kernel, out_shape=(shape((KIDS, T, CD), BF16), shape((...  2.05 us
  transfers between devices with their start and end apart: 11, of which 6 were waited for; matrix products, arithmetic and copies ran while one was open for 1% of the time, Pallas kernels for 7%

commit v1 on v0

v1 whole, which is shorter than its diff:
```python
import functools

import jax
import jax.numpy as jnp
from jax import lax
from jax.experimental import pallas as pl
from jax.experimental.pallas import tpu as pltpu
from jax.sharding import PartitionSpec as P

CH = 8192
EPS = 1e-05
KIDS = 2
T = 64
CD = 2048
HD = 32
N = 128
GC = 1024
F32 = jnp.float32
BF16 = jnp.bfloat16
HIGHEST = lax.Precision.HIGHEST
VMEM = pl.BlockSpec(memory_space=pltpu.VMEM)
SMEM = pl.BlockSpec(memory_space=pltpu.SMEM)
HBM = pl.BlockSpec(memory_space=pl.ANY)
BIG = 60


def iota(shape, dim):
    return lax.broadcasted_iota(jnp.int32, shape, dim)


def as_row(col):
    size = col.shape[0]
    keep = iota((size, size), 0) == iota((size, size), 1)
    return jnp.sum(jnp.where(keep, col, 0.0), axis=0, keepdims=True)


def as_col(row):
    size = row.shape[1]
    keep = iota((size, size), 0) == iota((size, size), 1)
    return jnp.sum(jnp.where(keep, row, 0.0), axis=1, keepdims=True)


def silu(v):
    return 0.5 * v * (1.0 + jnp.tanh(0.5 * v))


def dot(a, b, dims, precision=None):
    return lax.dot_general(
        a, b, (dims, ((), ())), precision=precision, preferred_element_type=F32
    )


def three_parts(v):
    high = v.astype(BF16)
    rest = v - high.astype(F32)
    mid = rest.astype(BF16)
    low = (rest - mid.astype(F32)).astype(BF16)
    return [high, mid, low]


def pick_kernel(
    parents_in_ref,
    conv_x_in_ref,
    conv_bc_in_ref,
    state_in_ref,
    one_ref,
    two_ref,
    parents_ref,
    conv_x_ref,
    conv_bc_ref,
    state_ref,
    rows_ref,
    sems,
    out_sems,
):
    get_parents = pltpu.make_async_copy(parents_in_ref, parents_ref, sems.at[0])
    get_states = [
        pltpu.make_async_copy(state_in_ref.at[i], state_ref.at[i], sems.at[1 + i])
        for i in range(KIDS)
    ]
    get_x = pltpu.make_async_copy(conv_x_in_ref, conv_x_ref, sems.at[3])
    get_bc = pltpu.make_async_copy(conv_bc_in_ref, conv_bc_ref, sems.at[4])
    for copy in (get_parents, *get_states, get_x, get_bc):
        copy.start()
    peers = lax.axis_size("beam")
    me = lax.axis_index("beam")
    get_parents.wait()
    picks = (
        lax.rem(parents_ref[KIDS * lax.rem(me + 1, peers)], KIDS),
        lax.rem(parents_ref[KIDS * lax.rem(me + peers - 1, peers) + 1], KIDS),
    )
    outs = (one_ref, two_ref)
    for copy in get_states:
        copy.wait()
    puts = []
    for i in range(2):
        puts.append(
            pltpu.make_async_copy(state_ref.at[picks[i]], outs[i].at[:CD], out_sems.at[0, i])
        )
        puts[-1].start()
    get_x.wait()
    get_bc.wait()
    for i in range(2):
        low = picks[i] == 0
        pieces = []
        for k in range(3):
            both = conv_x_ref[k].astype(F32)
            row = jnp.where(low, both[0:1], both[1:2])
            pieces += [row[:, N * j : N * (j + 1)] for j in range(CD // N)]
        for k in range(3):
            both = conv_bc_ref[picks[i], k].astype(F32)
            pieces += [both[p : p + 1, N * j : N * (j + 1)] for p in range(2) for j in range(2)]
        pieces.append(jnp.zeros((4, N), F32))
        rows_ref[i] = jnp.concatenate(pieces, axis=0).astype(BF16)
        puts.append(pltpu.make_async_copy(rows_ref.at[i], outs[i].at[CD:], out_sems.at[1, i]))
        puts[-1].start()
    for copy in puts:
        copy.wait()


def square_kernel(stream_ref, part_ref):
    for c in range(KIDS):
        s = stream_ref[c].astype(F32)
        part_ref[c : c + 1, :] = as_row(jnp.sum(s * s, axis=1, keepdims=True))


def fresh_x(s, total, rows, gain, taps, valid, px_ref):
    scale = lax.rsqrt(total / CH + EPS)
    for k in range(3):
        for j in range(CD // N):
            at = 16 * k + j
            px_ref[5 + k : 6 + k, N * j : N * (j + 1)] = rows[at : at + 1, :]
    px_ref[8:72, :] = (s * scale * gain).astype(BF16).astype(F32)
    acc = taps[0:1] * px_ref[5:69, :]
    for k in range(1, 4):
        acc = acc + taps[k : k + 1] * px_ref[5 + k : 69 + k, :]
    return silu(acc) * valid


def fresh_bc(rows, bc, taps_ref, pbc_ref):
    for k in range(3):
        for j in range(4):
            at = 48 + 4 * k + j
            pbc_ref[5 + k : 6 + k, N * j : N * (j + 1)] = rows[at : at + 1, :]
    pbc_ref[8:72, :] = bc.astype(F32)
    acc = 0.0
    for k in range(4):
        taps = jnp.concatenate([taps_ref[k, 0:1, :], taps_ref[k, 1:2, :]], axis=1)
        acc = acc + taps * pbc_ref[5 + k : 69 + k, :]
    return silu(acc)


def mixing(bc, decay_ref, mix_ref):
    for g in range(2):
        bg = bc[:, N * g : N * (g + 1)]
        cg = bc[:, 256 + N * g : 256 + N * (g + 1)]
        inner = dot(cg, jnp.concatenate([bg, bg], axis=0), ((1,), (1,)), HIGHEST)
        for j in range(8 * g, 8 * g + 8):
            at = slice(N * j, N * (j + 1))
            mix_ref[:, at] = (decay_ref[:, at] * inner).astype(BF16)


def readout(bc, state, grow):
    cb = bc[:, 256:].astype(BF16)
    read = [
        dot(cb[:, N * g : N * (g + 1)], state[GC * g : GC * (g + 1), :], ((1,), (1,)))
        for g in range(2)
    ]
    return jnp.concatenate(read, axis=1) * grow


def intra(mix_ref, x):
    xb = x.astype(BF16)
    outs = []
    lane = iota((T, 256), 1) // 64
    masks = [jnp.where(lane == j, 1.0, 0.0).astype(BF16) for j in range(4)]
    for q in range(CD // 256):
        xq = xb[:, 256 * q : 256 * (q + 1)]
        rhs = jnp.concatenate([xq * mask for mask in masks], axis=0)
        outs.append(dot(mix_ref[:, 256 * q : 256 * (q + 1)], rhs, ((1,), (0,))))
    return jnp.concatenate(outs, axis=1)


def finish(y, s, gain, valid):
    outs = []
    for g in range(CD // GC):
        part = y[:, GC * g : GC * (g + 1)]
        mean = jnp.sum(part * part, axis=1, keepdims=True) * (1.0 / GC)
        outs.append(part * lax.rsqrt(mean + EPS))
    z = jnp.concatenate(outs, axis=1) * gain
    return (s + z * valid).astype(BF16)


def valid_col(length):
    return jnp.where(iota((T, 1), 0) < length, 1.0, 0.0)


def spread_heads(compact):
    onehot = jnp.where(iota((HD, CD), 0) == iota((HD, CD), 1) // 64, 1.0, 0.0).astype(BF16)
    onehot = jnp.concatenate([onehot] * 3, axis=0)
    return dot(jnp.concatenate(three_parts(compact), axis=0), onehot, ((0,), (0,)))


def pre_kernel(
    len_ref, inc_ref, log_ref, bias_ref, decay0_ref, decay1_ref, grow_ref, weight_ref, last_ref
):
    rate = as_col(jnp.exp(log_ref[...]))
    bias = as_col(bias_ref[...])
    upper = jnp.where(iota((T, T), 0) <= iota((T, T), 1), 1.0, 0.0)
    diag = iota((T, CD), 1) % T == iota((T, CD), 0)
    causal = iota((T, CD), 0) >= iota((T, CD), 1) % T
    for c in range(KIDS):
        valid_row = jnp.where(iota((1, T), 1) < len_ref[c], 1.0, 0.0)
        raw = inc_ref[c] + bias
        dt = (jnp.maximum(raw, 0.0) + jnp.log1p(jnp.exp(-jnp.abs(raw)))) * valid_row
        cum = dot(-dt * rate, upper, ((1,), (0,)), HIGHEST)
        final = cum[:, T - 1 : T]
        last_ref[c] = jnp.broadcast_to(jnp.exp(final), (HD, N))
        grow_ref[c] = jnp.exp(cum)
        weight_ref[c] = jnp.exp(final - cum) * dt
        edt = spread_heads(dt)
        ecum = spread_heads(cum)
        row_dt = jnp.sum(jnp.where(diag, edt, 0.0), axis=0, keepdims=True)
        row_cum = jnp.sum(jnp.where(diag, ecum, 0.0), axis=0, keepdims=True)
        gap = jnp.exp(jnp.minimum(ecum - row_cum, 0.0))
        (decay0_ref, decay1_ref)[c][...] = jnp.where(causal, gap * row_dt, 0.0)


def mid_kernel(
    c,
    len_ref,
    message_ref,
    bc_ref,
    taps_bc_ref,
    stream_ref,
    p0_ref,
    p1_ref,
    p2_ref,
    p3_ref,
    gain_in_ref,
    taps_ref,
    skip_ref,
    gain_ref,
    decay_ref,
    grow_ref,
    *refs,
):
    if c == 1:
        early_ref, early_part_ref, early_bc_ref = refs[:3]
        refs = refs[3:]
    out_ref, part_ref, bc_out_ref, mix_ref, read_ref, b_ref = refs[:6]
    pbc_ref, px_ref = refs[6:]
    length = len_ref[c]
    rows = message_ref[CD:, :].astype(F32)
    bc = fresh_bc(rows, bc_ref[c], taps_bc_ref, pbc_ref)
    if c == 1:
        bc_out_ref[0] = early_bc_ref[0]
    for k in range(3):
        row = pbc_ref[pl.ds(5 + length + k, 1), :]
        bc_out_ref[c, k] = jnp.concatenate([row[:, :256], row[:, 256:]], axis=0).astype(BF16)
    b_ref[...] = bc[:, :256].astype(BF16)
    read = readout(bc, message_ref[:CD, :], spread_heads(grow_ref[c]))
    read_ref[...] = read.astype(BF16)
    mixing(bc, decay_ref, mix_ref)
    s = stream_ref[c].astype(F32)
    valid = valid_col(length)
    total = p0_ref[c : c + 1] + p1_ref[c : c + 1] + p2_ref[c : c + 1] + p3_ref[c : c + 1]
    x = fresh_x(s, as_col(total), rows, gain_in_ref[...], taps_ref[...], valid, px_ref)
    y = intra(mix_ref, x) + skip_ref[...] * x + read
    out = finish(y, s, gain_ref[...], valid)
    s = out.astype(F32)
    part = as_row(jnp.sum(s * s, axis=1, keepdims=True))
    if c == 0:
        out_ref[...] = out
        part_ref[...] = part
    else:
        out_ref[0] = early_ref[...]
        out_ref[1] = out
        part_ref[0:1, :] = early_part_ref[...]
        part_ref[1:2, :] = part


def others_kernel(sec_ref, r1_ref, r2_ref, r3_ref, q1_ref, q2_ref, q3_ref, others_ref):
    others_ref[...] = jnp.where(
        sec_ref[0] == 0,
        r1_ref[...] + r2_ref[...] + r3_ref[...],
        q1_ref[...] + q2_ref[...] + q3_ref[...],
    )


def last_kernel(
    sec_ref,
    len_ref,
    others_ref,
    gain_in_ref,
    taps_ref,
    skip_ref,
    gain_ref,
    b0_ref,
    b1_ref,
    last_ref,
    stream_ref,
    moved_ref,
    weight_ref,
    mix0_ref,
    mix1_ref,
    read0_ref,
    read1_ref,
    message0_in_ref,
    message1_in_ref,
    out_in_ref,
    new_in_ref,
    x_out_ref,
    px_ref,
    message_ref,
    out_ref,
    new_ref,
    sems,
):
    first = sec_ref[0] == 0

    gets = []
    puts = []
    for c in range(KIDS):
        gets.append(
            pltpu.make_async_copy(
                (message0_in_ref, message1_in_ref)[c], message_ref.at[c], sems.at[0, c]
            )
        )
        gets[c].start()
        puts.append(pltpu.make_async_copy(out_ref.at[c], out_in_ref.at[c], sems.at[1, c]))
        puts.append(pltpu.make_async_copy(new_ref.at[c], new_in_ref.at[c], sems.at[2, c]))
    tails = []
    for c in range(KIDS):
        length = len_ref[c]
        valid = valid_col(length)
        b_ref = (b0_ref, b1_ref)[c]
        s = jnp.where(first, stream_ref[c].astype(F32), moved_ref[c].astype(F32))
        total = jnp.sum(s * s, axis=1, keepdims=True) + as_col(others_ref[c : c + 1])
        gets[c].wait()
        rows = message_ref[c, CD:, :].astype(F32)
        x = fresh_x(s, total, rows, gain_in_ref[...], taps_ref[...], valid, px_ref)
        tails.append([px_ref[pl.ds(5 + length + k, 1), :] for k in range(3)])
        y = intra((mix0_ref, mix1_ref)[c], x) + skip_ref[...] * x
        y = y + (read0_ref, read1_ref)[c][...].astype(F32)
        out_ref[c] = finish(y, s, gain_ref[...], valid)
        puts[2 * c].start()
        xw = (x * spread_heads(weight_ref[c])).astype(BF16)
        for g in range(2):
            fresh = dot(xw[:, GC * g : GC * (g + 1)], b_ref[:, N * g : N * (g + 1)], ((0,), (0,)))
            for h in range(16 * g, 16 * g + 16):
                at = slice(64 * h, 64 * (h + 1))
                off = 64 * (h - 16 * g)
                new_ref[c, at, :] = (
                    last_ref[c, h : h + 1, :] * message_ref[c, at, :].astype(F32)
                    + fresh[off : off + 64]
                ).astype(BF16)
        puts[2 * c + 1].start()
    for k in range(3):
        x_out_ref[k] = jnp.concatenate([tails[0][k], tails[1][k]], axis=0).astype(BF16)
    for copy in puts:
        copy.wait()


def shape(dims, kind):
    return jax.ShapeDtypeStruct(dims, kind)


def params(mib):
    return pltpu.CompilerParams(vmem_limit_bytes=mib * 2**20)


def cost(flops, moved, exps=0):
    return pl.CostEstimate(flops=flops, bytes_accessed=moved, transcendentals=exps)


def on_device(
    streams_in,
    beam_state_cache,
    conv_x_cache,
    conv_bc_cache,
    bc_inputs,
    unbiased_increments,
    parents,
    lengths,
    input_norm_gain,
    conv_x_weight,
    conv_bc_weight,
    a_log,
    dt_bias,
    skip_gain,
    out_gain,
):
    tens = lax.axis_size("tensor")
    peers = lax.axis_size("beam")
    section = lax.axis_index("section").astype(jnp.int32)[None]
    message = shape((CD + 64, N), BF16)
    fwd, bwd = pl.pallas_call(
        pick_kernel,
        out_shape=(message, message),
        in_specs=[HBM] * 4,
        out_specs=(HBM, HBM),
        scratch_shapes=[
            pltpu.SMEM(parents.shape, jnp.int32),
            pltpu.VMEM((3, KIDS, CD), BF16),
            pltpu.VMEM((KIDS, 3, 2, 256), BF16),
            pltpu.VMEM((KIDS, CD, N), BF16),
            pltpu.VMEM((2, 64, N), BF16),
            pltpu.SemaphoreType.DMA((5,)),
            pltpu.SemaphoreType.DMA((2, 2)),
        ],
        compiler_params=params(BIG),
        name="pick",
    )(
        parents,
        jnp.transpose(conv_x_cache[0], (1, 0, 2)),
        conv_bc_cache[0],
        beam_state_cache[0].reshape(KIDS, CD, N),
    )
    part = pl.pallas_call(
        square_kernel,
        out_shape=shape((KIDS, T), F32),
        in_specs=[VMEM],
        out_specs=VMEM,
        compiler_params=params(4),
        name="square",
    )(streams_in)

    def along(value, axis, steps):
        size = lax.axis_size(axis)
        return lax.ppermute(value, axis, [(i, (i + steps) % size) for i in range(size)])

    messages = (along(fwd, "beam", 1), along(bwd, "beam", -1))
    r1, r2, r3 = [along(part, "tensor", k) for k in range(1, tens)]

    bc = bc_inputs[0].reshape(KIDS, T, 512)
    inc = jnp.transpose(unbiased_increments[0], (0, 2, 1))
    skip = jnp.repeat(skip_gain, 64, axis=1)
    taps_bc = conv_bc_weight[0]
    taps = conv_x_weight[0]
    *decays, grow, weight, last = pl.pallas_call(
        pre_kernel,
        out_shape=(
            shape((T, CD), F32),
            shape((T, CD), F32),
            shape((KIDS, HD, T), F32),
            shape((KIDS, HD, T), F32),
            shape((KIDS, HD, N), F32),
        ),
        in_specs=[SMEM] + [VMEM] * 3,
        out_specs=tuple([VMEM] * 5),
        compiler_params=params(10),
        cost_estimate=cost(200_000_000, 5_000_000, 1_000_000),
        name="pre",
    )(lengths, inc, a_log, dt_bias)

    early = ()
    kept = []
    for c in range(KIDS):
        out_dims = ((T, CD), (1, T)) if c == 0 else ((KIDS, T, CD), (KIDS, T))
        result = pl.pallas_call(
            functools.partial(mid_kernel, c),
            out_shape=(
                shape(out_dims[0], BF16),
                shape(out_dims[1], F32),
                shape((c + 1, 3, 2, 256), BF16),
                shape((T, CD), BF16),
                shape((T, CD), BF16),
                shape((T, 256), BF16),
            ),
            in_specs=[SMEM] + [VMEM] * (14 + len(early)),
            out_specs=tuple([VMEM] * 6),
            scratch_shapes=[pltpu.VMEM((72, 512), F32), pltpu.VMEM((72, CD), F32)],
            compiler_params=params(12),
            cost_estimate=cost(100_000_000, 3_000_000, 500_000),
            name="mid%d" % c,
        )(
            lengths,
            messages[c],
            bc,
            taps_bc,
            streams_in,
            part,
            r1,
            r2,
            r3,
            input_norm_gain,
            taps,
            skip,
            out_gain,
            decays[c],
            grow,
            *early,
        )
        early = result[:3]
        kept.append(result[3:])
    mid, mid_part, bc_out = early
    mixes, reads, b_mats = zip(*kept)

    moved = lax.ppermute(mid, "section", [(0, 1), (1, 0)])
    q1, q2, q3 = [
        lax.ppermute(
            mid_part, ("section", "tensor"), [(i, tens + (i + k) % tens) for i in range(tens)]
        )
        for k in range(1, tens)
    ]

    others = pl.pallas_call(
        others_kernel,
        out_shape=shape((KIDS, T), F32),
        in_specs=[SMEM] + [VMEM] * 6,
        out_specs=VMEM,
        compiler_params=params(4),
        cost_estimate=cost(10_000_000_000, 100_000_000, 0),
        name="others",
    )(section, r1, r2, r3, q1, q2, q3)

    out, new, x_out = pl.pallas_call(
        last_kernel,
        out_shape=(
            shape((KIDS, T, CD), BF16),
            shape((KIDS, CD, N), BF16),
            shape((3, KIDS, CD), BF16),
        ),
        in_specs=[SMEM] * 2 + [VMEM] * 15 + [HBM] * 2,
        out_specs=(HBM, HBM, VMEM),
        scratch_shapes=[
            pltpu.VMEM((72, CD), F32),
            pltpu.VMEM((KIDS, CD + 64, N), BF16),
            pltpu.VMEM((KIDS, T, CD), BF16),
            pltpu.VMEM((KIDS, CD, N), BF16),
            pltpu.SemaphoreType.DMA((3, KIDS)),
        ],
        compiler_params=params(14),
        cost_estimate=cost(200_000_000, 5_000_000, 1_000_000),
        name="last",
    )(
        section,
        lengths,
        others,
        input_norm_gain,
        taps,
        skip,
        out_gain,
        *b_mats,
        last,
        streams_in,
        moved,
        weight,
        *mixes,
        *reads,
        *messages,
    )
    return (
        out[None],
        new.reshape(1, KIDS, HD, 64, N),
        jnp.transpose(x_out, (1, 0, 2))[None],
        bc_out[None],
    )


def solution(mesh):
    placed = (
        P("beam", None, "tensor"),
        P("section", "beam", "tensor", None, None),
        P("section", "beam", None, "tensor"),
        P("section", "beam", None, None, "tensor"),
        P("section", "beam", None, None, "tensor"),
        P("section", "beam", None, "tensor"),
        P(),
        P("beam"),
        P("section", "tensor"),
        P("section", None, "tensor"),
        P("section", None, None, "tensor"),
        P("section", "tensor"),
        P("section", "tensor"),
        P("section", "tensor"),
        P("section", "tensor"),
    )
    return jax.shard_map(
        on_device,
        mesh=mesh,
        in_specs=placed,
        out_specs=(
            P("section", "beam", None, "tensor"),
            P("section", "beam", "tensor", None, None),
            P("section", "beam", None, "tensor"),
            P("section", "beam", None, None, "tensor"),
        ),
        check_vma=False,
    )
```

time: 63.2 us -> 45.7 us (0.72)
  waiting for transfers between devices: 13.4 us -> 7.39 us
  local copies, waits for them, and re-layouts: 6.65 us -> 2.43 us
  starting transfers between devices: 24.7 us -> 20.5 us
  between operations: 4.81 us -> 0.84 us
  Pallas kernels: 13 us -> 14.4 us
    ppermute x7 -> x5, starting transfers between devices: 19.4 us -> 12.6 us  [along(): lax.ppermute(value, axis, [(i, (i + steps) % size) for i in range(size)])]
    ppermute x3, waiting for transfers between devices: 7.76 us -> 1.99 us  [on_device(): lax.ppermute(mid_part, ('section', 'tensor'), [(i, tens + (i + k) % tens)...]
    unnamed x39 -> x30, local copies, waits for them, and re-layouts: 5.81 us -> 2.18 us
    ppermute x1, starting transfers between devices: 1.28 us -> 4.01 us  [on_device(): moved = lax.ppermute(mid, 'section', [(0, 1), (1, 0)])]
    pallas_call x3 -> x6, Pallas kernels: 8.01 us -> 9.15 us  [the longest x2 5 us: on_device(): pl.pallas_call(functools.partial(mid_kernel, c), out_shape=(shape(out_dim...]
    ppermute x7 -> x5, waiting for transfers between devices: 5.64 us -> 5.4 us  [along(): lax.ppermute(value, axis, [(i, (i + steps) % size) for i in range(size)])]
  transfers between devices with their start and end apart: 11 -> 9, of which waited for: 6 -> 5; matrix products, arithmetic and copies ran while one was open for 1% -> 1% of each run, Pallas kernels for 7% -> 9%
where the time goes in v1:
time: 45.7 us; the launch traced here: 45.6 us
  starting transfers between devices  20.5 us (45%)
  Pallas kernels  14.4 us (32%)
  waiting for transfers between devices  7.39 us (16%)
  local copies, waits for them, and re-layouts  2.43 us (5%)
  between operations  0.84 us (2%)
    ppermute x5, starting transfers between devices, along(): lax.ppermute(value, axis, [(i, (i + steps) % size) for i in range(size)])  12.6 us
    ppermute x5, waiting for transfers between devices, along(): lax.ppermute(value, axis, [(i, (i + steps) % size) for i in range(size)])  5.4 us
    pallas_call x1, Pallas kernels, on_device(): pl.pallas_call(last_kernel, out_shape=(shape((KIDS, T, CD), BF16), shape(...  5.25 us
    pallas_call x2, Pallas kernels, on_device(): pl.pallas_call(functools.partial(mid_kernel, c), out_shape=(shape(out_dim...  5 us
    ppermute x1, starting transfers between devices, on_device(): moved = lax.ppermute(mid, 'section', [(0, 1), (1, 0)])  4.01 us
    ppermute x3, starting transfers between devices, on_device(): lax.ppermute(mid_part, ('section', 'tensor'), [(i, tens + (i + k) % tens)...  3.86 us
    pallas_call x1, Pallas kernels, on_device(): pl.pallas_call(pick_kernel, out_shape=(message, message), in_specs=[HBM]...  2.32 us
    unnamed x30, local copies, waits for them, and re-layouts  2.18 us
  transfers between devices with their start and end apart: 9, of which 5 were waited for; matrix products, arithmetic and copies ran while one was open for 1% of the time, Pallas kernels for 9%

profile of v1, /device:TPU:1, one launch (start us, length us, event | category | flops | bytes accessed | tf_op | source)
XLA Modules:
  0.0 45.6 jit_solution(2211468080272379265)
XLA Ops:
  0.6 0.0 copy-start
  0.6 2.3 %pick.1 = (bf16[2112,128]{1,0:T(8,128)(2,1)}, bf16[2112,128]{1,0:T(8,128)(2,1)}) custom-call(s32[64]{0:T(128)} %parents_in_ref.1, bf16[3,2,2048]{2,1,0:T(2,128)(2,1)} %bitcast.25, bf16[2,3,2,256]{3,2,1,0:T(2,128)(2,1)} %bitcast.26, bf16[2,2048,128]{2,1,0:T(8,128)(2,1)} %bitcast.24), custom_call_target="tpu_custom_call" | custom-call | tf_op jit(solution)/shard_map/pick/pallas_call | solution.py:398
  3.0 2.1 %collective-permute-start.4 = (bf16[2112,128]{1,0:T(8,128)(2,1)}, bf16[2112,128]{1,0:T(8,128)(2,1)S(1)}, u32[]{:S(2)}, u32[]{:S(2)}) collective-permute-start(bf16[2112,128]{1,0:T(8,128)(2,1)} %get-tuple-element.29), channel_id=1, source_target_pairs={{0,4},{4,8},{8,12},{12,16},{16,20},{20,24},{24,28},{28,32},{32,36}... | collective-permute-start | bytes 1622024 | tf_op jit(solution)/shard_map/ppermute | solution.py:431
  5.1 6.7 %collective-permute-start.3 = (bf16[2112,128]{1,0:T(8,128)(2,1)}, bf16[2112,128]{1,0:T(8,128)(2,1)S(1)}, u32[]{:S(2)}, u32[]{:S(2)}) collective-permute-start(bf16[2112,128]{1,0:T(8,128)(2,1)} %get-tuple-element.26), channel_id=1, source_target_pairs={{0,124},{4,0},{8,4},{12,8},{16,12},{20,16},{24,20},{28,24},{32,28}... | collective-permute-start | bytes 1622024 | tf_op jit(solution)/shard_map/ppermute | solution.py:431
  11.8 0.0 copy-done
  11.8 0.2 square.1.p0_ref
  12.0 0.0 copy-start.11
  12.0 0.0 copy-start.12
  12.0 2.8 %collective-permute-start.2 = (f32[2,64]{1,0:T(2,128)S(1)}, f32[2,64]{1,0:T(2,128)S(1)}, u32[]{:S(2)}, u32[]{:S(2)}) collective-permute-start(f32[2,64]{1,0:T(2,128)S(1)} %square.1.p0_ref), channel_id=1, source_target_pairs={{0,3},{1,0},{2,1},{3,2},{4,7},{5,4},{6,5},{7,6},{8,11},{9,8},{10,9... | collective-permute-start | bytes 1544 | tf_op jit(solution)/shard_map/ppermute | solution.py:431
  14.8 0.3 collective-permute-start.1
  15.1 0.7 %collective-permute-start = (f32[2,64]{1,0:T(2,128)S(1)}, f32[2,64]{1,0:T(2,128)S(1)}, u32[]{:S(2)}, u32[]{:S(2)}) collective-permute-start(f32[2,64]{1,0:T(2,128)S(1)} %square.1.p0_ref), channel_id=1, source_target_pairs={{0,1},{1,2},{2,3},{3,0},{4,5},{5,6},{6,7},{7,4},{8,9},{9,10},{10,1... | collective-permute-start | bytes 1544 | tf_op jit(solution)/shard_map/ppermute | solution.py:431
  15.8 0.0 copy-done.10
  15.8 0.0 copy-done.5
  15.8 0.0 copy-done.11
  15.8 0.0 copy-done.12
  15.8 0.0 copy-start.13
  15.9 1.6 %pre.1 = (f32[64,2048]{1,0:T(8,128)S(1)}, f32[64,2048]{1,0:T(8,128)S(1)}, f32[2,32,64]{2,1,0:T(8,128)S(1)}, f32[2,32,64]{2,1,0:T(8,128)S(1)}, f32[2,32,128]{2,1,0:T(8,128)S(1)}) custom-call(s32[2]{0:T(128)S(1)} %copy-done.5, f32[2,32,64]{2,1,0:T(8,128)S(1)} %bitcast.23, f32[1,32]{1,0:T(1,128)S(1)} %copy-done.11, f32[1,32]{1,0:T(1,128)S(1)} %copy-done.12), custom_call_target="tpu_custom_call" | custom-call | flops 200000000 | bytes 5000000 | tf_op jit(solution)/shard_map/pre/pallas_call | solution.py:441
  17.5 0.0 copy-start.14
  17.5 0.6 %copy-done.14 = f32[1,32]{1,0:T(1,128)S(1)} copy-done((f32[1,32]{1,0:T(1,128)S(1)}, f32[1,32]{1,0:T(1,128)}, u32[]{:S(2)}) %copy-start.14) | copy-done | bytes 152
  18.2 0.1 broadcast_in_dim.18
  18.2 0.1 broadcast_in_dim.19.skip_ref
  18.3 0.0 copy-done.13
  18.3 0.0 copy-start.1
  18.3 0.0 copy-start.2
  18.3 0.0 copy-start.3
  18.3 0.0 copy-start.4
  18.4 0.1 reshape_squeeze.7.bc_ref
  18.5 0.0 collective-permute-done.2.p3_ref.r3_ref
  18.5 0.5 %collective-permute-done.1.p2_ref.r2_ref = f32[2,64]{1,0:T(2,128)S(1)} collective-permute-done((f32[2,64]{1,0:T(2,128)S(1)}, f32[2,64]{1,0:T(2,128)S(1)}, u32[]{:S(2)}, u32[]{:S(2)}) %collective-permute-start.1) | collective-permute-done | bytes 544 | tf_op jit(solution)/shard_map/ppermute | solution.py:431
  19.0 0.1 collective-permute-done.p1_ref.r1_ref
  19.1 4.8 %collective-permute-done.4.message_ref.message0_in_ref = bf16[2112,128]{1,0:T(8,128)(2,1)S(1)} collective-permute-done((bf16[2112,128]{1,0:T(8,128)(2,1)}, bf16[2112,128]{1,0:T(8,128)(2,1)S(1)}, u32[]{:S(2)}, u32[]{:S(2)}) %collective-permute-start.4) | collective-permute-done | bytes 540704 | tf_op jit(solution)/shard_map/ppermute | solution.py:431
  23.9 2.2 %mid0.1 = (bf16[64,2048]{1,0:T(8,128)(2,1)S(1)}, f32[1,64]{1,0:T(1,128)S(1)}, bf16[1,3,2,256]{3,2,1,0:T(2,128)(2,1)S(1)}, bf16[64,2048]{1,0:T(8,128)(2,1)S(1)}, ...) custom-call(s32[2]{0:T(128)S(1)} %copy-done.5, ...), custom_call_target="tpu_custom_call" | custom-call | flops 100000000 | bytes 3000000 | tf_op jit(solution)/shard_map/mid0/pallas_call | solution.py:461
  26.1 0.0 collective-permute-done.3.message_ref.message1_in_ref
  26.1 0.0 copy-start.7
  26.1 0.7 %copy-done.7 = f32[2,64]{1,0:T(2,128)S(1)} copy-done((f32[2,64]{1,0:T(2,128)S(1)}, f32[2,64]{1,0:T(2,128)}, u32[]{:S(2)}) %copy-start.7) | copy-done | bytes 536
  26.8 2.8 %mid1.1 = (bf16[2,64,2048]{2,1,0:T(8,128)(2,1)S(1)}, f32[2,64]{1,0:T(2,128)}, bf16[2,3,2,256]{3,2,1,0:T(2,128)(2,1)}, bf16[64,2048]{1,0:T(8,128)(2,1)S(1)}, bf16...) custom-call(s32[2]{0:T(128)S(1)} %copy-done.5, ...), custom_call_target="tpu_custom_call" | custom-call | flops 100000000 | bytes 3000000 | tf_op jit(solution)/shard_map/mid1/pallas_call | solution.py:461
  29.6 0.8 %copy-done.9 = bf16[2,64,2048]{2,1,0:T(8,128)(2,1)} copy-done((bf16[2,64,2048]{2,1,0:T(8,128)(2,1)}, bf16[2,64,2048]{2,1,0:T(8,128)(2,1)S(1)}, u32[]{:S(2)}) %copy-start.9) | copy-done | bytes 524312
  30.4 1.3 %collective-permute-start.7 = (f32[2,64]{1,0:T(2,128)}, f32[2,64]{1,0:T(2,128)S(1)}, u32[]{:S(2)}, u32[]{:S(2)}) collective-permute-start(f32[2,64]{1,0:T(2,128)} %get-tuple-element.34), channel_id=1, source_target_pairs={{0,131},{1,128},{2,129},{3,130},{4,135},{5,132},{6,133},{7,134},{8... | collective-permute-start | bytes 1544 | tf_op jit(solution)/shard_map/ppermute | solution.py:502
  31.7 1.3 %collective-permute-start.6 = (f32[2,64]{1,0:T(2,128)}, f32[2,64]{1,0:T(2,128)S(1)}, u32[]{:S(2)}, u32[]{:S(2)}) collective-permute-start(f32[2,64]{1,0:T(2,128)} %get-tuple-element.34), channel_id=1, source_target_pairs={{0,130},{1,131},{2,128},{3,129},{4,134},{5,135},{6,132},{7,133},{8... | collective-permute-start | bytes 1544 | tf_op jit(solution)/shard_map/ppermute | solution.py:502
  33.0 1.3 %collective-permute-start.5 = (f32[2,64]{1,0:T(2,128)}, f32[2,64]{1,0:T(2,128)S(1)}, u32[]{:S(2)}, u32[]{:S(2)}) collective-permute-start(f32[2,64]{1,0:T(2,128)} %get-tuple-element.34), channel_id=1, source_target_pairs={{0,129},{1,130},{2,131},{3,128},{4,133},{5,134},{6,135},{7,132},{8... | collective-permute-start | bytes 1544 | tf_op jit(solution)/shard_map/ppermute | solution.py:502
  34.3 0.0 copy-start.8
  34.3 4.0 %collective-permute-start.8 = (bf16[2,64,2048]{2,1,0:T(8,128)(2,1)}, bf16[2,64,2048]{2,1,0:T(8,128)(2,1)S(1)}, u32[]{:S(2)}, u32[]{:S(2)}) collective-permute-start(bf16[2,64,2048]{2,1,0:T(8,128)(2,1)} %copy-done.9), channel_id=1, source_target_pairs={{0,128},{128,0},{1,129},{129,1},{2,130},{130,2},{3,131},{131,3},{4... | collective-permute-start | bytes 1572872 | tf_op jit(solution)/shard_map/ppermute | solution.py:500
  38.3 0.0 collective-permute-done.7.q3_ref
  38.3 0.1 collective-permute-done.6.q2_ref
  38.4 1.9 %collective-permute-done.5.q1_ref = f32[2,64]{1,0:T(2,128)S(1)} collective-permute-done((f32[2,64]{1,0:T(2,128)}, f32[2,64]{1,0:T(2,128)S(1)}, u32[]{:S(2)}, u32[]{:S(2)}) %collective-permute-start.5) | collective-permute-done | bytes 544 | tf_op jit(solution)/shard_map/ppermute | solution.py:502
  40.3 0.0 copy-done.8
  40.3 0.0 collective-permute-done.8.moved_ref
  40.3 5.3 %last.1 = (bf16[2,64,2048]{2,1,0:T(8,128)(2,1)}, bf16[2,2048,128]{2,1,0:T(8,128)(2,1)}, bf16[3,2,2048]{2,1,0:T(2,128)(2,1)}) custom-call(s32[1]{0:T(128)} %bitcast.sec_ref, s32[2]{0:T(128)S(1)} %copy-done.5, f32[2,64]{1,0:T(2,128)S(1)} %others.1.others_ref, f32[1,2048]{1,0:T(1,128)S(1)} %copy-done.2, f32[4,2048]{1,0:T(4,128)S(1)} %bitcast.20, ...), custom_call_target="tpu_custom_call" | custom-call | flops 200000000 | bytes 5000000 | tf_op jit(solution)/shard_map/last/pallas_call | solution.py:518
  (10 shorter events, 0.0 us)
Async XLA Ops:
  0.6 11.1 %copy-start = (bf16[2,64,2048]{2,1,0:T(8,128)(2,1)S(1)}, bf16[2,64,2048]{2,1,0:T(8,128)(2,1)}, u32[]{:S(2)}) copy-start(bf16[2,64,2048]{2,1,0:T(8,128)(2,1)} %stream_ref.7) | copy-start | bytes 1572868
  3.0 20.9 %collective-permute-start.4 = (bf16[2112,128]{1,0:T(8,128)(2,1)}, bf16[2112,128]{1,0:T(8,128)(2,1)S(1)}, u32[]{:S(2)}, u32[]{:S(2)}) collective-permute-start(bf16[2112,128]{1,0:T(8,128)(2,1)} %get-tuple-element.29), channel_id=1, source_target_pairs={{0,4},{4,8},{8,12},{12,16},{16,20},{20,24},{24,28},{28,32},{32,36}... | collective-permute-start | bytes 1622024 | tf_op jit(solution)/shard_map/ppermute | solution.py:431
  5.1 10.7 %copy-start.10 = (f32[1,2,64,32]{2,3,1,0:T(8,128)S(1)}, f32[1,2,64,32]{2,3,1,0:T(8,128)}, u32[]{:S(2)}) copy-start(f32[1,2,64,32]{2,3,1,0:T(8,128)} %param.20) | copy-start | bytes 49156
  5.1 21.0 %collective-permute-start.3 = (bf16[2112,128]{1,0:T(8,128)(2,1)}, bf16[2112,128]{1,0:T(8,128)(2,1)S(1)}, u32[]{:S(2)}, u32[]{:S(2)}) collective-permute-start(bf16[2112,128]{1,0:T(8,128)(2,1)} %get-tuple-element.26), channel_id=1, source_target_pairs={{0,124},{4,0},{8,4},{12,8},{16,12},{20,16},{24,20},{28,24},{32,28}... | collective-permute-start | bytes 1622024 | tf_op jit(solution)/shard_map/ppermute | solution.py:431
  11.9 3.9 %copy-start.5 = (s32[2]{0:T(128)S(1)}, s32[2]{0:T(128)}, u32[]{:S(2)}) copy-start(s32[2]{0:T(128)} %len_ref.7) | copy-start | bytes 28
  12.0 3.9 %copy-start.11 = (f32[1,32]{1,0:T(1,128)S(1)}, f32[1,32]{1,0:T(1,128)}, u32[]{:S(2)}) copy-start(f32[1,32]{1,0:T(1,128)} %log_ref.1) | copy-start | bytes 388
  12.0 3.9 %copy-start.12 = (f32[1,32]{1,0:T(1,128)S(1)}, f32[1,32]{1,0:T(1,128)}, u32[]{:S(2)}) copy-start(f32[1,32]{1,0:T(1,128)} %bias_ref.1) | copy-start | bytes 388
  12.0 6.5 %collective-permute-start.2 = (f32[2,64]{1,0:T(2,128)S(1)}, f32[2,64]{1,0:T(2,128)S(1)}, u32[]{:S(2)}, u32[]{:S(2)}) collective-permute-start(f32[2,64]{1,0:T(2,128)S(1)} %square.1.p0_ref), channel_id=1, source_target_pairs={{0,3},{1,0},{2,1},{3,2},{4,7},{5,4},{6,5},{7,6},{8,11},{9,8},{10,9... | collective-permute-start | bytes 1544 | tf_op jit(solution)/shard_map/ppermute | solution.py:431
  14.8 4.2 %collective-permute-start.1 = (f32[2,64]{1,0:T(2,128)S(1)}, f32[2,64]{1,0:T(2,128)S(1)}, u32[]{:S(2)}, u32[]{:S(2)}) collective-permute-start(f32[2,64]{1,0:T(2,128)S(1)} %square.1.p0_ref), channel_id=1, source_target_pairs={{0,2},{1,3},{2,0},{3,1},{4,6},{5,7},{6,4},{7,5},{8,10},{9,11},{10,... | collective-permute-start | bytes 1544 | tf_op jit(solution)/shard_map/ppermute | solution.py:431
  15.1 3.9 %collective-permute-start = (f32[2,64]{1,0:T(2,128)S(1)}, f32[2,64]{1,0:T(2,128)S(1)}, u32[]{:S(2)}, u32[]{:S(2)}) collective-permute-start(f32[2,64]{1,0:T(2,128)S(1)} %square.1.p0_ref), channel_id=1, source_target_pairs={{0,1},{1,2},{2,3},{3,0},{4,5},{5,6},{6,7},{7,4},{8,9},{9,10},{10,1... | collective-permute-start | bytes 1544 | tf_op jit(solution)/shard_map/ppermute | solution.py:431
  15.8 2.5 %copy-start.13 = (bf16[1,2,64,2,256]{4,3,2,1,0:T(2,128)(2,1)S(1)}, bf16[1,2,64,2,256]{4,3,2,1,0:T(2,128)(2,1)}, u32[]{:S(2)}) copy-start(bf16[1,2,64,2,256]{4,3,2,1,0:T(2,128)(2,1)} %param.19) | copy-start | bytes 393220
  17.5 0.7 %copy-start.14 = (f32[1,32]{1,0:T(1,128)S(1)}, f32[1,32]{1,0:T(1,128)}, u32[]{:S(2)}) copy-start(f32[1,32]{1,0:T(1,128)} %param.28) | copy-start | bytes 388
  18.3 5.6 %copy-start.1 = (f32[1,4,2048]{2,1,0:T(4,128)S(1)}, f32[1,4,2048]{2,1,0:T(4,128)}, u32[]{:S(2)}) copy-start(f32[1,4,2048]{2,1,0:T(4,128)} %param.24) | copy-start | bytes 98308
  18.3 5.5 %copy-start.2 = (f32[1,2048]{1,0:T(1,128)S(1)}, f32[1,2048]{1,0:T(1,128)}, u32[]{:S(2)}) copy-start(f32[1,2048]{1,0:T(1,128)} %gain_in_ref.5) | copy-start | bytes 24580
  18.3 5.5 %copy-start.3 = (f32[1,2048]{1,0:T(1,128)S(1)}, f32[1,2048]{1,0:T(1,128)}, u32[]{:S(2)}) copy-start(f32[1,2048]{1,0:T(1,128)} %gain_ref.5) | copy-start | bytes 24580
  18.3 5.5 %copy-start.4 = (f32[1,4,2,256]{3,2,1,0:T(2,128)S(1)}, f32[1,4,2,256]{3,2,1,0:T(2,128)}, u32[]{:S(2)}) copy-start(f32[1,4,2,256]{3,2,1,0:T(2,128)} %param.25) | copy-start | bytes 24580
  19.1 4.8 %copy-start.6 = (f32[2,64]{1,0:T(2,128)}, f32[2,64]{1,0:T(2,128)S(1)}, u32[]{:S(2)}) copy-start(f32[2,64]{1,0:T(2,128)S(1)} %collective-permute-done.p1_ref.r1_ref) | copy-start | bytes 1540
  26.1 0.7 %copy-start.7 = (f32[2,64]{1,0:T(2,128)S(1)}, f32[2,64]{1,0:T(2,128)}, u32[]{:S(2)}) copy-start(f32[2,64]{1,0:T(2,128)} %copy-done.6) | copy-start | bytes 1540
  29.6 0.8 %copy-start.9 = (bf16[2,64,2048]{2,1,0:T(8,128)(2,1)}, bf16[2,64,2048]{2,1,0:T(8,128)(2,1)S(1)}, u32[]{:S(2)}) copy-start(bf16[2,64,2048]{2,1,0:T(8,128)(2,1)S(1)} %get-tuple-element.38) | copy-start | bytes 1572868
  30.4 7.9 %collective-permute-start.7 = (f32[2,64]{1,0:T(2,128)}, f32[2,64]{1,0:T(2,128)S(1)}, u32[]{:S(2)}, u32[]{:S(2)}) collective-permute-start(f32[2,64]{1,0:T(2,128)} %get-tuple-element.34), channel_id=1, source_target_pairs={{0,131},{1,128},{2,129},{3,130},{4,135},{5,132},{6,133},{7,134},{8... | collective-permute-start | bytes 1544 | tf_op jit(solution)/shard_map/ppermute | solution.py:502
  31.7 6.8 %collective-permute-start.6 = (f32[2,64]{1,0:T(2,128)}, f32[2,64]{1,0:T(2,128)S(1)}, u32[]{:S(2)}, u32[]{:S(2)}) collective-permute-start(f32[2,64]{1,0:T(2,128)} %get-tuple-element.34), channel_id=1, source_target_pairs={{0,130},{1,131},{2,128},{3,129},{4,134},{5,135},{6,132},{7,133},{8... | collective-permute-start | bytes 1544 | tf_op jit(solution)/shard_map/ppermute | solution.py:502
  33.0 7.3 %collective-permute-start.5 = (f32[2,64]{1,0:T(2,128)}, f32[2,64]{1,0:T(2,128)S(1)}, u32[]{:S(2)}, u32[]{:S(2)}) collective-permute-start(f32[2,64]{1,0:T(2,128)} %get-tuple-element.34), channel_id=1, source_target_pairs={{0,129},{1,130},{2,131},{3,128},{4,133},{5,134},{6,135},{7,132},{8... | collective-permute-start | bytes 1544 | tf_op jit(solution)/shard_map/ppermute | solution.py:502
  34.3 6.0 %copy-start.8 = (f32[2,64]{1,0:T(2,128)S(1)}, f32[2,64]{1,0:T(2,128)}, u32[]{:S(2)}) copy-start(f32[2,64]{1,0:T(2,128)} %copy-done.6) | copy-start | bytes 1540
  34.3 6.0 %collective-permute-start.8 = (bf16[2,64,2048]{2,1,0:T(8,128)(2,1)}, bf16[2,64,2048]{2,1,0:T(8,128)(2,1)S(1)}, u32[]{:S(2)}, u32[]{:S(2)}) collective-permute-start(bf16[2,64,2048]{2,1,0:T(8,128)(2,1)} %copy-done.9), channel_id=1, source_target_pairs={{0,128},{128,0},{1,129},{129,1},{2,130},{130,2},{3,131},{131,3},{4... | collective-permute-start | bytes 1572872 | tf_op jit(solution)/shard_map/ppermute | solution.py:500

commit v2 on v1

--- a/solution.py
+++ b/solution.py
@@ -14,6 +14,7 @@
 CD = 2048
 HD = 32
 N = 128
+W = 256
 GC = 1024
 F32 = jnp.float32
 BF16 = jnp.bfloat16
@@ -124,17 +125,51 @@
         part_ref[c : c + 1, :] = as_row(jnp.sum(s * s, axis=1, keepdims=True))
 
 
-def fresh_x(s, total, rows, gain, taps, valid, px_ref):
-    scale = lax.rsqrt(total / CH + EPS)
+def lay_rows(rows, past_ref):
     for k in range(3):
         for j in range(CD // N):
             at = 16 * k + j
-            px_ref[5 + k : 6 + k, N * j : N * (j + 1)] = rows[at : at + 1, :]
-    px_ref[8:72, :] = (s * scale * gain).astype(BF16).astype(F32)
-    acc = taps[0:1] * px_ref[5:69, :]
+            past_ref[5 + k : 6 + k, N * j : N * (j + 1)] = rows[at : at + 1, :]
+
+
+def delayed(value, past, steps):
+    rolled = pltpu.roll(value, steps, 0)
+    head = jnp.where(iota(past.shape, 0) < steps, pltpu.roll(past, steps, 0), rolled[:8])
+    return jnp.concatenate([head, rolled[8:]], axis=0)
+
+
+def scaled_x(s, at, scale, gain_ref):
+    return (s * scale * gain_ref[:, at]).astype(BF16).astype(F32)
+
+
+def fresh_x(x_in, at, taps_ref, valid, past_ref):
+    acc = taps_ref[3:4, at] * x_in
     for k in range(1, 4):
-        acc = acc + taps[k : k + 1] * px_ref[5 + k : 69 + k, :]
+        acc = acc + taps_ref[3 - k : 4 - k, at] * delayed(x_in, past_ref[:8, at], k)
     return silu(acc) * valid
+
+
+def head_masks():
+    lane = iota((T, W), 1) // 64
+    return [jnp.where(lane == j, 1.0, 0.0).astype(BF16) for j in range(4)]
+
+
+def intra(mix, x, masks):
+    xb = x.astype(BF16)
+    return dot(mix, jnp.concatenate([xb * mask for mask in masks], axis=0), ((1,), (0,)))
+
+
+def head_offsets():
+    return iota((3 * HD, W), 0) % HD - iota((3 * HD, W), 1) // 64
+
+
+def spread(parts, offsets, q):
+    onehot = jnp.where(offsets == 4 * q, 1.0, 0.0).astype(BF16)
+    return dot(parts, onehot, ((1,), (0,)))
+
+
+def halves(v):
+    return v[:, :N] + v[:, N:]
 
 
 def fresh_bc(rows, bc, taps_ref, pbc_ref):
@@ -148,47 +183,6 @@
         taps = jnp.concatenate([taps_ref[k, 0:1, :], taps_ref[k, 1:2, :]], axis=1)
         acc = acc + taps * pbc_ref[5 + k : 69 + k, :]
     return silu(acc)
-
-
-def mixing(bc, decay_ref, mix_ref):
-    for g in range(2):
-        bg = bc[:, N * g : N * (g + 1)]
-        cg = bc[:, 256 + N * g : 256 + N * (g + 1)]
-        inner = dot(cg, jnp.concatenate([bg, bg], axis=0), ((1,), (1,)), HIGHEST)
-        for j in range(8 * g, 8 * g + 8):
-            at = slice(N * j, N * (j + 1))
-            mix_ref[:, at] = (decay_ref[:, at] * inner).astype(BF16)
-
-
-def readout(bc, state, grow):
-    cb = bc[:, 256:].astype(BF16)
-    read = [
-        dot(cb[:, N * g : N * (g + 1)], state[GC * g : GC * (g + 1), :], ((1,), (1,)))
-        for g in range(2)
-    ]
-    return jnp.concatenate(read, axis=1) * grow
-
-
-def intra(mix_ref, x):
-    xb = x.astype(BF16)
-    outs = []
-    lane = iota((T, 256), 1) // 64
-    masks = [jnp.where(lane == j, 1.0, 0.0).astype(BF16) for j in range(4)]
-    for q in range(CD // 256):
-        xq = xb[:, 256 * q : 256 * (q + 1)]
-        rhs = jnp.concatenate([xq * mask for mask in masks], axis=0)
-        outs.append(dot(mix_ref[:, 256 * q : 256 * (q + 1)], rhs, ((1,), (0,))))
-    return jnp.concatenate(outs, axis=1)
-
-
-def finish(y, s, gain, valid):
-    outs = []
-    for g in range(CD // GC):
-        part = y[:, GC * g : GC * (g + 1)]
-        mean = jnp.sum(part * part, axis=1, keepdims=True) * (1.0 / GC)
-        outs.append(part * lax.rsqrt(mean + EPS))
-    z = jnp.concatenate(outs, axis=1) * gain
-    return (s + z * valid).astype(BF16)
 
 
 def valid_col(length):
@@ -216,8 +210,9 @@
         cum = dot(-dt * rate, upper, ((1,), (0,)), HIGHEST)
         final = cum[:, T - 1 : T]
         last_ref[c] = jnp.broadcast_to(jnp.exp(final), (HD, N))
-        grow_ref[c] = jnp.exp(cum)
-        weight_ref[c] = jnp.exp(final - cum) * dt
+        for ref, value in ((grow_ref, jnp.exp(cum)), (weight_ref, jnp.exp(final - cum) * dt)):
+            parts = jnp.concatenate([part.astype(F32) for part in three_parts(value)], axis=0)
+            ref[c] = parts.T.astype(BF16)
         edt = spread_heads(dt)
         ecum = spread_heads(cum)
         row_dt = jnp.sum(jnp.where(diag, edt, 0.0), axis=0, keepdims=True)
@@ -228,15 +223,13 @@
 
 def mid_kernel(
     c,
+    sec_ref,
     len_ref,
     message_ref,
     bc_ref,
     taps_bc_ref,
     stream_ref,
-    p0_ref,
-    p1_ref,
-    p2_ref,
-    p3_ref,
+    totals_ref,
     gain_in_ref,
     taps_ref,
     skip_ref,
@@ -246,60 +239,84 @@
     *refs,
 ):
     if c == 1:
-        early_ref, early_part_ref, early_bc_ref = refs[:3]
-        refs = refs[3:]
-    out_ref, part_ref, bc_out_ref, mix_ref, read_ref, b_ref = refs[:6]
-    pbc_ref, px_ref = refs[6:]
-    length = len_ref[c]
+        early_ref, early_part_ref = refs[:2]
+        refs = refs[2:]
+    out_ref, part_ref, mix_ref, read_ref, b_ref, pbc_ref, past_ref, y_ref = refs
     rows = message_ref[CD:, :].astype(F32)
     bc = fresh_bc(rows, bc_ref[c], taps_bc_ref, pbc_ref)
-    if c == 1:
-        bc_out_ref[0] = early_bc_ref[0]
-    for k in range(3):
-        row = pbc_ref[pl.ds(5 + length + k, 1), :]
-        bc_out_ref[c, k] = jnp.concatenate([row[:, :256], row[:, 256:]], axis=0).astype(BF16)
-    b_ref[...] = bc[:, :256].astype(BF16)
-    read = readout(bc, message_ref[:CD, :], spread_heads(grow_ref[c]))
-    read_ref[...] = read.astype(BF16)
-    mixing(bc, decay_ref, mix_ref)
-    s = stream_ref[c].astype(F32)
-    valid = valid_col(length)
-    total = p0_ref[c : c + 1] + p1_ref[c : c + 1] + p2_ref[c : c + 1] + p3_ref[c : c + 1]
-    x = fresh_x(s, as_col(total), rows, gain_in_ref[...], taps_ref[...], valid, px_ref)
-    y = intra(mix_ref, x) + skip_ref[...] * x + read
-    out = finish(y, s, gain_ref[...], valid)
-    s = out.astype(F32)
-    part = as_row(jnp.sum(s * s, axis=1, keepdims=True))
+    b_ref[...] = bc[:, :W].astype(BF16)
+    inner = []
+    for g in range(2):
+        bg = bc[:, N * g : N * (g + 1)]
+        cg = bc[:, W + N * g : W + N * (g + 1)]
+        inner.append(dot(cg, jnp.concatenate([bg] * 4, axis=0), ((1,), (1,)), HIGHEST))
+    cb = bc[:, W:].astype(BF16)
+    valid = valid_col(len_ref[c])
+    scale = lax.rsqrt(as_col(totals_ref[c : c + 1]) / CH + EPS)
+    lay_rows(rows, past_ref)
+    masks = head_masks()
+    offsets = head_offsets()
+    sums = [0.0, 0.0]
+    for q in range(CD // W):
+        at = slice(W * q, W * (q + 1))
+        g = q // 4
+        s = stream_ref[c, :, at].astype(F32)
+        x = fresh_x(scaled_x(s, at, scale, gain_in_ref), at, taps_ref, valid, past_ref)
+        mix = (decay_ref[:, at] * inner[g]).astype(BF16)
+        mix_ref[:, at] = mix
+        read = dot(cb[:, N * g : N * (g + 1)], message_ref[at, :], ((1,), (1,)))
+        read = read * spread(grow_ref[c], offsets, q)
+        read_ref[:, at] = read.astype(BF16)
+        y = intra(mix, x, masks) + skip_ref[:, at] * x + read
+        y_ref[:, at] = y
+        sums[g] = sums[g] + halves(y * y)
+    norm = [
+        lax.rsqrt(jnp.sum(v, axis=1, keepdims=True) * (1.0 / GC) + EPS) * valid for v in sums
+    ]
+    squares = 0.0
+    first = sec_ref[0] == 0
+    for q in range(CD // W):
+        at = slice(W * q, W * (q + 1))
+        z = y_ref[:, at] * norm[q // 4] * gain_ref[:, at]
+        out = (stream_ref[c, :, at].astype(F32) + jnp.where(first, z, 0.0)).astype(BF16)
+        s = out.astype(F32)
+        squares = squares + halves(s * s)
+        if c == 0:
+            out_ref[:, at] = out
+        else:
+            out_ref[1, :, at] = out
+            out_ref[0, :, at] = early_ref[:, at]
+    part = as_row(jnp.sum(squares, axis=1, keepdims=True))
     if c == 0:
-        out_ref[...] = out
         part_ref[...] = part
     else:
-        out_ref[0] = early_ref[...]
-        out_ref[1] = out
         part_ref[0:1, :] = early_part_ref[...]
         part_ref[1:2, :] = part
 
 
-def others_kernel(sec_ref, r1_ref, r2_ref, r3_ref, q1_ref, q2_ref, q3_ref, others_ref):
+def totals_kernel(p_ref, r1_ref, r2_ref, r3_ref, totals_ref, rest_ref):
+    rest = r1_ref[...] + r2_ref[...] + r3_ref[...]
+    rest_ref[...] = rest
+    totals_ref[...] = p_ref[...] + rest
+
+
+def others_kernel(sec_ref, rest_ref, q1_ref, q2_ref, q3_ref, others_ref):
     others_ref[...] = jnp.where(
-        sec_ref[0] == 0,
-        r1_ref[...] + r2_ref[...] + r3_ref[...],
-        q1_ref[...] + q2_ref[...] + q3_ref[...],
+        sec_ref[0] == 0, rest_ref[...], q1_ref[...] + q2_ref[...] + q3_ref[...]
     )
 
 
 def last_kernel(
-    sec_ref,
     len_ref,
     others_ref,
     gain_in_ref,
     taps_ref,
     skip_ref,
     gain_ref,
+    bc_ref,
     b0_ref,
     b1_ref,
     last_ref,
-    stream_ref,
     moved_ref,
     weight_ref,
     mix0_ref,
@@ -308,56 +325,96 @@
     read1_ref,
     message0_in_ref,
     message1_in_ref,
-    out_in_ref,
-    new_in_ref,
-    x_out_ref,
+    out_to_ref,
+    new_to_ref,
+    x_to_ref,
+    bc_to_ref,
     px_ref,
+    y_ref,
+    xw_ref,
+    pbc_ref,
     message_ref,
     out_ref,
     new_ref,
+    x_out_ref,
+    bc_out_ref,
     sems,
+    new_sems,
 ):
-    first = sec_ref[0] == 0
-
-    gets = []
+    gets = [
+        pltpu.make_async_copy(
+            (message0_in_ref, message1_in_ref)[c], message_ref.at[c], sems.at[c]
+        )
+        for c in range(KIDS)
+    ]
+    for copy in gets:
+        copy.start()
     puts = []
-    for c in range(KIDS):
-        gets.append(
-            pltpu.make_async_copy(
-                (message0_in_ref, message1_in_ref)[c], message_ref.at[c], sems.at[0, c]
-            )
-        )
-        gets[c].start()
-        puts.append(pltpu.make_async_copy(out_ref.at[c], out_in_ref.at[c], sems.at[1, c]))
-        puts.append(pltpu.make_async_copy(new_ref.at[c], new_in_ref.at[c], sems.at[2, c]))
+
+    def send(source, target, sem):
+        puts.append(pltpu.make_async_copy(source, target, sem))
+        puts[-1].start()
+
+    masks = head_masks()
+    offsets = head_offsets()
+    chunks = [slice(W * q, W * (q + 1)) for q in range(CD // W)]
     tails = []
     for c in range(KIDS):
         length = len_ref[c]
         valid = valid_col(length)
-        b_ref = (b0_ref, b1_ref)[c]
-        s = jnp.where(first, stream_ref[c].astype(F32), moved_ref[c].astype(F32))
-        total = jnp.sum(s * s, axis=1, keepdims=True) + as_col(others_ref[c : c + 1])
+        squares = 0.0
+        for at in chunks:
+            s = moved_ref[c, :, at].astype(F32)
+            squares = squares + halves(s * s)
+        total = jnp.sum(squares, axis=1, keepdims=True) + as_col(others_ref[c : c + 1])
+        scale = lax.rsqrt(total / CH + EPS)
         gets[c].wait()
         rows = message_ref[c, CD:, :].astype(F32)
-        x = fresh_x(s, total, rows, gain_in_ref[...], taps_ref[...], valid, px_ref)
+        lay_rows(rows, px_ref)
+        for k in range(3):
+            for j in range(4):
+                at = 48 + 4 * k + j
+                pbc_ref[5 + k : 6 + k, N * j : N * (j + 1)] = rows[at : at + 1, :]
+        pbc_ref[8:72, :] = bc_ref[c].astype(F32)
+        for k in range(3):
+            row = pbc_ref[pl.ds(5 + length + k, 1), :]
+            bc_out_ref[c, k] = jnp.concatenate([row[:, :W], row[:, W:]], axis=0).astype(BF16)
+        sums = [0.0, 0.0]
+        for q, at in enumerate(chunks):
+            x_in = scaled_x(moved_ref[c, :, at].astype(F32), at, scale, gain_in_ref)
+            px_ref[8:72, at] = x_in
+            x = fresh_x(x_in, at, taps_ref, valid, px_ref)
+            xw_ref[:, at] = (x * spread(weight_ref[c], offsets, q)).astype(BF16)
+            y = intra((mix0_ref, mix1_ref)[c][:, at], x, masks) + skip_ref[:, at] * x
+            y = y + (read0_ref, read1_ref)[c][:, at].astype(F32)
+            y_ref[:, at] = y
+            sums[q // 4] = sums[q // 4] + halves(y * y)
         tails.append([px_ref[pl.ds(5 + length + k, 1), :] for k in range(3)])
-        y = intra((mix0_ref, mix1_ref)[c], x) + skip_ref[...] * x
-        y = y + (read0_ref, read1_ref)[c][...].astype(F32)
-        out_ref[c] = finish(y, s, gain_ref[...], valid)
-        puts[2 * c].start()
-        xw = (x * spread_heads(weight_ref[c])).astype(BF16)
-        for g in range(2):
-            fresh = dot(xw[:, GC * g : GC * (g + 1)], b_ref[:, N * g : N * (g + 1)], ((0,), (0,)))
-            for h in range(16 * g, 16 * g + 16):
-                at = slice(64 * h, 64 * (h + 1))
-                off = 64 * (h - 16 * g)
-                new_ref[c, at, :] = (
-                    last_ref[c, h : h + 1, :] * message_ref[c, at, :].astype(F32)
-                    + fresh[off : off + 64]
+        if c == KIDS - 1:
+            for k in range(3):
+                x_out_ref[k] = jnp.concatenate([tails[0][k], tails[1][k]], axis=0).astype(BF16)
+            send(x_out_ref, x_to_ref, sems.at[2])
+            send(bc_out_ref, bc_to_ref, sems.at[3])
+        norm = [
+            lax.rsqrt(jnp.sum(v, axis=1, keepdims=True) * (1.0 / GC) + EPS) * valid for v in sums
+        ]
+        for q, at in enumerate(chunks):
+            z = y_ref[:, at] * norm[q // 4] * gain_ref[:, at]
+            out_ref[c, :, at] = (moved_ref[c, :, at].astype(F32) + z).astype(BF16)
+        send(out_ref.at[c], out_to_ref.at[c], sems.at[4 + c])
+        for q, at in enumerate(chunks):
+            g = q // 4
+            fresh = dot(xw_ref[:, at], (b0_ref, b1_ref)[c][:, N * g : N * (g + 1)], ((0,), (0,)))
+            for j in range(4):
+                rows_at = slice(W * q + 64 * j, W * q + 64 * (j + 1))
+                h = 4 * q + j
+                new_ref[c, rows_at, :] = (
+                    last_ref[c, h : h + 1, :] * message_ref[c, rows_at, :].astype(F32)
+                    + fresh[64 * j : 64 * (j + 1)]
                 ).astype(BF16)
-        puts[2 * c + 1].start()
-    for k in range(3):
-        x_out_ref[k] = jnp.concatenate([tails[0][k], tails[1][k]], axis=0).astype(BF16)
+            if q % 4 == 3:
+                half = pl.ds(GC * g, GC)
+                send(new_ref.at[c, half], new_to_ref.at[c, half], new_sems.at[c, g])
     for copy in puts:
         copy.wait()
 
@@ -443,8 +500,8 @@
         out_shape=(
             shape((T, CD), F32),
             shape((T, CD), F32),
-            shape((KIDS, HD, T), F32),
-            shape((KIDS, HD, T), F32),
+            shape((KIDS, T, 3 * HD), BF16),
+            shape((KIDS, T, 3 * HD), BF16),
             shape((KIDS, HD, N), F32),
         ),
         in_specs=[SMEM] + [VMEM] * 3,
@@ -453,6 +510,15 @@
         cost_estimate=cost(200_000_000, 5_000_000, 1_000_000),
         name="pre",
     )(lengths, inc, a_log, dt_bias)
+
+    totals, rest = pl.pallas_call(
+        totals_kernel,
+        out_shape=(shape((KIDS, T), F32), shape((KIDS, T), F32)),
+        in_specs=[VMEM] * 4,
+        out_specs=(VMEM, VMEM),
+        compiler_params=params(4),
+        name="totals",
+    )(part, r1, r2, r3)
 
     early = ()
     kept = []
@@ -463,27 +529,28 @@
             out_shape=(
                 shape(out_dims[0], BF16),
                 shape(out_dims[1], F32),
-                shape((c + 1, 3, 2, 256), BF16),
                 shape((T, CD), BF16),
                 shape((T, CD), BF16),
                 shape((T, 256), BF16),
             ),
-            in_specs=[SMEM] + [VMEM] * (14 + len(early)),
-            out_specs=tuple([VMEM] * 6),
-            scratch_shapes=[pltpu.VMEM((72, 512), F32), pltpu.VMEM((72, CD), F32)],
+            in_specs=[SMEM] * 2 + [VMEM] * (11 + len(early)),
+            out_specs=tuple([VMEM] * 5),
+            scratch_shapes=[
+                pltpu.VMEM((72, 512), F32),
+                pltpu.VMEM((8, CD), F32),
+                pltpu.VMEM((T, CD), F32),
+            ],
             compiler_params=params(12),
             cost_estimate=cost(100_000_000, 3_000_000, 500_000),
             name="mid%d" % c,
         )(
+            section,
             lengths,
             messages[c],
             bc,
             taps_bc,
             streams_in,
-            part,
-            r1,
-            r2,
-            r3,
+            totals,
             input_norm_gain,
             taps,
             skip,
@@ -492,9 +559,9 @@
             grow,
             *early,
         )
-        early = result[:3]
-        kept.append(result[3:])
-    mid, mid_part, bc_out = early
+        early = result[:2]
+        kept.append(result[2:])
+    mid, mid_part = early
     mixes, reads, b_mats = zip(*kept)
 
     moved = lax.ppermute(mid, "section", [(0, 1), (1, 0)])
@@ -508,43 +575,49 @@
     others = pl.pallas_call(
         others_kernel,
         out_shape=shape((KIDS, T), F32),
-        in_specs=[SMEM] + [VMEM] * 6,
+        in_specs=[SMEM] + [VMEM] * 4,
         out_specs=VMEM,
         compiler_params=params(4),
         cost_estimate=cost(10_000_000_000, 100_000_000, 0),
         name="others",
-    )(section, r1, r2, r3, q1, q2, q3)
-
-    out, new, x_out = pl.pallas_call(
+    )(section, rest, q1, q2, q3)
+
+    out, new, x_out, bc_out = pl.pallas_call(
         last_kernel,
         out_shape=(
             shape((KIDS, T, CD), BF16),
             shape((KIDS, CD, N), BF16),
             shape((3, KIDS, CD), BF16),
+            shape((KIDS, 3, 2, W), BF16),
         ),
-        in_specs=[SMEM] * 2 + [VMEM] * 15 + [HBM] * 2,
-        out_specs=(HBM, HBM, VMEM),
+        in_specs=[SMEM] + [VMEM] * 15 + [HBM] * 2,
+        out_specs=(HBM, HBM, HBM, HBM),
         scratch_shapes=[
             pltpu.VMEM((72, CD), F32),
+            pltpu.VMEM((T, CD), F32),
+            pltpu.VMEM((T, CD), BF16),
+            pltpu.VMEM((72, 512), F32),
             pltpu.VMEM((KIDS, CD + 64, N), BF16),
             pltpu.VMEM((KIDS, T, CD), BF16),
             pltpu.VMEM((KIDS, CD, N), BF16),
-            pltpu.SemaphoreType.DMA((3, KIDS)),
+            pltpu.VMEM((3, KIDS, CD), BF16),
+            pltpu.VMEM((KIDS, 3, 2, W), BF16),
+            pltpu.SemaphoreType.DMA((6,)),
+            pltpu.SemaphoreType.DMA((KIDS, 2)),
         ],
         compiler_params=params(14),
         cost_estimate=cost(200_000_000, 5_000_000, 1_000_000),
         name="last",
     )(
-        section,
         lengths,
         others,
         input_norm_gain,
         taps,
         skip,
         out_gain,
+        bc,
         *b_mats,
         last,
-        streams_in,
         moved,
         weight,
         *mixes,

time: 45.7 us -> 41.6 us (0.910)
  Pallas kernels: 14.4 us -> 11.9 us
  waiting for transfers between devices: 7.39 us -> 6.54 us
  local copies, waits for them, and re-layouts: 2.43 us -> 1.61 us
    pallas_call x1, Pallas kernels: 5.25 us -> 3.79 us  [on_device(): pl.pallas_call(last_kernel, out_shape=(shape((KIDS, T, CD), BF16), shape(...]
    pallas_call x2, Pallas kernels: 5 us -> 3.98 us  [on_device(): pl.pallas_call(functools.partial(mid_kernel, c), out_shape=(shape(out_dim...]
    unnamed x30 -> x22, local copies, waits for them, and re-layouts: 2.18 us -> 1.37 us
    ppermute x5, waiting for transfers between devices: 5.4 us -> 4.74 us  [along(): lax.ppermute(value, axis, [(i, (i + steps) % size) for i in range(size)])]
  transfers between devices with their start and end apart: 9 -> 9, of which waited for: 5 -> 2; matrix products, arithmetic and copies ran while one was open for 1% -> 1% of each run, Pallas kernels for 9% -> 9%
where the time goes in v2:
time: 41.6 us; the launch traced here: 41.4 us
  starting transfers between devices  20.5 us (49%)
  Pallas kernels  11.9 us (29%)
  waiting for transfers between devices  6.54 us (16%)
  local copies, waits for them, and re-layouts  1.61 us (4%)
  between operations  0.8 us (2%)
    ppermute x5, starting transfers between devices, along(): lax.ppermute(value, axis, [(i, (i + steps) % size) for i in range(size)])  12.6 us
    ppermute x5, waiting for transfers between devices, along(): lax.ppermute(value, axis, [(i, (i + steps) % size) for i in range(size)])  4.74 us
    ppermute x1, starting transfers between devices, on_device(): moved = lax.ppermute(mid, 'section', [(0, 1), (1, 0)])  4.01 us
    pallas_call x2, Pallas kernels, on_device(): pl.pallas_call(functools.partial(mid_kernel, c), out_shape=(shape(out_dim...  3.98 us
    ppermute x3, starting transfers between devices, on_device(): lax.ppermute(mid_part, ('section', 'tensor'), [(i, tens + (i + k) % tens)...  3.87 us
    pallas_call x1, Pallas kernels, on_device(): pl.pallas_call(last_kernel, out_shape=(shape((KIDS, T, CD), BF16), shape(...  3.79 us
    pallas_call x1, Pallas kernels, on_device(): pl.pallas_call(pick_kernel, out_shape=(message, message), in_specs=[HBM]...  2.31 us
    ppermute x3, waiting for transfers between devices, on_device(): lax.ppermute(mid_part, ('section', 'tensor'), [(i, tens + (i + k) % tens)...  1.8 us
  transfers between devices with their start and end apart: 9, of which 2 were waited for; matrix products, arithmetic and copies ran while one was open for 1% of the time, Pallas kernels for 9%

profile of v2, /device:TPU:1, one launch (start us, length us, event | category | flops | bytes accessed | tf_op | source)
XLA Modules:
  0.0 41.4 jit_solution(2291640073738066636)
XLA Ops:
  0.6 0.0 copy-start
  0.6 2.3 %pick.1 = (bf16[2112,128]{1,0:T(8,128)(2,1)}, bf16[2112,128]{1,0:T(8,128)(2,1)}) custom-call(s32[64]{0:T(128)} %parents_in_ref.1, bf16[3,2,2048]{2,1,0:T(2,128)(2,1)} %bitcast.25, bf16[2,3,2,256]{3,2,1,0:T(2,128)(2,1)} %bitcast.26, bf16[2,2048,128]{2,1,0:T(8,128)(2,1)} %bitcast.24), custom_call_target="tpu_custom_call" | custom-call | tf_op jit(solution)/shard_map/pick/pallas_call | solution.py:455
  3.0 2.1 %collective-permute-start.4 = (bf16[2112,128]{1,0:T(8,128)(2,1)}, bf16[2112,128]{1,0:T(8,128)(2,1)S(1)}, u32[]{:S(2)}, u32[]{:S(2)}) collective-permute-start(bf16[2112,128]{1,0:T(8,128)(2,1)} %get-tuple-element.32), channel_id=1, source_target_pairs={{0,4},{4,8},{8,12},{12,16},{16,20},{20,24},{24,28},{28,32},{32,36}... | collective-permute-start | bytes 1622024 | tf_op jit(solution)/shard_map/ppermute | solution.py:488
  5.1 0.0 copy-start.6
  5.1 6.7 %collective-permute-start.3 = (bf16[2112,128]{1,0:T(8,128)(2,1)}, bf16[2112,128]{1,0:T(8,128)(2,1)S(1)}, u32[]{:S(2)}, u32[]{:S(2)}) collective-permute-start(bf16[2112,128]{1,0:T(8,128)(2,1)} %get-tuple-element.28), channel_id=1, source_target_pairs={{0,124},{4,0},{8,4},{12,8},{16,12},{20,16},{24,20},{28,24},{32,28}... | collective-permute-start | bytes 1622024 | tf_op jit(solution)/shard_map/ppermute | solution.py:488
  11.7 0.0 copy-done
  11.7 0.2 square.1.p_ref
  11.9 2.8 %collective-permute-start.2 = (f32[2,64]{1,0:T(2,128)S(1)}, f32[2,64]{1,0:T(2,128)S(1)}, u32[]{:S(2)}, u32[]{:S(2)}) collective-permute-start(f32[2,64]{1,0:T(2,128)S(1)} %square.1.p_ref), channel_id=1, source_target_pairs={{0,3},{1,0},{2,1},{3,2},{4,7},{5,4},{6,5},{7,6},{8,11},{9,8},{10,9... | collective-permute-start | bytes 1544 | tf_op jit(solution)/shard_map/ppermute | solution.py:488
  14.7 0.3 collective-permute-start.1
  15.1 0.7 %collective-permute-start = (f32[2,64]{1,0:T(2,128)S(1)}, f32[2,64]{1,0:T(2,128)S(1)}, u32[]{:S(2)}, u32[]{:S(2)}) collective-permute-start(f32[2,64]{1,0:T(2,128)S(1)} %square.1.p_ref), channel_id=1, source_target_pairs={{0,1},{1,2},{2,3},{3,0},{4,5},{5,6},{6,7},{7,4},{8,9},{9,10},{10,1... | collective-permute-start | bytes 1544 | tf_op jit(solution)/shard_map/ppermute | solution.py:488
  15.8 0.0 copy-start.5
  15.8 0.0 copy-start.7
  15.8 0.0 copy-start.8
  15.8 0.0 copy-done.6
  15.8 0.6 %copy-done.5 = s32[2]{0:T(128)S(1)} copy-done((s32[2]{0:T(128)S(1)}, s32[2]{0:T(128)}, u32[]{:S(2)}) %copy-start.5) | copy-done | bytes 32
  16.4 0.0 copy-done.7
  16.5 0.0 copy-done.8
  16.5 1.6 %pre.1 = (f32[64,2048]{1,0:T(8,128)S(1)}, f32[64,2048]{1,0:T(8,128)S(1)}, bf16[2,64,96]{2,1,0:T(8,128)(2,1)S(1)}, bf16[2,64,96]{2,1,0:T(8,128)(2,1)S(1)}, f32[2,32,128]{2,1,0:T(8,128)S(1)}) custom-call(s32[2]{0:T(128)S(1)} %copy-done.5, f32[2,32,64]{2,1,0:T(8,128)S(1)} %bitcast.23, f32[1,32]{1,0:T(1,128)S(1)} %copy-done.7, f32[1,32]{1,0:T(1,128)S(1)} %copy-done.8), custom_call_target="tpu_custom_call" | custom-call | flops 200000000 | bytes 5000000 | tf_op jit(solution)/shard_map/pre/pallas_call | solution.py:498
  18.1 0.0 copy-start.10
  18.1 0.6 %copy-done.10 = f32[1,32]{1,0:T(1,128)S(1)} copy-done((f32[1,32]{1,0:T(1,128)S(1)}, f32[1,32]{1,0:T(1,128)}, u32[]{:S(2)}) %copy-start.10) | copy-done | bytes 152
  18.8 0.1 broadcast_in_dim.18
  18.8 0.1 broadcast_in_dim.19.skip_ref
  18.9 0.0 copy-done.9
  18.9 0.0 copy-start.1
  18.9 0.0 copy-start.3
  19.0 0.0 copy-start.4
  19.0 0.1 reshape_squeeze.7.bc_ref
  19.1 0.0 copy-start.2
  19.1 0.0 collective-permute-done.2.r3_ref
  19.1 0.0 collective-permute-done.1.r2_ref
  19.1 0.0 collective-permute-done.r1_ref
  19.1 4.7 %collective-permute-done.4.message_ref.message0_in_ref = bf16[2112,128]{1,0:T(8,128)(2,1)S(1)} collective-permute-done((bf16[2112,128]{1,0:T(8,128)(2,1)}, bf16[2112,128]{1,0:T(8,128)(2,1)S(1)}, u32[]{:S(2)}, u32[]{:S(2)}) %collective-permute-start.4) | collective-permute-done | bytes 540704 | tf_op jit(solution)/shard_map/ppermute | solution.py:488
  23.9 0.0 copy-done.1
  23.9 0.0 copy-done.3
  23.9 0.0 copy-done.4
  23.9 0.0 copy-done.2
  23.9 2.0 %mid0.1 = (bf16[64,2048]{1,0:T(8,128)(2,1)S(1)}, f32[1,64]{1,0:T(1,128)S(1)}, bf16[64,2048]{1,0:T(8,128)(2,1)S(1)}, bf16[64,2048]{1,0:T(8,128)(2,1)S(1)}, bf16[64,256]{1,0:T(8,128)(2,1)S(1)}) custom-call(s32[1]{0:T(128)} %bitcast.sec_ref, s32[2]{0:T(128)S(1)} %copy-done.5, bf16[2112,128]{1,0:T(8,128)(2,1)S(1)} %collective-permute-done.4.message_ref.message0_in_ref, ...), custom_call_target="tpu_custom_call" | custom-call | flops 100000000 | bytes 3000000 | tf_op jit(solution)/shard_map/mid0/pallas_call | solution.py:527
  25.9 0.0 collective-permute-done.3.message_ref.message1_in_ref
  25.9 2.0 %mid1.1 = (bf16[2,64,2048]{2,1,0:T(8,128)(2,1)S(1)}, f32[2,64]{1,0:T(2,128)S(1)}, bf16[64,2048]{1,0:T(8,128)(2,1)S(1)}, bf16[64,2048]{1,0:T(8,128)(2,1)S(1)}, bf16[64,256]{1,0:T(8,128)(2,1)S(1)}) custom-call(s32[1]{0:T(128)} %bitcast.sec_ref, s32[2]{0:T(128)S(1)} %copy-done.5, bf16[2112,128]{1,0:T(8,128)(2,1)S(1)} %collective-permute-done.3.message_ref.message1_in_ref, ...), custom_call_target="tpu_custom_call" | custom-call | flops 100000000 | bytes 3000000 | tf_op jit(solution)/shard_map/mid1/pallas_call | solution.py:527
  27.9 1.3 %collective-permute-start.7 = (f32[2,64]{1,0:T(2,128)S(1)}, f32[2,64]{1,0:T(2,128)S(1)}, u32[]{:S(2)}, u32[]{:S(2)}) collective-permute-start(f32[2,64]{1,0:T(2,128)S(1)} %get-tuple-element.36), channel_id=1, source_target_pairs={{0,131},{1,128},{2,129},{3,130},{4,135},{5,132},{6,133},{7,134},{8... | collective-permute-start | bytes 1544 | tf_op jit(solution)/shard_map/ppermute | solution.py:569
  29.2 1.3 %collective-permute-start.6 = (f32[2,64]{1,0:T(2,128)S(1)}, f32[2,64]{1,0:T(2,128)S(1)}, u32[]{:S(2)}, u32[]{:S(2)}) collective-permute-start(f32[2,64]{1,0:T(2,128)S(1)} %get-tuple-element.36), channel_id=1, source_target_pairs={{0,130},{1,131},{2,128},{3,129},{4,134},{5,135},{6,132},{7,133},{8... | collective-permute-start | bytes 1544 | tf_op jit(solution)/shard_map/ppermute | solution.py:569
  30.5 1.3 %collective-permute-start.5 = (f32[2,64]{1,0:T(2,128)S(1)}, f32[2,64]{1,0:T(2,128)S(1)}, u32[]{:S(2)}, u32[]{:S(2)}) collective-permute-start(f32[2,64]{1,0:T(2,128)S(1)} %get-tuple-element.36), channel_id=1, source_target_pairs={{0,129},{1,130},{2,131},{3,128},{4,133},{5,134},{6,135},{7,132},{8... | collective-permute-start | bytes 1544 | tf_op jit(solution)/shard_map/ppermute | solution.py:569
  31.8 4.0 %collective-permute-start.8 = (bf16[2,64,2048]{2,1,0:T(8,128)(2,1)S(1)}, bf16[2,64,2048]{2,1,0:T(8,128)(2,1)S(1)}, u32[]{:S(2)}, u32[]{:S(2)}) collective-permute-start(bf16[2,64,2048]{2,1,0:T(8,128)(2,1)S(1)} %get-tuple-element.40), channel_id=1, source_target_pairs={{0,128},{128,0},{1,129},{129,1},{2,130},{130,2},{3,131},{131,3},{4... | collective-permute-start | bytes 1572872 | tf_op jit(solution)/shard_map/ppermute | solution.py:567
  35.8 0.0 collective-permute-done.7.q3_ref
  35.8 0.0 collective-permute-done.6.q2_ref
  35.8 1.8 %collective-permute-done.5.q1_ref = f32[2,64]{1,0:T(2,128)S(1)} collective-permute-done((f32[2,64]{1,0:T(2,128)S(1)}, f32[2,64]{1,0:T(2,128)S(1)}, u32[]{:S(2)}, u32[]{:S(2)}) %collective-permute-start.5) | collective-permute-done | bytes 544 | tf_op jit(solution)/shard_map/ppermute | solution.py:569
  37.6 0.0 collective-permute-done.8.moved_ref
  37.6 3.8 %last.1 = (bf16[2,64,2048]{2,1,0:T(8,128)(2,1)}, bf16[2,2048,128]{2,1,0:T(8,128)(2,1)}, bf16[3,2,2048]{2,1,0:T(2,128)(2,1)}, bf16[2,3,2,256]{3,2,1,0:T(2,128)(2,1)}) custom-call(s32[2]{0:T(128)S(1)} %copy-done.5, f32[2,64]{1,0:T(2,128)S(1)} %others.1.others_ref, f32[1,2048]{1,0:T(1,128)S(1)} %copy-done.2, f32[4,2048]{1,0:T(4,128)S(1)} %bitcast.20, ...), custom_call_target="tpu_custom_call" | custom-call | flops 200000000 | bytes 5000000 | tf_op jit(solution)/shard_map/last/pallas_call | solution.py:585
  (3 shorter events, 0.0 us)
Async XLA Ops:
  0.6 11.1 %copy-start = (bf16[2,64,2048]{2,1,0:T(8,128)(2,1)S(1)}, bf16[2,64,2048]{2,1,0:T(8,128)(2,1)}, u32[]{:S(2)}) copy-start(bf16[2,64,2048]{2,1,0:T(8,128)(2,1)} %stream_ref.5) | copy-start | bytes 1572868
  3.0 20.9 %collective-permute-start.4 = (bf16[2112,128]{1,0:T(8,128)(2,1)}, bf16[2112,128]{1,0:T(8,128)(2,1)S(1)}, u32[]{:S(2)}, u32[]{:S(2)}) collective-permute-start(bf16[2112,128]{1,0:T(8,128)(2,1)} %get-tuple-element.32), channel_id=1, source_target_pairs={{0,4},{4,8},{8,12},{12,16},{16,20},{20,24},{24,28},{28,32},{32,36}... | collective-permute-start | bytes 1622024 | tf_op jit(solution)/shard_map/ppermute | solution.py:488
  5.1 10.7 %copy-start.6 = (f32[1,2,64,32]{2,3,1,0:T(8,128)S(1)}, f32[1,2,64,32]{2,3,1,0:T(8,128)}, u32[]{:S(2)}) copy-start(f32[1,2,64,32]{2,3,1,0:T(8,128)} %param.20) | copy-start | bytes 49156
  5.1 20.8 %collective-permute-start.3 = (bf16[2112,128]{1,0:T(8,128)(2,1)}, bf16[2112,128]{1,0:T(8,128)(2,1)S(1)}, u32[]{:S(2)}, u32[]{:S(2)}) collective-permute-start(bf16[2112,128]{1,0:T(8,128)(2,1)} %get-tuple-element.28), channel_id=1, source_target_pairs={{0,124},{4,0},{8,4},{12,8},{16,12},{20,16},{24,20},{28,24},{32,28}... | collective-permute-start | bytes 1622024 | tf_op jit(solution)/shard_map/ppermute | solution.py:488
  11.9 7.1 %collective-permute-start.2 = (f32[2,64]{1,0:T(2,128)S(1)}, f32[2,64]{1,0:T(2,128)S(1)}, u32[]{:S(2)}, u32[]{:S(2)}) collective-permute-start(f32[2,64]{1,0:T(2,128)S(1)} %square.1.p_ref), channel_id=1, source_target_pairs={{0,3},{1,0},{2,1},{3,2},{4,7},{5,4},{6,5},{7,6},{8,11},{9,8},{10,9... | collective-permute-start | bytes 1544 | tf_op jit(solution)/shard_map/ppermute | solution.py:488
  14.7 4.3 %collective-permute-start.1 = (f32[2,64]{1,0:T(2,128)S(1)}, f32[2,64]{1,0:T(2,128)S(1)}, u32[]{:S(2)}, u32[]{:S(2)}) collective-permute-start(f32[2,64]{1,0:T(2,128)S(1)} %square.1.p_ref), channel_id=1, source_target_pairs={{0,2},{1,3},{2,0},{3,1},{4,6},{5,7},{6,4},{7,5},{8,10},{9,11},{10,... | collective-permute-start | bytes 1544 | tf_op jit(solution)/shard_map/ppermute | solution.py:488
  15.1 4.0 %collective-permute-start = (f32[2,64]{1,0:T(2,128)S(1)}, f32[2,64]{1,0:T(2,128)S(1)}, u32[]{:S(2)}, u32[]{:S(2)}) collective-permute-start(f32[2,64]{1,0:T(2,128)S(1)} %square.1.p_ref), channel_id=1, source_target_pairs={{0,1},{1,2},{2,3},{3,0},{4,5},{5,6},{6,7},{7,4},{8,9},{9,10},{10,1... | collective-permute-start | bytes 1544 | tf_op jit(solution)/shard_map/ppermute | solution.py:488
  15.8 0.7 %copy-start.5 = (s32[2]{0:T(128)S(1)}, s32[2]{0:T(128)}, u32[]{:S(2)}) copy-start(s32[2]{0:T(128)} %len_ref.7) | copy-start | bytes 28
  15.8 0.7 %copy-start.7 = (f32[1,32]{1,0:T(1,128)S(1)}, f32[1,32]{1,0:T(1,128)}, u32[]{:S(2)}) copy-start(f32[1,32]{1,0:T(1,128)} %log_ref.1) | copy-start | bytes 388
  15.8 0.7 %copy-start.8 = (f32[1,32]{1,0:T(1,128)S(1)}, f32[1,32]{1,0:T(1,128)}, u32[]{:S(2)}) copy-start(f32[1,32]{1,0:T(1,128)} %bias_ref.1) | copy-start | bytes 388
  16.5 2.5 %copy-start.9 = (bf16[1,2,64,2,256]{4,3,2,1,0:T(2,128)(2,1)S(1)}, bf16[1,2,64,2,256]{4,3,2,1,0:T(2,128)(2,1)}, u32[]{:S(2)}) copy-start(bf16[1,2,64,2,256]{4,3,2,1,0:T(2,128)(2,1)} %param.19) | copy-start | bytes 393220
  18.1 0.7 %copy-start.10 = (f32[1,32]{1,0:T(1,128)S(1)}, f32[1,32]{1,0:T(1,128)}, u32[]{:S(2)}) copy-start(f32[1,32]{1,0:T(1,128)} %param.28) | copy-start | bytes 388
  18.9 4.9 %copy-start.1 = (f32[1,4,2048]{2,1,0:T(4,128)S(1)}, f32[1,4,2048]{2,1,0:T(4,128)}, u32[]{:S(2)}) copy-start(f32[1,4,2048]{2,1,0:T(4,128)} %param.24) | copy-start | bytes 98308
  18.9 4.9 %copy-start.3 = (f32[1,2048]{1,0:T(1,128)S(1)}, f32[1,2048]{1,0:T(1,128)}, u32[]{:S(2)}) copy-start(f32[1,2048]{1,0:T(1,128)} %gain_ref.5) | copy-start | bytes 24580
  19.0 4.9 %copy-start.4 = (f32[1,4,2,256]{3,2,1,0:T(2,128)S(1)}, f32[1,4,2,256]{3,2,1,0:T(2,128)}, u32[]{:S(2)}) copy-start(f32[1,4,2,256]{3,2,1,0:T(2,128)} %param.25) | copy-start | bytes 24580
  19.1 4.8 %copy-start.2 = (f32[1,2048]{1,0:T(1,128)S(1)}, f32[1,2048]{1,0:T(1,128)}, u32[]{:S(2)}) copy-start(f32[1,2048]{1,0:T(1,128)} %gain_in_ref.5) | copy-start | bytes 24580
  27.9 7.9 %collective-permute-start.7 = (f32[2,64]{1,0:T(2,128)S(1)}, f32[2,64]{1,0:T(2,128)S(1)}, u32[]{:S(2)}, u32[]{:S(2)}) collective-permute-start(f32[2,64]{1,0:T(2,128)S(1)} %get-tuple-element.36), channel_id=1, source_target_pairs={{0,131},{1,128},{2,129},{3,130},{4,135},{5,132},{6,133},{7,134},{8... | collective-permute-start | bytes 1544 | tf_op jit(solution)/shard_map/ppermute | solution.py:569
  29.2 6.6 %collective-permute-start.6 = (f32[2,64]{1,0:T(2,128)S(1)}, f32[2,64]{1,0:T(2,128)S(1)}, u32[]{:S(2)}, u32[]{:S(2)}) collective-permute-start(f32[2,64]{1,0:T(2,128)S(1)} %get-tuple-element.36), channel_id=1, source_target_pairs={{0,130},{1,131},{2,128},{3,129},{4,134},{5,135},{6,132},{7,133},{8... | collective-permute-start | bytes 1544 | tf_op jit(solution)/shard_map/ppermute | solution.py:569
  30.5 7.1 %collective-permute-start.5 = (f32[2,64]{1,0:T(2,128)S(1)}, f32[2,64]{1,0:T(2,128)S(1)}, u32[]{:S(2)}, u32[]{:S(2)}) collective-permute-start(f32[2,64]{1,0:T(2,128)S(1)} %get-tuple-element.36), channel_id=1, source_target_pairs={{0,129},{1,130},{2,131},{3,128},{4,133},{5,134},{6,135},{7,132},{8... | collective-permute-start | bytes 1544 | tf_op jit(solution)/shard_map/ppermute | solution.py:569
  31.8 5.8 %collective-permute-start.8 = (bf16[2,64,2048]{2,1,0:T(8,128)(2,1)S(1)}, bf16[2,64,2048]{2,1,0:T(8,128)(2,1)S(1)}, u32[]{:S(2)}, u32[]{:S(2)}) collective-permute-start(bf16[2,64,2048]{2,1,0:T(8,128)(2,1)S(1)} %get-tuple-element.40), channel_id=1, source_target_pairs={{0,128},{128,0},{1,129},{129,1},{2,130},{130,2},{3,131},{131,3},{4... | collective-permute-start | bytes 1572872 | tf_op jit(solution)/shard_map/ppermute | solution.py:567

commit v3 on v2

--- a/solution.py
+++ b/solution.py
@@ -23,6 +23,8 @@
 SMEM = pl.BlockSpec(memory_space=pltpu.SMEM)
 HBM = pl.BlockSpec(memory_space=pl.ANY)
 BIG = 60
+PARTS = 4
+LATE = 1
 
 
 def iota(shape, dim):
@@ -75,13 +77,15 @@
     out_sems,
 ):
     get_parents = pltpu.make_async_copy(parents_in_ref, parents_ref, sems.at[0])
+    parts = [pl.ds(CD // PARTS * j, CD // PARTS) for j in range(PARTS)]
     get_states = [
-        pltpu.make_async_copy(state_in_ref.at[i], state_ref.at[i], sems.at[1 + i])
+        pltpu.make_async_copy(state_in_ref.at[i, at], state_ref.at[i, at], sems.at[3 + KIDS * j + i])
+        for j, at in enumerate(parts)
         for i in range(KIDS)
     ]
-    get_x = pltpu.make_async_copy(conv_x_in_ref, conv_x_ref, sems.at[3])
-    get_bc = pltpu.make_async_copy(conv_bc_in_ref, conv_bc_ref, sems.at[4])
-    for copy in (get_parents, *get_states, get_x, get_bc):
+    get_x = pltpu.make_async_copy(conv_x_in_ref, conv_x_ref, sems.at[1])
+    get_bc = pltpu.make_async_copy(conv_bc_in_ref, conv_bc_ref, sems.at[2])
+    for copy in (get_parents, get_x, get_bc, *get_states):
         copy.start()
     peers = lax.axis_size("beam")
     me = lax.axis_index("beam")
@@ -91,16 +95,9 @@
         lax.rem(parents_ref[KIDS * lax.rem(me + peers - 1, peers) + 1], KIDS),
     )
     outs = (one_ref, two_ref)
-    for copy in get_states:
-        copy.wait()
-    puts = []
-    for i in range(2):
-        puts.append(
-            pltpu.make_async_copy(state_ref.at[picks[i]], outs[i].at[:CD], out_sems.at[0, i])
-        )
-        puts[-1].start()
     get_x.wait()
     get_bc.wait()
+    puts = []
     for i in range(2):
         low = picks[i] == 0
         pieces = []
@@ -113,8 +110,18 @@
             pieces += [both[p : p + 1, N * j : N * (j + 1)] for p in range(2) for j in range(2)]
         pieces.append(jnp.zeros((4, N), F32))
         rows_ref[i] = jnp.concatenate(pieces, axis=0).astype(BF16)
-        puts.append(pltpu.make_async_copy(rows_ref.at[i], outs[i].at[CD:], out_sems.at[1, i]))
+        puts.append(pltpu.make_async_copy(rows_ref.at[i], outs[i].at[CD:], out_sems.at[i, PARTS]))
         puts[-1].start()
+    for j, at in enumerate(parts):
+        for i in range(KIDS):
+            get_states[KIDS * j + i].wait()
+        for i in range(2):
+            puts.append(
+                pltpu.make_async_copy(
+                    state_ref.at[picks[i], at], outs[i].at[at], out_sems.at[i, j]
+                )
+            )
+            puts[-1].start()
     for copy in puts:
         copy.wait()
 
@@ -238,7 +245,7 @@
     grow_ref,
     *refs,
 ):
-    if c == 1:
+    if c == LATE:
         early_ref, early_part_ref = refs[:2]
         refs = refs[2:]
     out_ref, part_ref, mix_ref, read_ref, b_ref, pbc_ref, past_ref, y_ref = refs
@@ -281,29 +288,25 @@
         out = (stream_ref[c, :, at].astype(F32) + jnp.where(first, z, 0.0)).astype(BF16)
         s = out.astype(F32)
         squares = squares + halves(s * s)
-        if c == 0:
+        if c == LATE:
+            out_ref[c, :, at] = out
+            out_ref[1 - c, :, at] = early_ref[:, at]
+        else:
             out_ref[:, at] = out
-        else:
-            out_ref[1, :, at] = out
-            out_ref[0, :, at] = early_ref[:, at]
     part = as_row(jnp.sum(squares, axis=1, keepdims=True))
-    if c == 0:
+    if c == LATE:
+        part_ref[c : c + 1, :] = part
+        part_ref[1 - c : 2 - c, :] = early_part_ref[...]
+    else:
         part_ref[...] = part
-    else:
-        part_ref[0:1, :] = early_part_ref[...]
-        part_ref[1:2, :] = part
-
-
-def totals_kernel(p_ref, r1_ref, r2_ref, r3_ref, totals_ref, rest_ref):
-    rest = r1_ref[...] + r2_ref[...] + r3_ref[...]
-    rest_ref[...] = rest
-    totals_ref[...] = p_ref[...] + rest
-
-
-def others_kernel(sec_ref, rest_ref, q1_ref, q2_ref, q3_ref, others_ref):
-    others_ref[...] = jnp.where(
-        sec_ref[0] == 0, rest_ref[...], q1_ref[...] + q2_ref[...] + q3_ref[...]
-    )
+
+
+def totals_kernel(p_ref, r1_ref, r2_ref, r3_ref, totals_ref):
+    totals_ref[...] = p_ref[...] + r1_ref[...] + r2_ref[...] + r3_ref[...]
+
+
+def others_kernel(q1_ref, q2_ref, q3_ref, others_ref):
+    others_ref[...] = q1_ref[...] + q2_ref[...] + q3_ref[...]
 
 
 def last_kernel(
@@ -323,8 +326,8 @@
     mix1_ref,
     read0_ref,
     read1_ref,
-    message0_in_ref,
-    message1_in_ref,
+    message0_ref,
+    message1_ref,
     out_to_ref,
     new_to_ref,
     x_to_ref,
@@ -333,7 +336,6 @@
     y_ref,
     xw_ref,
     pbc_ref,
-    message_ref,
     out_ref,
     new_ref,
     x_out_ref,
@@ -341,14 +343,6 @@
     sems,
     new_sems,
 ):
-    gets = [
-        pltpu.make_async_copy(
-            (message0_in_ref, message1_in_ref)[c], message_ref.at[c], sems.at[c]
-        )
-        for c in range(KIDS)
-    ]
-    for copy in gets:
-        copy.start()
     puts = []
 
     def send(source, target, sem):
@@ -358,63 +352,66 @@
     masks = head_masks()
     offsets = head_offsets()
     chunks = [slice(W * q, W * (q + 1)) for q in range(CD // W)]
-    tails = []
+    messages = (message0_ref, message1_ref)
+    valids = [valid_col(len_ref[c]) for c in range(KIDS)]
+    scales = []
     for c in range(KIDS):
-        length = len_ref[c]
-        valid = valid_col(length)
         squares = 0.0
         for at in chunks:
             s = moved_ref[c, :, at].astype(F32)
             squares = squares + halves(s * s)
         total = jnp.sum(squares, axis=1, keepdims=True) + as_col(others_ref[c : c + 1])
-        scale = lax.rsqrt(total / CH + EPS)
-        gets[c].wait()
-        rows = message_ref[c, CD:, :].astype(F32)
-        lay_rows(rows, px_ref)
+        scales.append(lax.rsqrt(total / CH + EPS))
+        rows = messages[c][CD:, :].astype(F32)
+        lay_rows(rows, px_ref.at[c])
         for k in range(3):
             for j in range(4):
                 at = 48 + 4 * k + j
-                pbc_ref[5 + k : 6 + k, N * j : N * (j + 1)] = rows[at : at + 1, :]
-        pbc_ref[8:72, :] = bc_ref[c].astype(F32)
-        for k in range(3):
-            row = pbc_ref[pl.ds(5 + length + k, 1), :]
-            bc_out_ref[c, k] = jnp.concatenate([row[:, :W], row[:, W:]], axis=0).astype(BF16)
-        sums = [0.0, 0.0]
-        for q, at in enumerate(chunks):
-            x_in = scaled_x(moved_ref[c, :, at].astype(F32), at, scale, gain_in_ref)
-            px_ref[8:72, at] = x_in
-            x = fresh_x(x_in, at, taps_ref, valid, px_ref)
-            xw_ref[:, at] = (x * spread(weight_ref[c], offsets, q)).astype(BF16)
+                pbc_ref[c, 5 + k : 6 + k, N * j : N * (j + 1)] = rows[at : at + 1, :]
+        pbc_ref[c, 8:72, :] = bc_ref[c].astype(F32)
+    sums = [[0.0, 0.0] for _ in range(KIDS)]
+    for q, at in enumerate(chunks):
+        for c in range(KIDS):
+            x_in = scaled_x(moved_ref[c, :, at].astype(F32), at, scales[c], gain_in_ref)
+            px_ref[c, 8:72, at] = x_in
+            x = fresh_x(x_in, at, taps_ref, valids[c], px_ref.at[c])
+            xw_ref[c, :, at] = (x * spread(weight_ref[c], offsets, q)).astype(BF16)
             y = intra((mix0_ref, mix1_ref)[c][:, at], x, masks) + skip_ref[:, at] * x
             y = y + (read0_ref, read1_ref)[c][:, at].astype(F32)
-            y_ref[:, at] = y
-            sums[q // 4] = sums[q // 4] + halves(y * y)
-        tails.append([px_ref[pl.ds(5 + length + k, 1), :] for k in range(3)])
-        if c == KIDS - 1:
-            for k in range(3):
-                x_out_ref[k] = jnp.concatenate([tails[0][k], tails[1][k]], axis=0).astype(BF16)
-            send(x_out_ref, x_to_ref, sems.at[2])
-            send(bc_out_ref, bc_to_ref, sems.at[3])
+            y_ref[c, :, at] = y
+            sums[c][q // 4] = sums[c][q // 4] + halves(y * y)
+    for c in range(KIDS):
         norm = [
-            lax.rsqrt(jnp.sum(v, axis=1, keepdims=True) * (1.0 / GC) + EPS) * valid for v in sums
+            lax.rsqrt(jnp.sum(v, axis=1, keepdims=True) * (1.0 / GC) + EPS) * valids[c]
+            for v in sums[c]
         ]
         for q, at in enumerate(chunks):
-            z = y_ref[:, at] * norm[q // 4] * gain_ref[:, at]
+            z = y_ref[c, :, at] * norm[q // 4] * gain_ref[:, at]
             out_ref[c, :, at] = (moved_ref[c, :, at].astype(F32) + z).astype(BF16)
+    for c in range(KIDS):
         send(out_ref.at[c], out_to_ref.at[c], sems.at[4 + c])
-        for q, at in enumerate(chunks):
-            g = q // 4
-            fresh = dot(xw_ref[:, at], (b0_ref, b1_ref)[c][:, N * g : N * (g + 1)], ((0,), (0,)))
-            for j in range(4):
-                rows_at = slice(W * q + 64 * j, W * q + 64 * (j + 1))
-                h = 4 * q + j
-                new_ref[c, rows_at, :] = (
-                    last_ref[c, h : h + 1, :] * message_ref[c, rows_at, :].astype(F32)
-                    + fresh[64 * j : 64 * (j + 1)]
-                ).astype(BF16)
-            if q % 4 == 3:
-                half = pl.ds(GC * g, GC)
-                send(new_ref.at[c, half], new_to_ref.at[c, half], new_sems.at[c, g])
+    for k in range(3):
+        tails = [px_ref[c, pl.ds(5 + len_ref[c] + k, 1), :] for c in range(KIDS)]
+        x_out_ref[k] = jnp.concatenate(tails, axis=0).astype(BF16)
+        for c in range(KIDS):
+            row = pbc_ref[c, pl.ds(5 + len_ref[c] + k, 1), :]
+            bc_out_ref[c, k] = jnp.concatenate([row[:, :W], row[:, W:]], axis=0).astype(BF16)
+    send(x_out_ref, x_to_ref, sems.at[2])
+    send(bc_out_ref, bc_to_ref, sems.at[3])
+    for g in range(2):
+        for c in range(KIDS):
+            for q in range(4 * g, 4 * g + 4):
+                b = (b0_ref, b1_ref)[c][:, N * g : N * (g + 1)]
+                fresh = dot(xw_ref[c, :, chunks[q]], b, ((0,), (0,)))
+                for j in range(4):
+                    rows_at = slice(W * q + 64 * j, W * q + 64 * (j + 1))
+                    h = 4 * q + j
+                    new_ref[c, rows_at, :] = (
+                        last_ref[c, h : h + 1, :] * messages[c][rows_at, :].astype(F32)
+                        + fresh[64 * j : 64 * (j + 1)]
+                    ).astype(BF16)
+            half = pl.ds(GC * g, GC)
+            send(new_ref.at[c, half], new_to_ref.at[c, half], new_sems.at[c, g])
     for copy in puts:
         copy.wait()
 
@@ -463,8 +460,8 @@
             pltpu.VMEM((KIDS, 3, 2, 256), BF16),
             pltpu.VMEM((KIDS, CD, N), BF16),
             pltpu.VMEM((2, 64, N), BF16),
-            pltpu.SemaphoreType.DMA((5,)),
-            pltpu.SemaphoreType.DMA((2, 2)),
+            pltpu.SemaphoreType.DMA((3 + KIDS * PARTS,)),
+            pltpu.SemaphoreType.DMA((2, PARTS + 1)),
         ],
         compiler_params=params(BIG),
         name="pick",
@@ -511,19 +508,19 @@
         name="pre",
     )(lengths, inc, a_log, dt_bias)
 
-    totals, rest = pl.pallas_call(
+    totals = pl.pallas_call(
         totals_kernel,
-        out_shape=(shape((KIDS, T), F32), shape((KIDS, T), F32)),
+        out_shape=shape((KIDS, T), F32),
         in_specs=[VMEM] * 4,
-        out_specs=(VMEM, VMEM),
+        out_specs=VMEM,
         compiler_params=params(4),
         name="totals",
     )(part, r1, r2, r3)
 
     early = ()
-    kept = []
-    for c in range(KIDS):
-        out_dims = ((T, CD), (1, T)) if c == 0 else ((KIDS, T, CD), (KIDS, T))
+    kept = {}
+    for c in (1 - LATE, LATE):
+        out_dims = ((KIDS, T, CD), (KIDS, T)) if c == LATE else ((T, CD), (1, T))
         result = pl.pallas_call(
             functools.partial(mid_kernel, c),
             out_shape=(
@@ -560,14 +557,16 @@
             *early,
         )
         early = result[:2]
-        kept.append(result[2:])
+        kept[c] = result[2:]
     mid, mid_part = early
-    mixes, reads, b_mats = zip(*kept)
+    mixes, reads, b_mats = zip(kept[0], kept[1])
 
     moved = lax.ppermute(mid, "section", [(0, 1), (1, 0)])
     q1, q2, q3 = [
         lax.ppermute(
-            mid_part, ("section", "tensor"), [(i, tens + (i + k) % tens) for i in range(tens)]
+            mid_part,
+            ("section", "tensor"),
+            [(c * tens + i, (1 - c) * tens + (i + k) % tens) for c in range(2) for i in range(tens)],
         )
         for k in range(1, tens)
     ]
@@ -575,12 +574,12 @@
     others = pl.pallas_call(
         others_kernel,
         out_shape=shape((KIDS, T), F32),
-        in_specs=[SMEM] + [VMEM] * 4,
+        in_specs=[VMEM] * 3,
         out_specs=VMEM,
         compiler_params=params(4),
         cost_estimate=cost(10_000_000_000, 100_000_000, 0),
         name="others",
-    )(section, rest, q1, q2, q3)
+    )(q1, q2, q3)
 
     out, new, x_out, bc_out = pl.pallas_call(
         last_kernel,
@@ -590,14 +589,13 @@
             shape((3, KIDS, CD), BF16),
             shape((KIDS, 3, 2, W), BF16),
         ),
-        in_specs=[SMEM] + [VMEM] * 15 + [HBM] * 2,
+        in_specs=[SMEM] + [VMEM] * 17,
         out_specs=(HBM, HBM, HBM, HBM),
         scratch_shapes=[
-            pltpu.VMEM((72, CD), F32),
-            pltpu.VMEM((T, CD), F32),
-            pltpu.VMEM((T, CD), BF16),
-            pltpu.VMEM((72, 512), F32),
-            pltpu.VMEM((KIDS, CD + 64, N), BF16),
+            pltpu.VMEM((KIDS, 72, CD), F32),
+            pltpu.VMEM((KIDS, T, CD), F32),
+            pltpu.VMEM((KIDS, T, CD), BF16),
+            pltpu.VMEM((KIDS, 72, 512), F32),
             pltpu.VMEM((KIDS, T, CD), BF16),
             pltpu.VMEM((KIDS, CD, N), BF16),
             pltpu.VMEM((3, KIDS, CD), BF16),

time: 41.6 us -> 40 us (0.962)
  starting transfers between devices: 20.5 us -> 17.9 us
  waiting for transfers between devices: 6.54 us -> 7.97 us
    ppermute x1, starting transfers between devices: 4.01 us -> 0.01 us  [on_device(): moved = lax.ppermute(mid, 'section', [(0, 1), (1, 0)])]
    ppermute x3, waiting for transfers between devices: 1.8 us -> 3.23 us  [on_device(): lax.ppermute(mid_part, ('section', 'tensor'), [(c * tens + i, (1 - c) * t...]
    ppermute x3, starting transfers between devices: 3.87 us -> 5.23 us  [on_device(): lax.ppermute(mid_part, ('section', 'tensor'), [(c * tens + i, (1 - c) * t...]
  transfers between devices with their start and end apart: 9 -> 9, of which waited for: 2 -> 3; matrix products, arithmetic and copies ran while one was open for 1% -> 1% of each run, Pallas kernels for 9% -> 10%
where the time goes in v3:
time: 40 us; the launch traced here: 39.9 us
  starting transfers between devices  17.9 us (45%)
  Pallas kernels  11.7 us (29%)
  waiting for transfers between devices  7.97 us (20%)
  local copies, waits for them, and re-layouts  1.61 us (4%)
  between operations  0.77 us (2%)
    ppermute x5, starting transfers between devices, along(): lax.ppermute(value, axis, [(i, (i + steps) % size) for i in range(size)])  12.6 us
    ppermute x3, starting transfers between devices, on_device(): lax.ppermute(mid_part, ('section', 'tensor'), [(c * tens + i, (1 - c) * t...  5.23 us
    ppermute x5, waiting for transfers between devices, along(): lax.ppermute(value, axis, [(i, (i + steps) % size) for i in range(size)])  4.74 us
    pallas_call x2, Pallas kernels, on_device(): pl.pallas_call(functools.partial(mid_kernel, c), out_shape=(shape(out_dim...  3.98 us
    pallas_call x1, Pallas kernels, on_device(): pl.pallas_call(last_kernel, out_shape=(shape((KIDS, T, CD), BF16), shape(...  3.6 us
    ppermute x3, waiting for transfers between devices, on_device(): lax.ppermute(mid_part, ('section', 'tensor'), [(c * tens + i, (1 - c) * t...  3.23 us
    pallas_call x1, Pallas kernels, on_device(): pl.pallas_call(pick_kernel, out_shape=(message, message), in_specs=[HBM]...  2.26 us
    pallas_call x1, Pallas kernels, on_device(): pl.pallas_call(pre_kernel, out_shape=(shape((T, CD), F32), shape((T, CD),...  1.63 us
  transfers between devices with their start and end apart: 9, of which 3 were waited for; matrix products, arithmetic and copies ran while one was open for 1% of the time, Pallas kernels for 10%

profile of v3, /device:TPU:1, one launch (start us, length us, event | category | flops | bytes accessed | tf_op | source)
XLA Modules:
  0.0 39.9 jit_solution(13275977895706233471)
XLA Ops:
  0.6 0.0 copy-start
  0.6 2.3 %pick.1 = (bf16[2112,128]{1,0:T(8,128)(2,1)}, bf16[2112,128]{1,0:T(8,128)(2,1)}) custom-call(s32[64]{0:T(128)} %parents_in_ref.1, bf16[3,2,2048]{2,1,0:T(2,128)(2,1)} %bitcast.25, bf16[2,3,2,256]{3,2,1,0:T(2,128)(2,1)} %bitcast.26, bf16[2,2048,128]{2,1,0:T(8,128)(2,1)} %bitcast.24), custom_call_target="tpu_custom_call" | custom-call | tf_op jit(solution)/shard_map/pick/pallas_call | solution.py:452
  2.9 2.1 %collective-permute-start.4 = (bf16[2112,128]{1,0:T(8,128)(2,1)}, bf16[2112,128]{1,0:T(8,128)(2,1)S(1)}, u32[]{:S(2)}, u32[]{:S(2)}) collective-permute-start(bf16[2112,128]{1,0:T(8,128)(2,1)} %get-tuple-element.28), channel_id=1, source_target_pairs={{0,4},{4,8},{8,12},{12,16},{16,20},{20,24},{24,28},{28,32},{32,36}... | collective-permute-start | bytes 1622024 | tf_op jit(solution)/shard_map/ppermute | solution.py:485
  5.0 0.0 copy-start.6
  5.0 6.7 %collective-permute-start = (bf16[2112,128]{1,0:T(8,128)(2,1)}, bf16[2112,128]{1,0:T(8,128)(2,1)S(1)}, u32[]{:S(2)}, u32[]{:S(2)}) collective-permute-start(bf16[2112,128]{1,0:T(8,128)(2,1)} %get-tuple-element.25), channel_id=1, source_target_pairs={{0,124},{4,0},{8,4},{12,8},{16,12},{20,16},{24,20},{28,24},{32,28}... | collective-permute-start | bytes 1622024 | tf_op jit(solution)/shard_map/ppermute | solution.py:485
  11.7 0.0 copy-done
  11.7 0.2 square.1.p_ref
  11.9 2.8 %collective-permute-start.3 = (f32[2,64]{1,0:T(2,128)S(1)}, f32[2,64]{1,0:T(2,128)S(1)}, u32[]{:S(2)}, u32[]{:S(2)}) collective-permute-start(f32[2,64]{1,0:T(2,128)S(1)} %square.1.p_ref), channel_id=1, source_target_pairs={{0,3},{1,0},{2,1},{3,2},{4,7},{5,4},{6,5},{7,6},{8,11},{9,8},{10,9... | collective-permute-start | bytes 1544 | tf_op jit(solution)/shard_map/ppermute | solution.py:485
  14.7 0.3 collective-permute-start.2
  15.0 0.7 %collective-permute-start.1 = (f32[2,64]{1,0:T(2,128)S(1)}, f32[2,64]{1,0:T(2,128)S(1)}, u32[]{:S(2)}, u32[]{:S(2)}) collective-permute-start(f32[2,64]{1,0:T(2,128)S(1)} %square.1.p_ref), channel_id=1, source_target_pairs={{0,1},{1,2},{2,3},{3,0},{4,5},{5,6},{6,7},{7,4},{8,9},{9,10},{10,1... | collective-permute-start | bytes 1544 | tf_op jit(solution)/shard_map/ppermute | solution.py:485
  15.7 0.0 copy-start.5
  15.7 0.0 copy-start.7
  15.7 0.0 copy-start.8
  15.7 0.0 copy-done.6
  15.8 0.6 %copy-done.5 = s32[2]{0:T(128)S(1)} copy-done((s32[2]{0:T(128)S(1)}, s32[2]{0:T(128)}, u32[]{:S(2)}) %copy-start.5) | copy-done | bytes 32
  16.4 0.0 copy-done.7
  16.4 0.0 copy-done.8
  16.4 1.6 %pre.1 = (f32[64,2048]{1,0:T(8,128)S(1)}, f32[64,2048]{1,0:T(8,128)S(1)}, bf16[2,64,96]{2,1,0:T(8,128)(2,1)S(1)}, bf16[2,64,96]{2,1,0:T(8,128)(2,1)S(1)}, f32[2,32,128]{2,1,0:T(8,128)S(1)}) custom-call(s32[2]{0:T(128)S(1)} %copy-done.5, f32[2,32,64]{2,1,0:T(8,128)S(1)} %bitcast.23, f32[1,32]{1,0:T(1,128)S(1)} %copy-done.7, f32[1,32]{1,0:T(1,128)S(1)} %copy-done.8), custom_call_target="tpu_custom_call" | custom-call | flops 200000000 | bytes 5000000 | tf_op jit(solution)/shard_map/pre/pallas_call | solution.py:495
  18.1 0.0 copy-start.10
  18.1 0.6 %copy-done.10 = f32[1,32]{1,0:T(1,128)S(1)} copy-done((f32[1,32]{1,0:T(1,128)S(1)}, f32[1,32]{1,0:T(1,128)}, u32[]{:S(2)}) %copy-start.10) | copy-done | bytes 152
  18.7 0.1 broadcast_in_dim.18
  18.8 0.1 broadcast_in_dim.19.skip_ref
  18.9 0.0 copy-done.9
  18.9 0.0 copy-start.1
  18.9 0.0 copy-start.3
  18.9 0.0 copy-start.4
  18.9 0.1 reshape_squeeze.7.bc_ref
  19.0 0.0 copy-start.2
  19.0 0.0 collective-permute-done.3.r3_ref
  19.0 0.0 collective-permute-done.2.r2_ref
  19.0 0.0 collective-permute-done.1.r1_ref
  19.1 4.7 %collective-permute-done.4.message_ref.message0_ref = bf16[2112,128]{1,0:T(8,128)(2,1)S(1)} collective-permute-done((bf16[2112,128]{1,0:T(8,128)(2,1)}, bf16[2112,128]{1,0:T(8,128)(2,1)S(1)}, u32[]{:S(2)}, u32[]{:S(2)}) %collective-permute-start.4) | collective-permute-done | bytes 540704 | tf_op jit(solution)/shard_map/ppermute | solution.py:485
  23.8 0.0 copy-done.1
  23.8 0.0 copy-done.3
  23.8 0.0 copy-done.4
  23.8 0.0 copy-done.2
  23.8 2.0 %mid0.1 = (bf16[64,2048]{1,0:T(8,128)(2,1)S(1)}, f32[1,64]{1,0:T(1,128)S(1)}, bf16[64,2048]{1,0:T(8,128)(2,1)S(1)}, bf16[64,2048]{1,0:T(8,128)(2,1)S(1)}, bf16[64,256]{1,0:T(8,128)(2,1)S(1)}) custom-call(s32[1]{0:T(128)} %bitcast.sec_ref, s32[2]{0:T(128)S(1)} %copy-done.5, bf16[2112,128]{1,0:T(8,128)(2,1)S(1)} %collective-permute-done.4.message_ref.message0_ref, ...), custom_call_target="tpu_custom_call" | custom-call | flops 100000000 | bytes 3000000 | tf_op jit(solution)/shard_map/mid0/pallas_call | solution.py:524
  25.8 0.0 collective-permute-done.message_ref.message1_ref
  25.8 2.0 %mid1.1 = (bf16[2,64,2048]{2,1,0:T(8,128)(2,1)S(1)}, f32[2,64]{1,0:T(2,128)S(1)}, bf16[64,2048]{1,0:T(8,128)(2,1)S(1)}, bf16[64,2048]{1,0:T(8,128)(2,1)S(1)}, bf16[64,256]{1,0:T(8,128)(2,1)S(1)}) custom-call(s32[1]{0:T(128)} %bitcast.sec_ref, s32[2]{0:T(128)S(1)} %copy-done.5, bf16[2112,128]{1,0:T(8,128)(2,1)S(1)} %collective-permute-done.message_ref.message1_ref, ...), custom_call_target="tpu_custom_call" | custom-call | flops 100000000 | bytes 3000000 | tf_op jit(solution)/shard_map/mid1/pallas_call | solution.py:524
  27.8 3.9 %collective-permute-start.7 = (f32[2,64]{1,0:T(2,128)S(1)}, f32[2,64]{1,0:T(2,128)S(1)}, u32[]{:S(2)}, u32[]{:S(2)}) collective-permute-start(f32[2,64]{1,0:T(2,128)S(1)} %get-tuple-element.32), channel_id=1, source_target_pairs={{0,131},{1,128},{2,129},{3,130},{128,3},{129,0},{130,1},{131,2},{4... | collective-permute-start | bytes 1544 | tf_op jit(solution)/shard_map/ppermute | solution.py:566
  31.7 0.3 collective-permute-start.6
  32.0 1.0 %collective-permute-start.5 = (f32[2,64]{1,0:T(2,128)S(1)}, f32[2,64]{1,0:T(2,128)S(1)}, u32[]{:S(2)}, u32[]{:S(2)}) collective-permute-start(f32[2,64]{1,0:T(2,128)S(1)} %get-tuple-element.32), channel_id=1, source_target_pairs={{0,129},{1,130},{2,131},{3,128},{128,1},{129,2},{130,3},{131,0},{4... | collective-permute-start | bytes 1544 | tf_op jit(solution)/shard_map/ppermute | solution.py:566
  33.0 0.0 collective-permute-start.8
  33.0 0.0 collective-permute-done.7.q3_ref
  33.0 3.2 %collective-permute-done.6.q2_ref = f32[2,64]{1,0:T(2,128)S(1)} collective-permute-done((f32[2,64]{1,0:T(2,128)S(1)}, f32[2,64]{1,0:T(2,128)S(1)}, u32[]{:S(2)}, u32[]{:S(2)}) %collective-permute-start.6) | collective-permute-done | bytes 544 | tf_op jit(solution)/shard_map/ppermute | solution.py:566
  36.2 0.1 collective-permute-done.5.q1_ref
  36.3 0.0 collective-permute-done.8.moved_ref
  36.3 3.6 %last.1 = (bf16[2,64,2048]{2,1,0:T(8,128)(2,1)}, bf16[2,2048,128]{2,1,0:T(8,128)(2,1)}, bf16[3,2,2048]{2,1,0:T(2,128)(2,1)}, bf16[2,3,2,256]{3,2,1,0:T(2,128)(2,1)}) custom-call(s32[2]{0:T(128)S(1)} %copy-done.5, f32[2,64]{1,0:T(2,128)S(1)} %others.1.others_ref, f32[1,2048]{1,0:T(1,128)S(1)} %copy-done.2, f32[4,2048]{1,0:T(4,128)S(1)} %bitcast.20, ...), custom_call_target="tpu_custom_call" | custom-call | flops 200000000 | bytes 5000000 | tf_op jit(solution)/shard_map/last/pallas_call | solution.py:584
  (3 shorter events, 0.0 us)
Async XLA Ops:
  0.6 11.1 %copy-start = (bf16[2,64,2048]{2,1,0:T(8,128)(2,1)S(1)}, bf16[2,64,2048]{2,1,0:T(8,128)(2,1)}, u32[]{:S(2)}) copy-start(bf16[2,64,2048]{2,1,0:T(8,128)(2,1)} %stream_ref.5) | copy-start | bytes 1572868
  2.9 20.9 %collective-permute-start.4 = (bf16[2112,128]{1,0:T(8,128)(2,1)}, bf16[2112,128]{1,0:T(8,128)(2,1)S(1)}, u32[]{:S(2)}, u32[]{:S(2)}) collective-permute-start(bf16[2112,128]{1,0:T(8,128)(2,1)} %get-tuple-element.28), channel_id=1, source_target_pairs={{0,4},{4,8},{8,12},{12,16},{16,20},{20,24},{24,28},{28,32},{32,36}... | collective-permute-start | bytes 1622024 | tf_op jit(solution)/shard_map/ppermute | solution.py:485
  5.0 10.7 %copy-start.6 = (f32[1,2,64,32]{2,3,1,0:T(8,128)S(1)}, f32[1,2,64,32]{2,3,1,0:T(8,128)}, u32[]{:S(2)}) copy-start(f32[1,2,64,32]{2,3,1,0:T(8,128)} %param.20) | copy-start | bytes 49156
  5.0 20.8 %collective-permute-start = (bf16[2112,128]{1,0:T(8,128)(2,1)}, bf16[2112,128]{1,0:T(8,128)(2,1)S(1)}, u32[]{:S(2)}, u32[]{:S(2)}) collective-permute-start(bf16[2112,128]{1,0:T(8,128)(2,1)} %get-tuple-element.25), channel_id=1, source_target_pairs={{0,124},{4,0},{8,4},{12,8},{16,12},{20,16},{24,20},{28,24},{32,28}... | collective-permute-start | bytes 1622024 | tf_op jit(solution)/shard_map/ppermute | solution.py:485
  11.9 7.1 %collective-permute-start.3 = (f32[2,64]{1,0:T(2,128)S(1)}, f32[2,64]{1,0:T(2,128)S(1)}, u32[]{:S(2)}, u32[]{:S(2)}) collective-permute-start(f32[2,64]{1,0:T(2,128)S(1)} %square.1.p_ref), channel_id=1, source_target_pairs={{0,3},{1,0},{2,1},{3,2},{4,7},{5,4},{6,5},{7,6},{8,11},{9,8},{10,9... | collective-permute-start | bytes 1544 | tf_op jit(solution)/shard_map/ppermute | solution.py:485
  14.7 4.3 %collective-permute-start.2 = (f32[2,64]{1,0:T(2,128)S(1)}, f32[2,64]{1,0:T(2,128)S(1)}, u32[]{:S(2)}, u32[]{:S(2)}) collective-permute-start(f32[2,64]{1,0:T(2,128)S(1)} %square.1.p_ref), channel_id=1, source_target_pairs={{0,2},{1,3},{2,0},{3,1},{4,6},{5,7},{6,4},{7,5},{8,10},{9,11},{10,... | collective-permute-start | bytes 1544 | tf_op jit(solution)/shard_map/ppermute | solution.py:485
  15.0 4.0 %collective-permute-start.1 = (f32[2,64]{1,0:T(2,128)S(1)}, f32[2,64]{1,0:T(2,128)S(1)}, u32[]{:S(2)}, u32[]{:S(2)}) collective-permute-start(f32[2,64]{1,0:T(2,128)S(1)} %square.1.p_ref), channel_id=1, source_target_pairs={{0,1},{1,2},{2,3},{3,0},{4,5},{5,6},{6,7},{7,4},{8,9},{9,10},{10,1... | collective-permute-start | bytes 1544 | tf_op jit(solution)/shard_map/ppermute | solution.py:485
  15.7 0.7 %copy-start.5 = (s32[2]{0:T(128)S(1)}, s32[2]{0:T(128)}, u32[]{:S(2)}) copy-start(s32[2]{0:T(128)} %len_ref.7) | copy-start | bytes 28
  15.7 0.7 %copy-start.7 = (f32[1,32]{1,0:T(1,128)S(1)}, f32[1,32]{1,0:T(1,128)}, u32[]{:S(2)}) copy-start(f32[1,32]{1,0:T(1,128)} %log_ref.1) | copy-start | bytes 388
  15.7 0.7 %copy-start.8 = (f32[1,32]{1,0:T(1,128)S(1)}, f32[1,32]{1,0:T(1,128)}, u32[]{:S(2)}) copy-start(f32[1,32]{1,0:T(1,128)} %bias_ref.1) | copy-start | bytes 388
  16.4 2.5 %copy-start.9 = (bf16[1,2,64,2,256]{4,3,2,1,0:T(2,128)(2,1)S(1)}, bf16[1,2,64,2,256]{4,3,2,1,0:T(2,128)(2,1)}, u32[]{:S(2)}) copy-start(bf16[1,2,64,2,256]{4,3,2,1,0:T(2,128)(2,1)} %param.19) | copy-start | bytes 393220
  18.1 0.7 %copy-start.10 = (f32[1,32]{1,0:T(1,128)S(1)}, f32[1,32]{1,0:T(1,128)}, u32[]{:S(2)}) copy-start(f32[1,32]{1,0:T(1,128)} %param.28) | copy-start | bytes 388
  18.9 4.9 %copy-start.1 = (f32[1,4,2048]{2,1,0:T(4,128)S(1)}, f32[1,4,2048]{2,1,0:T(4,128)}, u32[]{:S(2)}) copy-start(f32[1,4,2048]{2,1,0:T(4,128)} %param.24) | copy-start | bytes 98308
  18.9 4.9 %copy-start.3 = (f32[1,2048]{1,0:T(1,128)S(1)}, f32[1,2048]{1,0:T(1,128)}, u32[]{:S(2)}) copy-start(f32[1,2048]{1,0:T(1,128)} %gain_ref.5) | copy-start | bytes 24580
  18.9 4.9 %copy-start.4 = (f32[1,4,2,256]{3,2,1,0:T(2,128)S(1)}, f32[1,4,2,256]{3,2,1,0:T(2,128)}, u32[]{:S(2)}) copy-start(f32[1,4,2,256]{3,2,1,0:T(2,128)} %param.25) | copy-start | bytes 24580
  19.0 4.8 %copy-start.2 = (f32[1,2048]{1,0:T(1,128)S(1)}, f32[1,2048]{1,0:T(1,128)}, u32[]{:S(2)}) copy-start(f32[1,2048]{1,0:T(1,128)} %gain_in_ref.5) | copy-start | bytes 24580
  27.8 5.2 %collective-permute-start.7 = (f32[2,64]{1,0:T(2,128)S(1)}, f32[2,64]{1,0:T(2,128)S(1)}, u32[]{:S(2)}, u32[]{:S(2)}) collective-permute-start(f32[2,64]{1,0:T(2,128)S(1)} %get-tuple-element.32), channel_id=1, source_target_pairs={{0,131},{1,128},{2,129},{3,130},{128,3},{129,0},{130,1},{131,2},{4... | collective-permute-start | bytes 1544 | tf_op jit(solution)/shard_map/ppermute | solution.py:566
  31.7 4.5 %collective-permute-start.6 = (f32[2,64]{1,0:T(2,128)S(1)}, f32[2,64]{1,0:T(2,128)S(1)}, u32[]{:S(2)}, u32[]{:S(2)}) collective-permute-start(f32[2,64]{1,0:T(2,128)S(1)} %get-tuple-element.32), channel_id=1, source_target_pairs={{0,130},{1,131},{2,128},{3,129},{128,2},{129,3},{130,0},{131,1},{4... | collective-permute-start | bytes 1544 | tf_op jit(solution)/shard_map/ppermute | solution.py:566
  32.0 4.3 %collective-permute-start.5 = (f32[2,64]{1,0:T(2,128)S(1)}, f32[2,64]{1,0:T(2,128)S(1)}, u32[]{:S(2)}, u32[]{:S(2)}) collective-permute-start(f32[2,64]{1,0:T(2,128)S(1)} %get-tuple-element.32), channel_id=1, source_target_pairs={{0,129},{1,130},{2,131},{3,128},{128,1},{129,2},{130,3},{131,0},{4... | collective-permute-start | bytes 1544 | tf_op jit(solution)/shard_map/ppermute | solution.py:566
  33.0 3.2 %collective-permute-start.8 = (bf16[2,64,2048]{2,1,0:T(8,128)(2,1)S(1)}, bf16[2,64,2048]{2,1,0:T(8,128)(2,1)S(1)}, u32[]{:S(2)}, u32[]{:S(2)}) collective-permute-start(bf16[2,64,2048]{2,1,0:T(8,128)(2,1)S(1)} %get-tuple-element.36), channel_id=1, source_target_pairs={{0,128},{128,0},{1,129},{129,1},{2,130},{130,2},{3,131},{131,3},{4... | collective-permute-start | bytes 1572872 | tf_op jit(solution)/shard_map/ppermute | solution.py:564

commit v4 on v3

--- a/solution.py
+++ b/solution.py
@@ -166,13 +166,15 @@
     return dot(mix, jnp.concatenate([xb * mask for mask in masks], axis=0), ((1,), (0,)))
 
 
-def head_offsets():
-    return iota((3 * HD, W), 0) % HD - iota((3 * HD, W), 1) // 64
-
-
-def spread(parts, offsets, q):
-    onehot = jnp.where(offsets == 4 * q, 1.0, 0.0).astype(BF16)
-    return dot(parts, onehot, ((1,), (0,)))
+def head_onehot():
+    row = iota((N, W), 0)
+    same = row % HD == iota((N, W), 1) // 64
+    return jnp.where(same & (row < 3 * HD), 1.0, 0.0).astype(BF16)
+
+
+def spread(parts, onehot, q):
+    turned = pltpu.roll(parts, (N - 4 * q) % N, 1).astype(BF16) if q else parts.astype(BF16)
+    return dot(turned, onehot, ((1,), (0,)))
 
 
 def halves(v):
@@ -218,8 +220,8 @@
         final = cum[:, T - 1 : T]
         last_ref[c] = jnp.broadcast_to(jnp.exp(final), (HD, N))
         for ref, value in ((grow_ref, jnp.exp(cum)), (weight_ref, jnp.exp(final - cum) * dt)):
-            parts = jnp.concatenate([part.astype(F32) for part in three_parts(value)], axis=0)
-            ref[c] = parts.T.astype(BF16)
+            parts = [part.astype(F32) for part in three_parts(value)]
+            ref[c] = jnp.concatenate([*parts, jnp.zeros_like(value)], axis=0).T
         edt = spread_heads(dt)
         ecum = spread_heads(cum)
         row_dt = jnp.sum(jnp.where(diag, edt, 0.0), axis=0, keepdims=True)
@@ -256,13 +258,17 @@
     for g in range(2):
         bg = bc[:, N * g : N * (g + 1)]
         cg = bc[:, W + N * g : W + N * (g + 1)]
-        inner.append(dot(cg, jnp.concatenate([bg] * 4, axis=0), ((1,), (1,)), HIGHEST))
+        ch, cl = three_parts(cg)[:2]
+        bh, bl = three_parts(bg)[:2]
+        both = jnp.concatenate([bh, bl, bh], axis=1)
+        both = jnp.concatenate([both] * 4, axis=0)
+        inner.append(dot(jnp.concatenate([ch, ch, cl], axis=1), both, ((1,), (1,))))
     cb = bc[:, W:].astype(BF16)
     valid = valid_col(len_ref[c])
     scale = lax.rsqrt(as_col(totals_ref[c : c + 1]) / CH + EPS)
     lay_rows(rows, past_ref)
     masks = head_masks()
-    offsets = head_offsets()
+    onehot = head_onehot()
     sums = [0.0, 0.0]
     for q in range(CD // W):
         at = slice(W * q, W * (q + 1))
@@ -272,7 +278,7 @@
         mix = (decay_ref[:, at] * inner[g]).astype(BF16)
         mix_ref[:, at] = mix
         read = dot(cb[:, N * g : N * (g + 1)], message_ref[at, :], ((1,), (1,)))
-        read = read * spread(grow_ref[c], offsets, q)
+        read = read * spread(grow_ref[c], onehot, q)
         read_ref[:, at] = read.astype(BF16)
         y = intra(mix, x, masks) + skip_ref[:, at] * x + read
         y_ref[:, at] = y
@@ -350,7 +356,7 @@
         puts[-1].start()
 
     masks = head_masks()
-    offsets = head_offsets()
+    onehot = head_onehot()
     chunks = [slice(W * q, W * (q + 1)) for q in range(CD // W)]
     messages = (message0_ref, message1_ref)
     valids = [valid_col(len_ref[c]) for c in range(KIDS)]
@@ -375,7 +381,7 @@
             x_in = scaled_x(moved_ref[c, :, at].astype(F32), at, scales[c], gain_in_ref)
             px_ref[c, 8:72, at] = x_in
             x = fresh_x(x_in, at, taps_ref, valids[c], px_ref.at[c])
-            xw_ref[c, :, at] = (x * spread(weight_ref[c], offsets, q)).astype(BF16)
+            xw_ref[c, :, at] = (x * spread(weight_ref[c], onehot, q)).astype(BF16)
             y = intra((mix0_ref, mix1_ref)[c][:, at], x, masks) + skip_ref[:, at] * x
             y = y + (read0_ref, read1_ref)[c][:, at].astype(F32)
             y_ref[c, :, at] = y
@@ -497,8 +503,8 @@
         out_shape=(
             shape((T, CD), F32),
             shape((T, CD), F32),
-            shape((KIDS, T, 3 * HD), BF16),
-            shape((KIDS, T, 3 * HD), BF16),
+            shape((KIDS, T, N), F32),
+            shape((KIDS, T, N), F32),
             shape((KIDS, HD, N), F32),
         ),
         in_specs=[SMEM] + [VMEM] * 3,

time: 40 us -> 39.8 us (level)
  transfers between devices with their start and end apart: 9 -> 9, of which waited for: 3 -> 3; matrix products, arithmetic and copies ran while one was open for 1% -> 1% of each run, Pallas kernels for 10% -> 9%
where the time goes in v4:
time: 39.8 us; the launch traced here: 39.7 us
  starting transfers between devices  17.9 us (45%)
  Pallas kernels  11.5 us (29%)
  waiting for transfers between devices  7.97 us (20%)
  local copies, waits for them, and re-layouts  1.61 us (4%)
  between operations  0.77 us (2%)
    ppermute x5, starting transfers between devices, along(): lax.ppermute(value, axis, [(i, (i + steps) % size) for i in range(size)])  12.6 us
    ppermute x3, starting transfers between devices, on_device(): lax.ppermute(mid_part, ('section', 'tensor'), [(c * tens + i, (1 - c) * t...  5.23 us
    ppermute x5, waiting for transfers between devices, along(): lax.ppermute(value, axis, [(i, (i + steps) % size) for i in range(size)])  4.74 us
    pallas_call x2, Pallas kernels, on_device(): pl.pallas_call(functools.partial(mid_kernel, c), out_shape=(shape(out_dim...  3.73 us
    pallas_call x1, Pallas kernels, on_device(): pl.pallas_call(last_kernel, out_shape=(shape((KIDS, T, CD), BF16), shape(...  3.62 us
    ppermute x3, waiting for transfers between devices, on_device(): lax.ppermute(mid_part, ('section', 'tensor'), [(c * tens + i, (1 - c) * t...  3.23 us
    pallas_call x1, Pallas kernels, on_device(): pl.pallas_call(pick_kernel, out_shape=(message, message), in_specs=[HBM]...  2.26 us
    pallas_call x1, Pallas kernels, on_device(): pl.pallas_call(pre_kernel, out_shape=(shape((T, CD), F32), shape((T, CD),...  1.62 us
  transfers between devices with their start and end apart: 9, of which 3 were waited for; matrix products, arithmetic and copies ran while one was open for 1% of the time, Pallas kernels for 9%

profile of v4, /device:TPU:1, one launch (start us, length us, event | category | flops | bytes accessed | tf_op | source)
XLA Modules:
  0.0 39.7 jit_solution(7605917652650009966)
XLA Ops:
  0.6 0.0 copy-start
  0.6 2.3 %pick.1 = (bf16[2112,128]{1,0:T(8,128)(2,1)}, bf16[2112,128]{1,0:T(8,128)(2,1)}) custom-call(s32[64]{0:T(128)} %parents_in_ref.1, bf16[3,2,2048]{2,1,0:T(2,128)(2,1)} %bitcast.25, bf16[2,3,2,256]{3,2,1,0:T(2,128)(2,1)} %bitcast.26, bf16[2,2048,128]{2,1,0:T(8,128)(2,1)} %bitcast.24), custom_call_target="tpu_custom_call" | custom-call | tf_op jit(solution)/shard_map/pick/pallas_call | solution.py:458
  2.9 2.1 %collective-permute-start.4 = (bf16[2112,128]{1,0:T(8,128)(2,1)}, bf16[2112,128]{1,0:T(8,128)(2,1)S(1)}, u32[]{:S(2)}, u32[]{:S(2)}) collective-permute-start(bf16[2112,128]{1,0:T(8,128)(2,1)} %get-tuple-element.28), channel_id=1, source_target_pairs={{0,4},{4,8},{8,12},{12,16},{16,20},{20,24},{24,28},{28,32},{32,36}... | collective-permute-start | bytes 1622024 | tf_op jit(solution)/shard_map/ppermute | solution.py:491
  5.0 0.0 copy-start.6
  5.0 6.7 %collective-permute-start = (bf16[2112,128]{1,0:T(8,128)(2,1)}, bf16[2112,128]{1,0:T(8,128)(2,1)S(1)}, u32[]{:S(2)}, u32[]{:S(2)}) collective-permute-start(bf16[2112,128]{1,0:T(8,128)(2,1)} %get-tuple-element.25), channel_id=1, source_target_pairs={{0,124},{4,0},{8,4},{12,8},{16,12},{20,16},{24,20},{28,24},{32,28}... | collective-permute-start | bytes 1622024 | tf_op jit(solution)/shard_map/ppermute | solution.py:491
  11.7 0.0 copy-done
  11.7 0.2 square.1.p_ref
  11.9 2.8 %collective-permute-start.3 = (f32[2,64]{1,0:T(2,128)S(1)}, f32[2,64]{1,0:T(2,128)S(1)}, u32[]{:S(2)}, u32[]{:S(2)}) collective-permute-start(f32[2,64]{1,0:T(2,128)S(1)} %square.1.p_ref), channel_id=1, source_target_pairs={{0,3},{1,0},{2,1},{3,2},{4,7},{5,4},{6,5},{7,6},{8,11},{9,8},{10,9... | collective-permute-start | bytes 1544 | tf_op jit(solution)/shard_map/ppermute | solution.py:491
  14.7 0.3 collective-permute-start.2
  15.0 0.7 %collective-permute-start.1 = (f32[2,64]{1,0:T(2,128)S(1)}, f32[2,64]{1,0:T(2,128)S(1)}, u32[]{:S(2)}, u32[]{:S(2)}) collective-permute-start(f32[2,64]{1,0:T(2,128)S(1)} %square.1.p_ref), channel_id=1, source_target_pairs={{0,1},{1,2},{2,3},{3,0},{4,5},{5,6},{6,7},{7,4},{8,9},{9,10},{10,1... | collective-permute-start | bytes 1544 | tf_op jit(solution)/shard_map/ppermute | solution.py:491
  15.7 0.0 copy-start.5
  15.7 0.0 copy-start.7
  15.7 0.0 copy-start.8
  15.7 0.0 copy-done.6
  15.8 0.6 %copy-done.5 = s32[2]{0:T(128)S(1)} copy-done((s32[2]{0:T(128)S(1)}, s32[2]{0:T(128)}, u32[]{:S(2)}) %copy-start.5) | copy-done | bytes 32
  16.4 0.0 copy-done.7
  16.4 0.0 copy-done.8
  16.4 1.6 %pre.1 = (f32[64,2048]{1,0:T(8,128)S(1)}, f32[64,2048]{1,0:T(8,128)S(1)}, f32[2,64,128]{2,1,0:T(8,128)S(1)}, f32[2,64,128]{2,1,0:T(8,128)S(1)}, f32[2,32,128]{2,1,0:T(8,128)S(1)}) custom-call(s32[2]{0:T(128)S(1)} %copy-done.5, f32[2,32,64]{2,1,0:T(8,128)S(1)} %bitcast.23, f32[1,32]{1,0:T(1,128)S(1)} %copy-done.7, f32[1,32]{1,0:T(1,128)S(1)} %copy-done.8), custom_call_target="tpu_custom_call" | custom-call | flops 200000000 | bytes 5000000 | tf_op jit(solution)/shard_map/pre/pallas_call | solution.py:501
  18.1 0.0 copy-start.10
  18.1 0.6 %copy-done.10 = f32[1,32]{1,0:T(1,128)S(1)} copy-done((f32[1,32]{1,0:T(1,128)S(1)}, f32[1,32]{1,0:T(1,128)}, u32[]{:S(2)}) %copy-start.10) | copy-done | bytes 152
  18.7 0.1 broadcast_in_dim.18
  18.8 0.1 broadcast_in_dim.19.skip_ref
  18.9 0.0 copy-done.9
  18.9 0.0 copy-start.1
  18.9 0.0 copy-start.3
  18.9 0.0 copy-start.4
  18.9 0.1 reshape_squeeze.7.bc_ref
  19.0 0.0 copy-start.2
  19.0 0.0 collective-permute-done.3.r3_ref
  19.0 0.0 collective-permute-done.2.r2_ref
  19.0 0.0 collective-permute-done.1.r1_ref
  19.1 4.7 %collective-permute-done.4.message_ref.message0_ref = bf16[2112,128]{1,0:T(8,128)(2,1)S(1)} collective-permute-done((bf16[2112,128]{1,0:T(8,128)(2,1)}, bf16[2112,128]{1,0:T(8,128)(2,1)S(1)}, u32[]{:S(2)}, u32[]{:S(2)}) %collective-permute-start.4) | collective-permute-done | bytes 540704 | tf_op jit(solution)/shard_map/ppermute | solution.py:491
  23.8 0.0 copy-done.1
  23.8 0.0 copy-done.3
  23.8 0.0 copy-done.4
  23.8 0.0 copy-done.2
  23.8 1.9 %mid0.1 = (bf16[64,2048]{1,0:T(8,128)(2,1)S(1)}, f32[1,64]{1,0:T(1,128)S(1)}, bf16[64,2048]{1,0:T(8,128)(2,1)S(1)}, bf16[64,2048]{1,0:T(8,128)(2,1)S(1)}, bf16[64,256]{1,0:T(8,128)(2,1)S(1)}) custom-call(s32[1]{0:T(128)} %bitcast.sec_ref, s32[2]{0:T(128)S(1)} %copy-done.5, bf16[2112,128]{1,0:T(8,128)(2,1)S(1)} %collective-permute-done.4.message_ref.message0_ref, ...), custom_call_target="tpu_custom_call" | custom-call | flops 100000000 | bytes 3000000 | tf_op jit(solution)/shard_map/mid0/pallas_call | solution.py:530
  25.7 0.0 collective-permute-done.message_ref.message1_ref
  25.7 1.9 %mid1.1 = (bf16[2,64,2048]{2,1,0:T(8,128)(2,1)S(1)}, f32[2,64]{1,0:T(2,128)S(1)}, bf16[64,2048]{1,0:T(8,128)(2,1)S(1)}, bf16[64,2048]{1,0:T(8,128)(2,1)S(1)}, bf16[64,256]{1,0:T(8,128)(2,1)S(1)}) custom-call(s32[1]{0:T(128)} %bitcast.sec_ref, s32[2]{0:T(128)S(1)} %copy-done.5, bf16[2112,128]{1,0:T(8,128)(2,1)S(1)} %collective-permute-done.message_ref.message1_ref, ...), custom_call_target="tpu_custom_call" | custom-call | flops 100000000 | bytes 3000000 | tf_op jit(solution)/shard_map/mid1/pallas_call | solution.py:530
  27.6 3.9 %collective-permute-start.7 = (f32[2,64]{1,0:T(2,128)S(1)}, f32[2,64]{1,0:T(2,128)S(1)}, u32[]{:S(2)}, u32[]{:S(2)}) collective-permute-start(f32[2,64]{1,0:T(2,128)S(1)} %get-tuple-element.32), channel_id=1, source_target_pairs={{0,131},{1,128},{2,129},{3,130},{128,3},{129,0},{130,1},{131,2},{4... | collective-permute-start | bytes 1544 | tf_op jit(solution)/shard_map/ppermute | solution.py:572
  31.5 0.3 collective-permute-start.6
  31.8 1.0 %collective-permute-start.5 = (f32[2,64]{1,0:T(2,128)S(1)}, f32[2,64]{1,0:T(2,128)S(1)}, u32[]{:S(2)}, u32[]{:S(2)}) collective-permute-start(f32[2,64]{1,0:T(2,128)S(1)} %get-tuple-element.32), channel_id=1, source_target_pairs={{0,129},{1,130},{2,131},{3,128},{128,1},{129,2},{130,3},{131,0},{4... | collective-permute-start | bytes 1544 | tf_op jit(solution)/shard_map/ppermute | solution.py:572
  32.8 0.0 collective-permute-start.8
  32.8 0.0 collective-permute-done.7.q3_ref
  32.8 3.2 %collective-permute-done.6.q2_ref = f32[2,64]{1,0:T(2,128)S(1)} collective-permute-done((f32[2,64]{1,0:T(2,128)S(1)}, f32[2,64]{1,0:T(2,128)S(1)}, u32[]{:S(2)}, u32[]{:S(2)}) %collective-permute-start.6) | collective-permute-done | bytes 544 | tf_op jit(solution)/shard_map/ppermute | solution.py:572
  36.0 0.1 collective-permute-done.5.q1_ref
  36.0 0.0 collective-permute-done.8.moved_ref
  36.0 3.6 %last.1 = (bf16[2,64,2048]{2,1,0:T(8,128)(2,1)}, bf16[2,2048,128]{2,1,0:T(8,128)(2,1)}, bf16[3,2,2048]{2,1,0:T(2,128)(2,1)}, bf16[2,3,2,256]{3,2,1,0:T(2,128)(2,1)}) custom-call(s32[2]{0:T(128)S(1)} %copy-done.5, f32[2,64]{1,0:T(2,128)S(1)} %others.1.others_ref, f32[1,2048]{1,0:T(1,128)S(1)} %copy-done.2, f32[4,2048]{1,0:T(4,128)S(1)} %bitcast.20, ...), custom_call_target="tpu_custom_call" | custom-call | flops 200000000 | bytes 5000000 | tf_op jit(solution)/shard_map/last/pallas_call | solution.py:590
  (3 shorter events, 0.0 us)
Async XLA Ops:
  0.6 11.1 %copy-start = (bf16[2,64,2048]{2,1,0:T(8,128)(2,1)S(1)}, bf16[2,64,2048]{2,1,0:T(8,128)(2,1)}, u32[]{:S(2)}) copy-start(bf16[2,64,2048]{2,1,0:T(8,128)(2,1)} %stream_ref.5) | copy-start | bytes 1572868
  2.9 20.9 %collective-permute-start.4 = (bf16[2112,128]{1,0:T(8,128)(2,1)}, bf16[2112,128]{1,0:T(8,128)(2,1)S(1)}, u32[]{:S(2)}, u32[]{:S(2)}) collective-permute-start(bf16[2112,128]{1,0:T(8,128)(2,1)} %get-tuple-element.28), channel_id=1, source_target_pairs={{0,4},{4,8},{8,12},{12,16},{16,20},{20,24},{24,28},{28,32},{32,36}... | collective-permute-start | bytes 1622024 | tf_op jit(solution)/shard_map/ppermute | solution.py:491
  5.0 10.7 %copy-start.6 = (f32[1,2,64,32]{2,3,1,0:T(8,128)S(1)}, f32[1,2,64,32]{2,3,1,0:T(8,128)}, u32[]{:S(2)}) copy-start(f32[1,2,64,32]{2,3,1,0:T(8,128)} %param.20) | copy-start | bytes 49156
  5.0 20.7 %collective-permute-start = (bf16[2112,128]{1,0:T(8,128)(2,1)}, bf16[2112,128]{1,0:T(8,128)(2,1)S(1)}, u32[]{:S(2)}, u32[]{:S(2)}) collective-permute-start(bf16[2112,128]{1,0:T(8,128)(2,1)} %get-tuple-element.25), channel_id=1, source_target_pairs={{0,124},{4,0},{8,4},{12,8},{16,12},{20,16},{24,20},{28,24},{32,28}... | collective-permute-start | bytes 1622024 | tf_op jit(solution)/shard_map/ppermute | solution.py:491
  11.9 7.1 %collective-permute-start.3 = (f32[2,64]{1,0:T(2,128)S(1)}, f32[2,64]{1,0:T(2,128)S(1)}, u32[]{:S(2)}, u32[]{:S(2)}) collective-permute-start(f32[2,64]{1,0:T(2,128)S(1)} %square.1.p_ref), channel_id=1, source_target_pairs={{0,3},{1,0},{2,1},{3,2},{4,7},{5,4},{6,5},{7,6},{8,11},{9,8},{10,9... | collective-permute-start | bytes 1544 | tf_op jit(solution)/shard_map/ppermute | solution.py:491
  14.7 4.3 %collective-permute-start.2 = (f32[2,64]{1,0:T(2,128)S(1)}, f32[2,64]{1,0:T(2,128)S(1)}, u32[]{:S(2)}, u32[]{:S(2)}) collective-permute-start(f32[2,64]{1,0:T(2,128)S(1)} %square.1.p_ref), channel_id=1, source_target_pairs={{0,2},{1,3},{2,0},{3,1},{4,6},{5,7},{6,4},{7,5},{8,10},{9,11},{10,... | collective-permute-start | bytes 1544 | tf_op jit(solution)/shard_map/ppermute | solution.py:491
  15.0 4.0 %collective-permute-start.1 = (f32[2,64]{1,0:T(2,128)S(1)}, f32[2,64]{1,0:T(2,128)S(1)}, u32[]{:S(2)}, u32[]{:S(2)}) collective-permute-start(f32[2,64]{1,0:T(2,128)S(1)} %square.1.p_ref), channel_id=1, source_target_pairs={{0,1},{1,2},{2,3},{3,0},{4,5},{5,6},{6,7},{7,4},{8,9},{9,10},{10,1... | collective-permute-start | bytes 1544 | tf_op jit(solution)/shard_map/ppermute | solution.py:491
  15.7 0.7 %copy-start.5 = (s32[2]{0:T(128)S(1)}, s32[2]{0:T(128)}, u32[]{:S(2)}) copy-start(s32[2]{0:T(128)} %len_ref.7) | copy-start | bytes 28
  15.7 0.7 %copy-start.7 = (f32[1,32]{1,0:T(1,128)S(1)}, f32[1,32]{1,0:T(1,128)}, u32[]{:S(2)}) copy-start(f32[1,32]{1,0:T(1,128)} %log_ref.1) | copy-start | bytes 388
  15.7 0.7 %copy-start.8 = (f32[1,32]{1,0:T(1,128)S(1)}, f32[1,32]{1,0:T(1,128)}, u32[]{:S(2)}) copy-start(f32[1,32]{1,0:T(1,128)} %bias_ref.1) | copy-start | bytes 388
  16.4 2.5 %copy-start.9 = (bf16[1,2,64,2,256]{4,3,2,1,0:T(2,128)(2,1)S(1)}, bf16[1,2,64,2,256]{4,3,2,1,0:T(2,128)(2,1)}, u32[]{:S(2)}) copy-start(bf16[1,2,64,2,256]{4,3,2,1,0:T(2,128)(2,1)} %param.19) | copy-start | bytes 393220
  18.1 0.7 %copy-start.10 = (f32[1,32]{1,0:T(1,128)S(1)}, f32[1,32]{1,0:T(1,128)}, u32[]{:S(2)}) copy-start(f32[1,32]{1,0:T(1,128)} %param.28) | copy-start | bytes 388
  18.9 4.9 %copy-start.1 = (f32[1,4,2048]{2,1,0:T(4,128)S(1)}, f32[1,4,2048]{2,1,0:T(4,128)}, u32[]{:S(2)}) copy-start(f32[1,4,2048]{2,1,0:T(4,128)} %param.24) | copy-start | bytes 98308
  18.9 4.9 %copy-start.3 = (f32[1,2048]{1,0:T(1,128)S(1)}, f32[1,2048]{1,0:T(1,128)}, u32[]{:S(2)}) copy-start(f32[1,2048]{1,0:T(1,128)} %gain_ref.5) | copy-start | bytes 24580
  18.9 4.9 %copy-start.4 = (f32[1,4,2,256]{3,2,1,0:T(2,128)S(1)}, f32[1,4,2,256]{3,2,1,0:T(2,128)}, u32[]{:S(2)}) copy-start(f32[1,4,2,256]{3,2,1,0:T(2,128)} %param.25) | copy-start | bytes 24580
  19.0 4.8 %copy-start.2 = (f32[1,2048]{1,0:T(1,128)S(1)}, f32[1,2048]{1,0:T(1,128)}, u32[]{:S(2)}) copy-start(f32[1,2048]{1,0:T(1,128)} %gain_in_ref.5) | copy-start | bytes 24580
  27.6 5.2 %collective-permute-start.7 = (f32[2,64]{1,0:T(2,128)S(1)}, f32[2,64]{1,0:T(2,128)S(1)}, u32[]{:S(2)}, u32[]{:S(2)}) collective-permute-start(f32[2,64]{1,0:T(2,128)S(1)} %get-tuple-element.32), channel_id=1, source_target_pairs={{0,131},{1,128},{2,129},{3,130},{128,3},{129,0},{130,1},{131,2},{4... | collective-permute-start | bytes 1544 | tf_op jit(solution)/shard_map/ppermute | solution.py:572
  31.5 4.5 %collective-permute-start.6 = (f32[2,64]{1,0:T(2,128)S(1)}, f32[2,64]{1,0:T(2,128)S(1)}, u32[]{:S(2)}, u32[]{:S(2)}) collective-permute-start(f32[2,64]{1,0:T(2,128)S(1)} %get-tuple-element.32), channel_id=1, source_target_pairs={{0,130},{1,131},{2,128},{3,129},{128,2},{129,3},{130,0},{131,1},{4... | collective-permute-start | bytes 1544 | tf_op jit(solution)/shard_map/ppermute | solution.py:572
  31.8 4.3 %collective-permute-start.5 = (f32[2,64]{1,0:T(2,128)S(1)}, f32[2,64]{1,0:T(2,128)S(1)}, u32[]{:S(2)}, u32[]{:S(2)}) collective-permute-start(f32[2,64]{1,0:T(2,128)S(1)} %get-tuple-element.32), channel_id=1, source_target_pairs={{0,129},{1,130},{2,131},{3,128},{128,1},{129,2},{130,3},{131,0},{4... | collective-permute-start | bytes 1544 | tf_op jit(solution)/shard_map/ppermute | solution.py:572
  32.8 3.2 %collective-permute-start.8 = (bf16[2,64,2048]{2,1,0:T(8,128)(2,1)S(1)}, bf16[2,64,2048]{2,1,0:T(8,128)(2,1)S(1)}, u32[]{:S(2)}, u32[]{:S(2)}) collective-permute-start(bf16[2,64,2048]{2,1,0:T(8,128)(2,1)S(1)} %get-tuple-element.36), channel_id=1, source_target_pairs={{0,128},{128,0},{1,129},{129,1},{2,130},{130,2},{3,131},{131,3},{4... | collective-permute-start | bytes 1572872 | tf_op jit(solution)/shard_map/ppermute | solution.py:570

commit v5 on v4

--- a/solution.py
+++ b/solution.py
@@ -24,7 +24,8 @@
 HBM = pl.BlockSpec(memory_space=pl.ANY)
 BIG = 60
 PARTS = 4
-LATE = 1
+LATE = 0
+EXTRA = 16
 
 
 def iota(shape, dim):
@@ -110,7 +111,7 @@
             pieces += [both[p : p + 1, N * j : N * (j + 1)] for p in range(2) for j in range(2)]
         pieces.append(jnp.zeros((4, N), F32))
         rows_ref[i] = jnp.concatenate(pieces, axis=0).astype(BF16)
-        puts.append(pltpu.make_async_copy(rows_ref.at[i], outs[i].at[CD:], out_sems.at[i, PARTS]))
+        puts.append(pltpu.make_async_copy(rows_ref.at[i], outs[i].at[pl.ds(CD, 64)], out_sems.at[i, PARTS]))
         puts[-1].start()
     for j, at in enumerate(parts):
         for i in range(KIDS):
@@ -122,6 +123,12 @@
                 )
             )
             puts[-1].start()
+    puts.append(
+        pltpu.make_async_copy(
+            rows_ref.at[0, :EXTRA], one_ref.at[pl.ds(CD + 64, EXTRA)], out_sems.at[2, 0]
+        )
+    )
+    puts[-1].start()
     for copy in puts:
         copy.wait()
 
@@ -251,7 +258,7 @@
         early_ref, early_part_ref = refs[:2]
         refs = refs[2:]
     out_ref, part_ref, mix_ref, read_ref, b_ref, pbc_ref, past_ref, y_ref = refs
-    rows = message_ref[CD:, :].astype(F32)
+    rows = message_ref[CD : CD + 64, :].astype(F32)
     bc = fresh_bc(rows, bc_ref[c], taps_bc_ref, pbc_ref)
     b_ref[...] = bc[:, :W].astype(BF16)
     inner = []
@@ -368,7 +375,7 @@
             squares = squares + halves(s * s)
         total = jnp.sum(squares, axis=1, keepdims=True) + as_col(others_ref[c : c + 1])
         scales.append(lax.rsqrt(total / CH + EPS))
-        rows = messages[c][CD:, :].astype(F32)
+        rows = messages[c][CD : CD + 64, :].astype(F32)
         lay_rows(rows, px_ref.at[c])
         for k in range(3):
             for j in range(4):
@@ -454,10 +461,11 @@
     tens = lax.axis_size("tensor")
     peers = lax.axis_size("beam")
     section = lax.axis_index("section").astype(jnp.int32)[None]
+    longer = shape((CD + 64 + EXTRA, N), BF16)
     message = shape((CD + 64, N), BF16)
     fwd, bwd = pl.pallas_call(
         pick_kernel,
-        out_shape=(message, message),
+        out_shape=(longer, message),
         in_specs=[HBM] * 4,
         out_specs=(HBM, HBM),
         scratch_shapes=[
@@ -467,7 +475,7 @@
             pltpu.VMEM((KIDS, CD, N), BF16),
             pltpu.VMEM((2, 64, N), BF16),
             pltpu.SemaphoreType.DMA((3 + KIDS * PARTS,)),
-            pltpu.SemaphoreType.DMA((2, PARTS + 1)),
+            pltpu.SemaphoreType.DMA((3, PARTS + 1)),
         ],
         compiler_params=params(BIG),
         name="pick",
@@ -544,7 +552,7 @@
                 pltpu.VMEM((T, CD), F32),
             ],
             compiler_params=params(12),
-            cost_estimate=cost(100_000_000, 3_000_000, 500_000),
+            cost_estimate=cost(1, 1),
             name="mid%d" % c,
         )(
             section,

time: 39.8 us -> 39.4 us (0.990)
  waiting for transfers between devices: 7.97 us -> 7.13 us
    ppermute x5, waiting for transfers between devices: 4.74 us -> 3.9 us  [along(): lax.ppermute(value, axis, [(i, (i + steps) % size) for i in range(size)])]
where the time goes in v5:
time: 39.4 us; the launch traced here: 39.2 us
  starting transfers between devices  18.2 us (46%)
  Pallas kernels  11.6 us (29%)
  waiting for transfers between devices  7.13 us (18%)
  local copies, waits for them, and re-layouts  1.61 us (4%)
  between operations  0.77 us (2%)
    ppermute x5, starting transfers between devices, along(): lax.ppermute(value, axis, [(i, (i + steps) % size) for i in range(size)])  12.6 us
    ppermute x3, starting transfers between devices, on_device(): lax.ppermute(mid_part, ('section', 'tensor'), [(c * tens + i, (1 - c) * t...  5.54 us
    ppermute x5, waiting for transfers between devices, along(): lax.ppermute(value, axis, [(i, (i + steps) % size) for i in range(size)])  3.9 us
    pallas_call x2, Pallas kernels, on_device(): pl.pallas_call(functools.partial(mid_kernel, c), out_shape=(shape(out_dim...  3.76 us
    pallas_call x1, Pallas kernels, on_device(): pl.pallas_call(last_kernel, out_shape=(shape((KIDS, T, CD), BF16), shape(...  3.66 us
    ppermute x3, waiting for transfers between devices, on_device(): lax.ppermute(mid_part, ('section', 'tensor'), [(c * tens + i, (1 - c) * t...  3.23 us
    pallas_call x1, Pallas kernels, on_device(): pl.pallas_call(pick_kernel, out_shape=(longer, message), in_specs=[HBM] *...  2.31 us
    pallas_call x1, Pallas kernels, on_device(): pl.pallas_call(pre_kernel, out_shape=(shape((T, CD), F32), shape((T, CD),...  1.62 us
  transfers between devices with their start and end apart: 9, of which 3 were waited for; matrix products, arithmetic and copies ran while one was open for 1% of the time, Pallas kernels for 9%

profile of v5, /device:TPU:1, one launch (start us, length us, event | category | flops | bytes accessed | tf_op | source)
XLA Modules:
  0.0 39.2 jit_solution(2651127439511117342)
XLA Ops:
  0.6 0.0 copy-start
  0.6 2.3 %pick.1 = (bf16[2128,128]{1,0:T(8,128)(2,1)}, bf16[2112,128]{1,0:T(8,128)(2,1)}) custom-call(s32[64]{0:T(128)} %parents_in_ref.1, bf16[3,2,2048]{2,1,0:T(2,128)(2,1)} %bitcast.25, bf16[2,3,2,256]{3,2,1,0:T(2,128)(2,1)} %bitcast.26, bf16[2,2048,128]{2,1,0:T(8,128)(2,1)} %bitcast.24), custom_call_target="tpu_custom_call" | custom-call | tf_op jit(solution)/shard_map/pick/pallas_call | solution.py:466
  3.0 2.1 %collective-permute-start = (bf16[2128,128]{1,0:T(8,128)(2,1)}, bf16[2128,128]{1,0:T(8,128)(2,1)S(1)}, u32[]{:S(2)}, u32[]{:S(2)}) collective-permute-start(bf16[2128,128]{1,0:T(8,128)(2,1)} %get-tuple-element.25), channel_id=1, source_target_pairs={{0,4},{4,8},{8,12},{12,16},{16,20},{20,24},{24,28},{28,32},{32,36}... | collective-permute-start | bytes 1634312 | tf_op jit(solution)/shard_map/ppermute | solution.py:499
  5.1 0.0 copy-start.6
  5.1 6.7 %collective-permute-start.4 = (bf16[2112,128]{1,0:T(8,128)(2,1)}, bf16[2112,128]{1,0:T(8,128)(2,1)S(1)}, u32[]{:S(2)}, u32[]{:S(2)}) collective-permute-start(bf16[2112,128]{1,0:T(8,128)(2,1)} %get-tuple-element.28), channel_id=1, source_target_pairs={{0,124},{4,0},{8,4},{12,8},{16,12},{20,16},{24,20},{28,24},{32,28}... | collective-permute-start | bytes 1622024 | tf_op jit(solution)/shard_map/ppermute | solution.py:499
  11.7 0.0 copy-done
  11.7 0.2 square.1.p_ref
  11.9 2.8 %collective-permute-start.3 = (f32[2,64]{1,0:T(2,128)S(1)}, f32[2,64]{1,0:T(2,128)S(1)}, u32[]{:S(2)}, u32[]{:S(2)}) collective-permute-start(f32[2,64]{1,0:T(2,128)S(1)} %square.1.p_ref), channel_id=1, source_target_pairs={{0,3},{1,0},{2,1},{3,2},{4,7},{5,4},{6,5},{7,6},{8,11},{9,8},{10,9... | collective-permute-start | bytes 1544 | tf_op jit(solution)/shard_map/ppermute | solution.py:499
  14.7 0.3 collective-permute-start.2
  15.1 0.7 %collective-permute-start.1 = (f32[2,64]{1,0:T(2,128)S(1)}, f32[2,64]{1,0:T(2,128)S(1)}, u32[]{:S(2)}, u32[]{:S(2)}) collective-permute-start(f32[2,64]{1,0:T(2,128)S(1)} %square.1.p_ref), channel_id=1, source_target_pairs={{0,1},{1,2},{2,3},{3,0},{4,5},{5,6},{6,7},{7,4},{8,9},{9,10},{10,1... | collective-permute-start | bytes 1544 | tf_op jit(solution)/shard_map/ppermute | solution.py:499
  15.8 0.0 copy-start.5
  15.8 0.0 copy-start.7
  15.8 0.0 copy-start.8
  15.8 0.0 copy-done.6
  15.8 0.6 %copy-done.5 = s32[2]{0:T(128)S(1)} copy-done((s32[2]{0:T(128)S(1)}, s32[2]{0:T(128)}, u32[]{:S(2)}) %copy-start.5) | copy-done | bytes 32
  16.4 0.0 copy-done.7
  16.5 0.0 copy-done.8
  16.5 1.6 %pre.1 = (f32[64,2048]{1,0:T(8,128)S(1)}, f32[64,2048]{1,0:T(8,128)S(1)}, f32[2,64,128]{2,1,0:T(8,128)S(1)}, f32[2,64,128]{2,1,0:T(8,128)S(1)}, f32[2,32,128]{2,1,0:T(8,128)S(1)}) custom-call(s32[2]{0:T(128)S(1)} %copy-done.5, f32[2,32,64]{2,1,0:T(8,128)S(1)} %bitcast.23, f32[1,32]{1,0:T(1,128)S(1)} %copy-done.7, f32[1,32]{1,0:T(1,128)S(1)} %copy-done.8), custom_call_target="tpu_custom_call" | custom-call | flops 200000000 | bytes 5000000 | tf_op jit(solution)/shard_map/pre/pallas_call | solution.py:509
  18.1 0.0 copy-start.10
  18.1 0.6 %copy-done.10 = f32[1,32]{1,0:T(1,128)S(1)} copy-done((f32[1,32]{1,0:T(1,128)S(1)}, f32[1,32]{1,0:T(1,128)}, u32[]{:S(2)}) %copy-start.10) | copy-done | bytes 152
  18.8 0.1 broadcast_in_dim.18
  18.8 0.1 broadcast_in_dim.19.skip_ref
  18.9 0.0 copy-done.9
  18.9 0.0 copy-start.1
  18.9 0.0 copy-start.3
  18.9 0.0 copy-start.4
  19.0 0.1 reshape_squeeze.7.bc_ref
  19.1 0.0 copy-start.2
  19.1 0.0 collective-permute-done.3.r3_ref
  19.1 0.0 collective-permute-done.2.r2_ref
  19.1 0.0 collective-permute-done.1.r1_ref
  19.1 3.9 %collective-permute-done.4.message_ref.message1_ref = bf16[2112,128]{1,0:T(8,128)(2,1)S(1)} collective-permute-done((bf16[2112,128]{1,0:T(8,128)(2,1)}, bf16[2112,128]{1,0:T(8,128)(2,1)S(1)}, u32[]{:S(2)}, u32[]{:S(2)}) %collective-permute-start.4) | collective-permute-done | bytes 540704 | tf_op jit(solution)/shard_map/ppermute | solution.py:499
  23.0 0.0 copy-done.1
  23.0 0.0 copy-done.3
  23.0 0.0 copy-done.4
  23.0 0.0 copy-done.2
  23.0 1.9 %mid1.1 = (bf16[64,2048]{1,0:T(8,128)(2,1)S(1)}, f32[1,64]{1,0:T(1,128)S(1)}, bf16[64,2048]{1,0:T(8,128)(2,1)S(1)}, bf16[64,2048]{1,0:T(8,128)(2,1)S(1)}, bf16[64,256]{1,0:T(8,128)(2,1)S(1)}) custom-call(s32[1]{0:T(128)} %bitcast.sec_ref, s32[2]{0:T(128)S(1)} %copy-done.5, bf16[2112,128]{1,0:T(8,128)(2,1)S(1)} %collective-permute-done.4.message_ref.message1_ref, ...), custom_call_target="tpu_custom_call" | custom-call | flops 1 | bytes 1 | tf_op jit(solution)/shard_map/mid1/pallas_call | solution.py:538
  24.9 0.0 collective-permute-done.message_ref.message0_ref
  24.9 1.9 %mid0.1 = (bf16[2,64,2048]{2,1,0:T(8,128)(2,1)S(1)}, f32[2,64]{1,0:T(2,128)S(1)}, bf16[64,2048]{1,0:T(8,128)(2,1)S(1)}, bf16[64,2048]{1,0:T(8,128)(2,1)S(1)}, bf16[64,256]{1,0:T(8,128)(2,1)S(1)}) custom-call(s32[1]{0:T(128)} %bitcast.sec_ref, s32[2]{0:T(128)S(1)} %copy-done.5, bf16[2128,128]{1,0:T(8,128)(2,1)S(1)} %collective-permute-done.message_ref.message0_ref, ...), custom_call_target="tpu_custom_call" | custom-call | flops 1 | bytes 1 | tf_op jit(solution)/shard_map/mid0/pallas_call | solution.py:538
  26.8 4.2 %collective-permute-start.7 = (f32[2,64]{1,0:T(2,128)S(1)}, f32[2,64]{1,0:T(2,128)S(1)}, u32[]{:S(2)}, u32[]{:S(2)}) collective-permute-start(f32[2,64]{1,0:T(2,128)S(1)} %get-tuple-element.32), channel_id=1, source_target_pairs={{0,131},{1,128},{2,129},{3,130},{128,3},{129,0},{130,1},{131,2},{4... | collective-permute-start | bytes 1544 | tf_op jit(solution)/shard_map/ppermute | solution.py:580
  31.0 0.3 collective-permute-start.6
  31.3 1.0 %collective-permute-start.5 = (f32[2,64]{1,0:T(2,128)S(1)}, f32[2,64]{1,0:T(2,128)S(1)}, u32[]{:S(2)}, u32[]{:S(2)}) collective-permute-start(f32[2,64]{1,0:T(2,128)S(1)} %get-tuple-element.32), channel_id=1, source_target_pairs={{0,129},{1,130},{2,131},{3,128},{128,1},{129,2},{130,3},{131,0},{4... | collective-permute-start | bytes 1544 | tf_op jit(solution)/shard_map/ppermute | solution.py:580
  32.3 0.0 collective-permute-start.8
  32.3 0.0 collective-permute-done.7.q3_ref
  32.3 3.2 %collective-permute-done.6.q2_ref = f32[2,64]{1,0:T(2,128)S(1)} collective-permute-done((f32[2,64]{1,0:T(2,128)S(1)}, f32[2,64]{1,0:T(2,128)S(1)}, u32[]{:S(2)}, u32[]{:S(2)}) %collective-permute-start.6) | collective-permute-done | bytes 544 | tf_op jit(solution)/shard_map/ppermute | solution.py:580
  35.5 0.1 collective-permute-done.5.q1_ref
  35.6 0.0 collective-permute-done.8.moved_ref
  35.6 3.7 %last.1 = (bf16[2,64,2048]{2,1,0:T(8,128)(2,1)}, bf16[2,2048,128]{2,1,0:T(8,128)(2,1)}, bf16[3,2,2048]{2,1,0:T(2,128)(2,1)}, bf16[2,3,2,256]{3,2,1,0:T(2,128)(2,1)}) custom-call(s32[2]{0:T(128)S(1)} %copy-done.5, f32[2,64]{1,0:T(2,128)S(1)} %others.1.others_ref, f32[1,2048]{1,0:T(1,128)S(1)} %copy-done.2, f32[4,2048]{1,0:T(4,128)S(1)} %bitcast.20, ...), custom_call_target="tpu_custom_call" | custom-call | flops 200000000 | bytes 5000000 | tf_op jit(solution)/shard_map/last/pallas_call | solution.py:598
  (3 shorter events, 0.0 us)
Async XLA Ops:
  0.6 11.1 %copy-start = (bf16[2,64,2048]{2,1,0:T(8,128)(2,1)S(1)}, bf16[2,64,2048]{2,1,0:T(8,128)(2,1)}, u32[]{:S(2)}) copy-start(bf16[2,64,2048]{2,1,0:T(8,128)(2,1)} %stream_ref.5) | copy-start | bytes 1572868
  3.0 21.9 %collective-permute-start = (bf16[2128,128]{1,0:T(8,128)(2,1)}, bf16[2128,128]{1,0:T(8,128)(2,1)S(1)}, u32[]{:S(2)}, u32[]{:S(2)}) collective-permute-start(bf16[2128,128]{1,0:T(8,128)(2,1)} %get-tuple-element.25), channel_id=1, source_target_pairs={{0,4},{4,8},{8,12},{12,16},{16,20},{20,24},{24,28},{28,32},{32,36}... | collective-permute-start | bytes 1634312 | tf_op jit(solution)/shard_map/ppermute | solution.py:499
  5.1 10.7 %copy-start.6 = (f32[1,2,64,32]{2,3,1,0:T(8,128)S(1)}, f32[1,2,64,32]{2,3,1,0:T(8,128)}, u32[]{:S(2)}) copy-start(f32[1,2,64,32]{2,3,1,0:T(8,128)} %param.20) | copy-start | bytes 49156
  5.1 17.9 %collective-permute-start.4 = (bf16[2112,128]{1,0:T(8,128)(2,1)}, bf16[2112,128]{1,0:T(8,128)(2,1)S(1)}, u32[]{:S(2)}, u32[]{:S(2)}) collective-permute-start(bf16[2112,128]{1,0:T(8,128)(2,1)} %get-tuple-element.28), channel_id=1, source_target_pairs={{0,124},{4,0},{8,4},{12,8},{16,12},{20,16},{24,20},{28,24},{32,28}... | collective-permute-start | bytes 1622024 | tf_op jit(solution)/shard_map/ppermute | solution.py:499
  11.9 7.1 %collective-permute-start.3 = (f32[2,64]{1,0:T(2,128)S(1)}, f32[2,64]{1,0:T(2,128)S(1)}, u32[]{:S(2)}, u32[]{:S(2)}) collective-permute-start(f32[2,64]{1,0:T(2,128)S(1)} %square.1.p_ref), channel_id=1, source_target_pairs={{0,3},{1,0},{2,1},{3,2},{4,7},{5,4},{6,5},{7,6},{8,11},{9,8},{10,9... | collective-permute-start | bytes 1544 | tf_op jit(solution)/shard_map/ppermute | solution.py:499
  14.7 4.3 %collective-permute-start.2 = (f32[2,64]{1,0:T(2,128)S(1)}, f32[2,64]{1,0:T(2,128)S(1)}, u32[]{:S(2)}, u32[]{:S(2)}) collective-permute-start(f32[2,64]{1,0:T(2,128)S(1)} %square.1.p_ref), channel_id=1, source_target_pairs={{0,2},{1,3},{2,0},{3,1},{4,6},{5,7},{6,4},{7,5},{8,10},{9,11},{10,... | collective-permute-start | bytes 1544 | tf_op jit(solution)/shard_map/ppermute | solution.py:499
  15.1 4.0 %collective-permute-start.1 = (f32[2,64]{1,0:T(2,128)S(1)}, f32[2,64]{1,0:T(2,128)S(1)}, u32[]{:S(2)}, u32[]{:S(2)}) collective-permute-start(f32[2,64]{1,0:T(2,128)S(1)} %square.1.p_ref), channel_id=1, source_target_pairs={{0,1},{1,2},{2,3},{3,0},{4,5},{5,6},{6,7},{7,4},{8,9},{9,10},{10,1... | collective-permute-start | bytes 1544 | tf_op jit(solution)/shard_map/ppermute | solution.py:499
  15.8 0.7 %copy-start.5 = (s32[2]{0:T(128)S(1)}, s32[2]{0:T(128)}, u32[]{:S(2)}) copy-start(s32[2]{0:T(128)} %len_ref.7) | copy-start | bytes 28
  15.8 0.7 %copy-start.7 = (f32[1,32]{1,0:T(1,128)S(1)}, f32[1,32]{1,0:T(1,128)}, u32[]{:S(2)}) copy-start(f32[1,32]{1,0:T(1,128)} %log_ref.1) | copy-start | bytes 388
  15.8 0.7 %copy-start.8 = (f32[1,32]{1,0:T(1,128)S(1)}, f32[1,32]{1,0:T(1,128)}, u32[]{:S(2)}) copy-start(f32[1,32]{1,0:T(1,128)} %bias_ref.1) | copy-start | bytes 388
  16.5 2.4 %copy-start.9 = (bf16[1,2,64,2,256]{4,3,2,1,0:T(2,128)(2,1)S(1)}, bf16[1,2,64,2,256]{4,3,2,1,0:T(2,128)(2,1)}, u32[]{:S(2)}) copy-start(bf16[1,2,64,2,256]{4,3,2,1,0:T(2,128)(2,1)} %param.19) | copy-start | bytes 393220
  18.1 0.7 %copy-start.10 = (f32[1,32]{1,0:T(1,128)S(1)}, f32[1,32]{1,0:T(1,128)}, u32[]{:S(2)}) copy-start(f32[1,32]{1,0:T(1,128)} %param.28) | copy-start | bytes 388
  18.9 4.1 %copy-start.1 = (f32[1,4,2048]{2,1,0:T(4,128)S(1)}, f32[1,4,2048]{2,1,0:T(4,128)}, u32[]{:S(2)}) copy-start(f32[1,4,2048]{2,1,0:T(4,128)} %param.24) | copy-start | bytes 98308
  18.9 4.1 %copy-start.3 = (f32[1,2048]{1,0:T(1,128)S(1)}, f32[1,2048]{1,0:T(1,128)}, u32[]{:S(2)}) copy-start(f32[1,2048]{1,0:T(1,128)} %gain_ref.5) | copy-start | bytes 24580
  18.9 4.1 %copy-start.4 = (f32[1,4,2,256]{3,2,1,0:T(2,128)S(1)}, f32[1,4,2,256]{3,2,1,0:T(2,128)}, u32[]{:S(2)}) copy-start(f32[1,4,2,256]{3,2,1,0:T(2,128)} %param.25) | copy-start | bytes 24580
  19.1 4.0 %copy-start.2 = (f32[1,2048]{1,0:T(1,128)S(1)}, f32[1,2048]{1,0:T(1,128)}, u32[]{:S(2)}) copy-start(f32[1,2048]{1,0:T(1,128)} %gain_in_ref.5) | copy-start | bytes 24580
  26.8 5.6 %collective-permute-start.7 = (f32[2,64]{1,0:T(2,128)S(1)}, f32[2,64]{1,0:T(2,128)S(1)}, u32[]{:S(2)}, u32[]{:S(2)}) collective-permute-start(f32[2,64]{1,0:T(2,128)S(1)} %get-tuple-element.32), channel_id=1, source_target_pairs={{0,131},{1,128},{2,129},{3,130},{128,3},{129,0},{130,1},{131,2},{4... | collective-permute-start | bytes 1544 | tf_op jit(solution)/shard_map/ppermute | solution.py:580
  31.0 4.5 %collective-permute-start.6 = (f32[2,64]{1,0:T(2,128)S(1)}, f32[2,64]{1,0:T(2,128)S(1)}, u32[]{:S(2)}, u32[]{:S(2)}) collective-permute-start(f32[2,64]{1,0:T(2,128)S(1)} %get-tuple-element.32), channel_id=1, source_target_pairs={{0,130},{1,131},{2,128},{3,129},{128,2},{129,3},{130,0},{131,1},{4... | collective-permute-start | bytes 1544 | tf_op jit(solution)/shard_map/ppermute | solution.py:580
  31.3 4.3 %collective-permute-start.5 = (f32[2,64]{1,0:T(2,128)S(1)}, f32[2,64]{1,0:T(2,128)S(1)}, u32[]{:S(2)}, u32[]{:S(2)}) collective-permute-start(f32[2,64]{1,0:T(2,128)S(1)} %get-tuple-element.32), channel_id=1, source_target_pairs={{0,129},{1,130},{2,131},{3,128},{128,1},{129,2},{130,3},{131,0},{4... | collective-permute-start | bytes 1544 | tf_op jit(solution)/shard_map/ppermute | solution.py:580
  32.3 3.2 %collective-permute-start.8 = (bf16[2,64,2048]{2,1,0:T(8,128)(2,1)S(1)}, bf16[2,64,2048]{2,1,0:T(8,128)(2,1)S(1)}, u32[]{:S(2)}, u32[]{:S(2)}) collective-permute-start(bf16[2,64,2048]{2,1,0:T(8,128)(2,1)S(1)} %get-tuple-element.36), channel_id=1, source_target_pairs={{0,128},{128,0},{1,129},{129,1},{2,130},{130,2},{3,131},{131,3},{4... | collective-permute-start | bytes 1572872 | tf_op jit(solution)/shard_map/ppermute | solution.py:578
